TPU v7x, 32 devices: a whole 2x2x4 slice. The times are simulated.
32 devices in a mesh: grp: 4 (over y, core), pan: 8 (over z, x).
Axes of the slice: x: 2, y: 2, z: 4, core: 2. Of those that a mesh axis runs over, the one named last changes fastest.
Arguments:
- anc_rows: bfloat16 [4096, 4096], P('grp', 'pan'), as said below
- row_home: int32 [32], replicated, may hold values from 0 to 31, as said below
- block_lists: int32 [4, 16], replicated, may hold values from 0 to 31, as said below
- front_blocks: int32 [4], replicated, may hold values from 8 to 16, as said below
- panel: bfloat16 [4, 2048, 768], P('grp', 'pan'), may hold values from -0.29882812 to 0.29882812
- pivot_inverse: bfloat16 [4, 768, 768], P('grp'), as said below
Outputs:
- cross_cov: bfloat16 [4, 2048, 768], P('grp', 'pan')
- pivot_cov: float32 [4, 768, 768], P('grp', 'pan')
Inputs may be any that keep to these rules, and one draw needn't show every extreme that they name: `row_home`: A permutation of 0 to 31; the 4 index blocks of each window [4 q, 4 q + 4) have their storage row blocks in one front group. `block_lists`: rising along each row; entries 2 * q to 2 * q + 1 lie in [4 * q, 4 * q + 4). `front_blocks`: some front has all 16 blocks. `anc_rows`: storage row block row_home[b] holds row block b of a symmetric matrix. `pivot_inverse`: lower triangular.
All inputs are finite; a program needn't handle non-finite values.
Results may differ from a plain program's by a relative error of at most 0.0095.
Values may be sent and summed in bfloat16 or wider, within the bound.
No kernel may reach another device: no remote copies, remote signals or barrier semaphores. Data moves between devices by JAX's collectives and lax.ppermute only.
A program may use at most 128 MiB of HBM per device.

v0:
```python
import jax
import jax.numpy as jnp
from jax import lax
from jax.sharding import PartitionSpec as P

BLK = 128
P_SIZE = 768


def per_device(anc_rows, row_home, block_lists, front_blocks, panel, pivot_inverse):
    groups = lax.axis_size("grp")
    pan_count = lax.axis_size("pan")
    group_idx = lax.axis_index("grp")
    pan_idx = lax.axis_index("pan")
    block_count = row_home.shape[0]
    front_len = block_lists.shape[1]
    rb_local = front_len // pan_count
    cb_local = anc_rows.shape[1] // BLK
    stored_blocks = anc_rows.shape[0] // BLK
    contract = (((0,), (0,)), ((), ()))
    my_list = lax.dynamic_index_in_dim(block_lists, group_idx, 0, keepdims=False)
    column_table = block_lists.reshape(groups, pan_count, rb_local)
    column_pick = (
        lax.dynamic_index_in_dim(column_table, pan_idx, 1, keepdims=False) - cb_local * pan_idx
    )
    slot_block = jnp.argsort(row_home)
    owned_slots = lax.dynamic_slice_in_dim(slot_block, group_idx * stored_blocks, stored_blocks)
    wanted = jnp.any(owned_slots[None, :, None] == block_lists[:, None, :], axis=2)
    layered = anc_rows.reshape(stored_blocks, BLK, cb_local, BLK)[:, :, column_pick, :]
    layered = jnp.transpose(layered, (2, 0, 1, 3, 4))
    layered = jnp.where(wanted[:, :, None, None, None], layered, jnp.zeros_like(layered))
    outgoing = layered.reshape(groups, stored_blocks * BLK, rb_local * BLK)
    received = lax.all_to_all(outgoing, "grp", split_axis=0, concat_axis=0, tiled=True)
    picked = received.reshape(block_count, BLK, rb_local * BLK)
    sigma_cols = picked[row_home[my_list]].reshape(front_len * BLK, rb_local * BLK)
    my_blocks = pan_idx * rb_local + jnp.arange(rb_local, dtype=jnp.int32)
    front_live = lax.dynamic_index_in_dim(front_blocks, group_idx, 0, keepdims=False)
    alive_rows = jnp.repeat(my_blocks < front_live, BLK)
    inverse_pivot = pivot_inverse[0]
    scaled = jnp.dot(panel[0], inverse_pivot, preferred_element_type=jnp.float32)
    scaled = jnp.where(alive_rows[:, None], scaled, jnp.zeros_like(scaled)).astype(jnp.bfloat16)
    product = lax.dot_general(
        sigma_cols,
        lax.all_gather(scaled, "pan", axis=0, tiled=True),
        contract,
        preferred_element_type=jnp.float32,
    )
    cross = jnp.where(alive_rows[:, None], -product, jnp.zeros_like(product)).astype(jnp.bfloat16)
    pivot_rows = P_SIZE // pan_count
    summed = lax.psum(
        (-lax.dot_general(scaled, cross, contract, preferred_element_type=jnp.float32)).astype(
            jnp.bfloat16
        ),
        "pan",
    ).astype(jnp.float32)
    shared = lax.dynamic_slice_in_dim(summed, pan_idx * pivot_rows, pivot_rows, 0)
    own_columns = lax.dynamic_slice_in_dim(inverse_pivot, pan_idx * pivot_rows, pivot_rows, 1)
    triangle = lax.dot_general(
        own_columns, inverse_pivot, contract, preferred_element_type=jnp.float32
    )
    pivot = triangle + shared
    return (cross[None], pivot[None])


def solution(mesh):
    placed = (P("grp", "pan"), P(), P(), P(), P("grp", "pan", None), P("grp", None, None))
    return jax.shard_map(
        per_device,
        mesh=mesh,
        in_specs=placed,
        out_specs=(P("grp", "pan", None), P("grp", "pan", None)),
        check_vma=False,
    )
```

profile of v0, /device:TPU:1, one launch (start us, length us, event | category | flops | bytes accessed | tf_op | source)
XLA Modules:
  0.0 166.4 jit_solution(12918000824578316274)
XLA Ops:
  7.2 0.0 copy-start
  7.2 0.0 copy-start.4
  7.2 0.0 copy-start.2
  7.2 0.0 all-gather.2.cloned.1.call-start
  7.3 1.4 dynamic_slice.23
  8.6 0.7 add_compare_fusion
  9.3 0.1 broadcast_bitcast_fusion
  9.4 0.0 copy-done
  9.4 2.2 %fusion.2 = bf16[256,768]{1,0:T(8,128)(2,1)} fusion(bf16[1,768,768]{2,1,0:T(8,128)(2,1)S(1)} %copy-done, bf16[1,256,768]{2,1,0:T(8,128)(2,1)} %param.10, pred[256]{0:T(512)(128)(4,1)S(1)} %broadcast_bitcast_fusion), kind=kOutput, calls=%fused_computation.9 | convolution fusion | flops 302383104 | bytes 1966336 | tf_op jit(solution)/shard_map/dot_general | solution.py:40
  11.6 0.0 all-gather.2.cloned.1.call-update
  11.6 0.0 copy-done.4
  11.6 0.1 copy.19
  11.7 0.1 copy.20
  11.8 0.1 reshape.93
  11.9 0.0 copy-done.2
  11.9 0.3 reshape.116
  12.2 0.2 copy.21
  12.4 0.0 copy-start.1
  12.5 2.2 %gather_fusion = bf16[8,8,128,128]{3,2,1,0:T(8,128)(2,1)} fusion(bf16[8,128,4,128]{3,1,2,0:T(8,128)(2,1)S(1)} %copy.21, s32[1024]{0:T(1024)S(1)} %pad_clamp_fusion.2), kind=kCustom, calls=%fused_computation | custom fusion | bytes 4194336 | tf_op jit(solution)/shard_map/gather | solution.py:29
  14.6 0.0 copy-done.1
  14.6 1.6 sort.17
  16.2 0.1 dynamic_slice.24
  16.3 0.2 compare_reduce_fusion
  16.5 1.8 %select_bitcast_fusion = bf16[4,8,128,2,128]{4,2,1,3,0:T(8,128)(2,1)S(1)} fusion(bf16[4,2,8,128,128]{4,3,2,1,0:T(8,128)(2,1)} %bitcast.47, pred[4,8]{1,0:T(4,128)(4,1)S(1)} %compare_reduce_fusion), kind=kLoop, calls=%fused_computation.4 | loop fusion | flops 1048576 | bytes 4194336 | tf_op jit(solution)/shard_map/jit(_where)/select_n | solution.py:31
  18.3 2.2 %copy.22 = bf16[4,8,128,2,128]{4,3,2,1,0:T(2,128)(2,1)S(1)} copy(bf16[4,8,128,2,128]{4,2,1,3,0:T(8,128)(2,1)S(1)} %select_bitcast_fusion) | data formatting | bytes 4194304 | tf_op jit(solution)/shard_map/jit(_where)/select_n | solution.py:31
  20.5 2.6 %reshape.88 = bf16[4,1024,256]{2,1,0:T(8,128)(2,1)} reshape(bf16[4,8,128,2,128]{4,3,2,1,0:T(2,128)(2,1)S(1)} %copy.22) | data formatting | bytes 4194304 | tf_op jit(solution)/shard_map/reshape | solution.py:32
  23.2 4.3 %all-to-all-start = ((bf16[4,1024,256]{2,1,0:T(8,128)(2,1)}), bf16[4,1024,256]{2,1,0:T(8,128)(2,1)S(1)}, u32[]{:S(2)}, u32[]{:S(2)}) async-start(bf16[4,1024,256]{2,1,0:T(8,128)(2,1)} %reshape.88), calls=%async_computation | async-start | bytes 4194304 | tf_op jit(solution)/shard_map/all_to_all | solution.py:33
  27.5 0.0 all-reduce.2.cloned.1.call-start
  27.5 0.7 gather_fusion.1
  28.2 23.9 %all-to-all-done = bf16[4,1024,256]{2,1,0:T(8,128)(2,1)S(1)} async-done(((bf16[4,1024,256]{2,1,0:T(8,128)(2,1)}), bf16[4,1024,256]{2,1,0:T(8,128)(2,1)S(1)}, u32[]{:S(2)}, u32[]{:S(2)}) %all-to-all-start) | async-done | bytes 2097184 | tf_op jit(solution)/shard_map/all_to_all | solution.py:33
  52.1 1.6 gather_fusion.2
  53.7 19.8 %all-gather.2.cloned.1.call-done = bf16[2048,768]{1,0:T(8,128)(2,1)} async-done(((bf16[256,768]{1,0:T(8,128)(2,1)}), bf16[2048,768]{1,0:T(8,128)(2,1)}) %all-gather.2.cloned.1.call-update) | async-done | bytes 3145744 | tf_op jit(solution)/shard_map/all_gather | solution.py:44
  73.5 0.0 copy-start.3
  73.5 3.3 %fusion.1 = bf16[256,768]{1,0:T(8,128)(2,1)S(1)} fusion(bf16[2048,256]{1,0:T(8,128)(2,1)} %bitcast.49, bf16[2048,768]{1,0:T(8,128)(2,1)} %all-gather.2.cloned.1.call-done, pred[256]{0:T(512)(128)(4,1)S(1)} %broadcast_bitcast_fusion), kind=kOutput, calls=%fused_computation.8 | convolution fusion | flops 805896192 | bytes 4587776 | tf_op jit(solution)/shard_map/dot_general | solution.py:42
  76.7 0.0 copy-done.3
  76.8 0.0 copy-start.5
  76.8 1.6 negate_convert_fusion
  78.3 0.0 all-reduce.2.cloned.1.call-update
  78.4 79.1 %all-reduce.2.cloned.1.call-done = bf16[768,768]{1,0:T(8,128)(2,1)} async-done(((bf16[768,768]{1,0:T(8,128)(2,1)}), bf16[768,768]{1,0:T(8,128)(2,1)}) %all-reduce.2.cloned.1.call-update) | async-done | bytes 1179664 | tf_op jit(solution)/shard_map/psum | solution.py:50
  157.5 2.1 %fusion.9 = f32[1,96,768]{2,1,0:T(8,128)} fusion(bf16[1,768,768]{2,1,0:T(8,128)(2,1)S(1)} %copy-done, s32[]{:T(128)S(6)} %select_n.67, bf16[768,768]{1,0:T(8,128)(2,1)} %all-reduce.2.cloned.1.call-done), kind=kOutput, calls=%fused_computation.14 | convolution fusion | flops 113393664 | bytes 1819648 | tf_op jit(solution)/shard_map/dot_general | solution.py:58
  159.5 0.0 copy-done.5
  (7 shorter events, 0.0 us)
Async XLA Ops:
  7.2 2.2 %copy-start = (bf16[1,768,768]{2,1,0:T(8,128)(2,1)S(1)}, bf16[1,768,768]{2,1,0:T(8,128)(2,1)}, u32[]{:S(2)}) copy-start(bf16[1,768,768]{2,1,0:T(8,128)(2,1)} %param.11) | copy-start | bytes 3538948
  7.2 4.4 %copy-start.4 = (s32[4,16]{1,0:T(4,128)S(1)}, s32[4,16]{1,0:T(4,128)}, u32[]{:S(2)}) copy-start(s32[4,16]{1,0:T(4,128)} %param.8) | copy-start | bytes 772
  7.2 4.7 %copy-start.2 = (bf16[1024,512]{1,0:T(8,128)(2,1)S(1)}, bf16[1024,512]{1,0:T(8,128)(2,1)}, u32[]{:S(2)}) copy-start(bf16[1024,512]{1,0:T(8,128)(2,1)} %param.6) | copy-start | bytes 3145732
  7.2 66.3 %all-gather.2.cloned.1.call-start = ((), (), s32[]{:S(2)}) async-start(), calls=%async_computation.1 | async-start | bytes 3538944 | tf_op jit(solution)/shard_map/all_gather | solution.py:44
  12.4 2.2 %copy-start.1 = (s32[32]{0:T(128)S(1)}, s32[32]{0:T(128)}, u32[]{:S(2)}) copy-start(s32[32]{0:T(128)} %param.7) | copy-start | bytes 388
  23.2 28.9 %all-to-all-start = ((bf16[4,1024,256]{2,1,0:T(8,128)(2,1)}), bf16[4,1024,256]{2,1,0:T(8,128)(2,1)S(1)}, u32[]{:S(2)}, u32[]{:S(2)}) async-start(bf16[4,1024,256]{2,1,0:T(8,128)(2,1)} %reshape.88), calls=%async_computation | async-start | bytes 4194304 | tf_op jit(solution)/shard_map/all_to_all | solution.py:33
  27.5 130.0 %all-reduce.2.cloned.1.call-start = ((), (), s32[]{:S(2)}) async-start(), calls=%async_computation.2 | async-start | bytes 2359296 | tf_op jit(solution)/shard_map/psum | solution.py:50
  73.5 3.3 %copy-start.3 = (bf16[256,768]{1,0:T(8,128)(2,1)S(1)}, bf16[256,768]{1,0:T(8,128)(2,1)}, u32[]{:S(2)}) copy-start(bf16[256,768]{1,0:T(8,128)(2,1)} %fusion.2) | copy-start | bytes 1179652
  76.8 82.8 %copy-start.5 = (bf16[256,768]{1,0:T(8,128)(2,1)}, bf16[256,768]{1,0:T(8,128)(2,1)S(1)}, u32[]{:S(2)}) copy-start(bf16[256,768]{1,0:T(8,128)(2,1)S(1)} %fusion.1) | copy-start | bytes 1179652
Sparse Core Ops, SparseCore 0:
  11.7 61.6 all-gather.1
  78.5 78.9 all-reduce.1
where the time goes:
time: 168 us; the launch traced here: 166 us
  waiting for transfers between devices  123 us (73%)
  between operations  14.2 us (8%)
  local copies, waits for them, and re-layouts  11.6 us (7%)
  matrix products  9.12 us (5%)
  starting transfers between devices  4.33 us (3%)
  other arithmetic  4.31 us (3%)
    psum x1, waiting for transfers between devices, per_device(): lax.psum((-lax.dot_general(scaled, cross, contract, preferred_element_typ...  79.1 us
    all_to_all x1, waiting for transfers between devices, per_device(): lax.all_to_all(outgoing, 'grp', split_axis=0, concat_axis=0, tiled=True)  23.9 us
    all_gather x1, waiting for transfers between devices, per_device(): lax.all_gather(scaled, 'pan', axis=0, tiled=True)  19.8 us
    all_to_all x1, starting transfers between devices, per_device(): lax.all_to_all(outgoing, 'grp', split_axis=0, concat_axis=0, tiled=True)  4.29 us
  transfers between devices with their start and end apart: 3, of which 3 were waited for; matrix products, arithmetic and copies ran while one was open for 8% of the time, Pallas kernels for 0%

commit v1 on v0

v1 whole, which is shorter than its diff:
```python
import functools

import jax
import jax.numpy as jnp
from jax import lax
from jax.experimental import pallas as pl
from jax.experimental.pallas import tpu as pltpu
from jax.sharding import PartitionSpec as P

BLK = 128
F32 = jnp.float32
BF16 = jnp.bfloat16

VMEM = pl.BlockSpec(memory_space=pltpu.VMEM)
SMEM = pl.BlockSpec(memory_space=pltpu.SMEM)
HBM = pl.BlockSpec(memory_space=pl.ANY)


def power_of_two(n):
    return n & (n - 1) == 0


def peer(q, k, n):
    return q ^ k if power_of_two(n) else (q + k) % n


def source(q, k, n):
    return q ^ k if power_of_two(n) else (q + n - k) % n


def ring_place(position, n):
    return position ^ (position >> 1) if power_of_two(n) else position


def ring_position(place, n):
    position = place
    if power_of_two(n):
        shift = 1
        while shift < n:
            position = position ^ (place >> shift)
            shift += 1
    return position


def params():
    return pltpu.CompilerParams(vmem_limit_bytes=40 * 1024 * 1024)


def pack_kernel(groups, pan, me, row_home, lists, anc, *rest):
    outs, slots, sems = rest[:groups], rest[groups], rest[groups + 1]
    g, p = me[0], me[1]
    h, c, l = g >> 1, g & 1, p & 1
    stored = anc.shape[0] // BLK
    window_blocks = anc.shape[1] // BLK
    picked = lists.shape[1] // pan
    windows = pan // groups

    def window(w, rank):
        mine = row_home[window_blocks * w] // stored == g

        @pl.when(mine)
        def _():
            for k in range(groups):
                front = 2 * peer(h, k >> 1, groups // 2) + (c ^ (k & 1))
                for r in range(picked):
                    row = row_home[lists[front, picked * w + r]] - stored * g
                    for s in range(picked):
                        column = lists[front, picked * p + s] - window_blocks * p
                        pltpu.make_async_copy(
                            anc.at[pl.ds(row * BLK, BLK), pl.ds(column * BLK, BLK)],
                            outs[k].at[pl.ds((rank * picked + r) * BLK, BLK), pl.ds(s * BLK, BLK)],
                            sems.at[k],
                        ).start()

        return rank + mine.astype(jnp.int32)

    lax.fori_loop(0, pan, window, jnp.int32(0))
    owners = [row_home[window_blocks * w] // stored for w in range(pan)]
    for w in range(pan):
        rank = jnp.int32(0)
        for v in range(w):
            rank = rank + (owners[v] == owners[w]).astype(jnp.int32)
        step = owners[w] >> 1
        step = step ^ h if power_of_two(groups // 2) else (h + groups // 2 - step) % (groups // 2)
        slots[w] = (2 * step + ((owners[w] & 1) ^ l)) * windows + rank
    rows, columns = outs[0].shape
    for k in range(groups):
        pltpu.make_async_copy(
            anc.at[pl.ds(0, rows), pl.ds(0, columns)], outs[k], sems.at[k]
        ).wait()


def scale_kernel(pan, me, front_blocks, panel, inverse, keep, give, both, turned):
    g, p = me[0], me[1]
    c = g & 1
    rows, width = panel.shape
    n, share = pan // 2, width // pan
    padded = keep.shape[0] // n
    live = front_blocks[g]
    scaled = jnp.dot(panel[...], inverse[...], preferred_element_type=F32)
    row = lax.broadcasted_iota(jnp.int32, scaled.shape, 0)
    scaled = jnp.where(p * (rows // BLK) + row // BLK < live, scaled, 0.0)
    turned[...] = scaled.T
    if padded != share:
        keep[...] = jnp.zeros_like(keep)
        give[...] = jnp.zeros_like(give)
    for place in range(n):
        at = pl.ds(place * padded, share)
        keep[at] = turned[pl.ds(share * (2 * place + c), share)].astype(BF16)
        give[at] = turned[pl.ds(share * (2 * place + 1 - c), share)].astype(BF16)
    both[0] = keep[...]
    both[1] = give[...]


def cross_kernel(n, me, front_blocks, slots, *rest):
    near, far = rest[:n], rest[n : 2 * n]
    own_sigma, other_sigma = rest[2 * n : 2 * n + 2]
    mine, give, whole = rest[2 * n + 2 : 2 * n + 5]
    parts, total = rest[2 * n + 5 : 3 * n + 5], rest[3 * n + 5]
    g, p = me[0], me[1]
    h, c, q, l = g >> 1, g & 1, p >> 1, p & 1
    half, rows = near[0].shape
    padded = half // n
    own = jnp.zeros((half, rows), F32)
    other = jnp.zeros((half, rows), F32)
    position = ring_position(q, n)
    for step in range(n):
        origin = ring_place((position + n - step) % n, n)
        for side, chunks in ((0, near), (1, far)):
            member = 2 * origin + (l ^ side)
            slot = slots[member]
            chunk = chunks[step][...]
            whole[member] = chunk
            own = own + jnp.dot(chunk, own_sigma[slot], preferred_element_type=F32)
            other = other + jnp.dot(chunk, other_sigma[slot], preferred_element_type=F32)
    live = front_blocks[2 * h + l]
    block = lax.broadcasted_iota(jnp.int32, (half, rows), 1) // BLK
    own = jnp.where((2 * q + c) * (rows // BLK) + block < live, -own, 0.0)
    other = jnp.where((2 * q + 1 - c) * (rows // BLK) + block < live, -other, 0.0)
    mine[...] = own.astype(BF16)
    give[...] = other.astype(BF16)
    total[c] = own
    total[1 - c] = other
    for k in range(n):
        at = pl.ds(peer(q, k, n) * padded, padded)
        for side in range(2):
            parts[k][:, pl.ds(side * rows, rows)] = total[side, at].astype(BF16)


def pivot_kernel(n, share, me, *rest):
    parts, own_scaled, other_scaled, out = rest[:n], rest[n], rest[n + 1], rest[n + 2]
    g, p = me[0], me[1]
    c, q = g & 1, p >> 1
    rows = own_scaled.shape[2]
    padded = parts[0].shape[0]
    across = (((1,), (1,)), ((), ()))
    own = jnp.zeros((padded, n * padded), F32)
    other = jnp.zeros((padded, n * padded), F32)
    for k in range(n):
        origin = source(q, k, n)
        for side in range(2):
            part = parts[k][:, pl.ds(side * rows, rows)]
            member = 2 * origin + side
            own = own + lax.dot_general(
                part, own_scaled[member], across, preferred_element_type=F32
            )
            other = other + lax.dot_general(
                part, other_scaled[member], across, preferred_element_type=F32
            )
    low = jnp.where(c == 0, own, other)
    high = jnp.where(c == 0, other, own)
    pieces = []
    for place in range(n):
        at = slice(place * padded, place * padded + share)
        pieces += [low[:, at], high[:, at]]
    out[...] = (-jnp.concatenate(pieces, axis=1)).astype(BF16)


def turn_kernel(pan, share, me, mine, other, out, natural):
    c = me[0] & 1
    n = pan // 2
    padded = mine.shape[0] // n
    for place in range(n):
        at = pl.ds(place * padded, share)
        natural[pl.ds(share * (2 * place + c), share)] = mine[at].astype(F32)
        natural[pl.ds(share * (2 * place + 1 - c), share)] = other[at].astype(F32)
    out[...] = natural[...].T.astype(BF16)


def per_device(anc_rows, row_home, block_lists, front_blocks, panel, pivot_inverse):
    groups, pan = lax.axis_size("grp"), lax.axis_size("pan")
    n, pairs = pan // 2, groups // 2
    rows, width = panel.shape[1:]
    share = width // pan
    padded = -(-share // 16) * 16
    half = n * padded
    wanted = block_lists.shape[1] // groups * BLK
    windows = pan // groups
    me = jnp.stack([lax.axis_index("grp"), lax.axis_index("pan")]).astype(jnp.int32)
    diagonal = me[0] & 1 == me[1] & 1
    inverse = pivot_inverse[0]
    shape = jax.ShapeDtypeStruct

    def at(h, c, q, l):
        return (2 * h + c) * pan + 2 * q + l

    places = [
        (h, c, q, l) for h in range(pairs) for c in range(2) for q in range(n) for l in range(2)
    ]
    exchange = [(at(h, c, q, l), at(h, l, q, c)) for h, c, q, l in places]
    crossing = [(a, b) for a, b in exchange if a != b]
    cores = [(g, g ^ 1) for g in range(groups)]
    ring = [
        (2 * ring_place(i, n) + l, 2 * ring_place((i + 1) % n, n) + l)
        for i in range(n)
        for l in range(2)
    ]

    def swap(x):
        return lax.ppermute(x, "grp", cores)

    def everywhere(x, pairs_of):
        return lax.ppermute(x, ("grp", "pan"), pairs_of)

    keep, give, both = pl.pallas_call(
        functools.partial(scale_kernel, pan),
        out_shape=[shape((half, rows), BF16)] * 2 + [shape((2, half, rows), BF16)],
        in_specs=[SMEM, SMEM, VMEM, VMEM],
        out_specs=[VMEM] * 3,
        scratch_shapes=[pltpu.VMEM((width, rows), F32)],
        compiler_params=params(),
        name="scale",
    )(me, front_blocks, panel[0], inverse)
    near = jnp.where(diagonal, keep, swap(give))
    moved = everywhere(both, crossing)
    far = jnp.where(diagonal, swap(moved[0]), moved[1])

    *packed, slots = pl.pallas_call(
        functools.partial(pack_kernel, groups, pan),
        out_shape=[shape((wanted, rows), BF16)] * groups + [shape((pan,), jnp.int32)],
        in_specs=[SMEM, SMEM, SMEM, HBM],
        out_specs=[HBM] * groups + [SMEM],
        scratch_shapes=[pltpu.SemaphoreType.DMA((groups,))],
        compiler_params=params(),
        name="pack",
    )(me, row_home, block_lists, anc_rows)
    arrived = [
        everywhere(
            packed[k],
            [
                (at(h, c, q, l), at(peer(h, k >> 1, pairs), l, q, c ^ (k & 1)))
                for h, c, q, l in places
            ],
        )
        for k in range(groups)
    ]
    own_sigma = jnp.stack(arrived).reshape(groups * windows, wanted // windows, rows)
    other_sigma = swap(own_sigma)

    nears, fars = [near], [far]
    for _ in range(n - 1):
        nears.append(lax.ppermute(nears[-1], "pan", ring))
        fars.append(lax.ppermute(fars[-1], "pan", ring))

    mine, give, whole, *parts = pl.pallas_call(
        functools.partial(cross_kernel, n),
        out_shape=[shape((half, rows), BF16)] * 2
        + [shape((pan, half, rows), BF16)]
        + [shape((padded, 2 * rows), BF16)] * n,
        in_specs=[SMEM] * 3 + [VMEM] * (2 * n + 2),
        out_specs=[VMEM] * (n + 3),
        scratch_shapes=[pltpu.VMEM((2, half, rows), F32)],
        compiler_params=params(),
        name="cross",
    )(me, front_blocks, slots, *nears, *fars, own_sigma, other_sigma)

    for k in range(1, n):
        parts[k] = lax.ppermute(
            parts[k], "pan", [(2 * q + l, 2 * peer(q, k, n) + l) for q in range(n) for l in range(2)]
        )
    other_whole = swap(whole)
    turned = pl.pallas_call(
        functools.partial(turn_kernel, pan, share),
        out_shape=shape((rows, width), BF16),
        in_specs=[SMEM, VMEM, VMEM],
        out_specs=VMEM,
        scratch_shapes=[pltpu.VMEM((width, rows), F32)],
        compiler_params=params(),
        name="turn",
    )(me, mine, swap(give))
    cross = everywhere(turned, exchange)

    term = pl.pallas_call(
        functools.partial(pivot_kernel, n, share),
        out_shape=shape((padded, width), BF16),
        in_specs=[SMEM] + [VMEM] * (n + 2),
        out_specs=VMEM,
        compiler_params=params(),
        name="pivot",
    )(me, *parts, whole, other_whole)
    own_columns = lax.dynamic_slice_in_dim(inverse, me[1] * share, share, 1)
    triangle = lax.dot_general(
        own_columns, inverse, (((0,), (0,)), ((), ())), preferred_element_type=F32
    )
    pivot = triangle + everywhere(term, exchange)[:share].astype(F32)
    return cross[None], pivot[None]


def solution(mesh):
    placed = (P("grp", "pan"), P(), P(), P(), P("grp", "pan", None), P("grp", None, None))
    return jax.shard_map(
        per_device,
        mesh=mesh,
        in_specs=placed,
        out_specs=(P("grp", "pan", None), P("grp", "pan", None)),
        check_vma=False,
    )
```

time: 168 us -> 89.3 us (0.53)
  waiting for transfers between devices: 123 us -> 41.2 us
  starting transfers between devices: 4.33 us -> 29.7 us
  between operations: 14.2 us -> 0.83 us
  matrix products: 9.12 us -> 0.44 us
  Pallas kernels: 0 us -> 8.58 us
  local copies, waits for them, and re-layouts: 11.6 us -> 7.17 us
  other arithmetic: 4.31 us -> 1 us
    psum x1 -> x0, waiting for transfers between devices: 79.1 us -> none  [per_device(): lax.psum((-lax.dot_general(scaled, cross, contract, preferred_element_typ...]
    ppermute x0 -> x21, waiting for transfers between devices: none -> 41.2 us  [the longest x3 11.4 us: per_device(): fars.append(lax.ppermute(fars[-1], 'pan', ring))]
    ppermute x0 -> x21, starting transfers between devices: none -> 29.7 us  [the longest x7 17.3 us: everywhere(): return lax.ppermute(x, ('grp', 'pan'), pairs_of)]
    all_to_all x1 -> x0, waiting for transfers between devices: 23.9 us -> none  [per_device(): lax.all_to_all(outgoing, 'grp', split_axis=0, concat_axis=0, tiled=True)]
    all_gather x1 -> x0, waiting for transfers between devices: 19.8 us -> none  [per_device(): lax.all_gather(scaled, 'pan', axis=0, tiled=True)]
    dot_general x4 -> x1, matrix products: 9.12 us -> 0.44 us  [per_device(): lax.dot_general(own_columns, inverse, (((0,), (0,)), ((), ())), preferred...]
    pallas_call x0 -> x5, Pallas kernels: none -> 8.58 us  [the longest x1 2.29 us: per_device(): pl.pallas_call(functools.partial(cross_kernel, n), out_shape=[shape((half...]
    unnamed x13 -> x21, local copies, waits for them, and re-layouts: 0.12 us -> 7.16 us
  transfers between devices with their start and end apart: 3 -> 21, of which waited for: 3 -> 13; matrix products, arithmetic and copies ran while one was open for 8% -> 1% of each run, Pallas kernels for 0% -> 5%
where the time goes in v1:
time: 89.3 us; the launch traced here: 88.9 us
  waiting for transfers between devices  41.2 us (46%)
  starting transfers between devices  29.7 us (33%)
  Pallas kernels  8.58 us (10%)
  local copies, waits for them, and re-layouts  7.17 us (8%)
  other arithmetic  1 us (1%)
    ppermute x7, starting transfers between devices, everywhere(): return lax.ppermute(x, ('grp', 'pan'), pairs_of)  17.3 us
    ppermute x3, waiting for transfers between devices, per_device(): fars.append(lax.ppermute(fars[-1], 'pan', ring))  11.4 us
    ppermute x7, waiting for transfers between devices, everywhere(): return lax.ppermute(x, ('grp', 'pan'), pairs_of)  10.1 us
    ppermute x3, waiting for transfers between devices, per_device(): nears.append(lax.ppermute(nears[-1], 'pan', ring))  9.78 us
    unnamed x21, local copies, waits for them, and re-layouts  7.16 us
    ppermute x3, waiting for transfers between devices, per_device(): lax.ppermute(parts[k], 'pan', [(2 * q + l, 2 * peer(q, k, n) + l) for q i...  6.59 us
    ppermute x3, starting transfers between devices, per_device(): lax.ppermute(parts[k], 'pan', [(2 * q + l, 2 * peer(q, k, n) + l) for q i...  3.67 us
    ppermute x3, starting transfers between devices, per_device(): fars.append(lax.ppermute(fars[-1], 'pan', ring))  3.55 us
  transfers between devices with their start and end apart: 21, of which 13 were waited for; matrix products, arithmetic and copies ran while one was open for 1% of the time, Pallas kernels for 5%

profile of v1, /device:TPU:1, one launch (start us, length us, event | category | flops | bytes accessed | tf_op | source)
XLA Modules:
  0.0 88.9 jit_solution(6490735256447492374)
XLA Ops:
  0.6 0.1 pad_add_fusion.me
  0.7 1.2 %copy-done.2 = bf16[1024,512]{1,0:T(8,128)(2,1)S(1)} copy-done((bf16[1024,512]{1,0:T(8,128)(2,1)S(1)}, bf16[1024,512]{1,0:T(8,128)(2,1)}, u32[]{:S(2)}) %copy-start.2) | copy-done | bytes 1048600
  1.9 0.7 copy-done.6
  2.6 0.7 copy-done.9
  3.3 2.0 %pack.1 = (bf16[512,256]{1,0:T(8,128)(2,1)S(1)}, bf16[512,256]{1,0:T(8,128)(2,1)S(1)}, bf16[512,256]{1,0:T(8,128)(2,1)S(1)}, bf16[512,256]{1,0:T(8,128)(2,1)S(1)}, s32[8]{0:T(128)S(1)}) custom-call(s32[2]{0:T(128)S(1)} %pad_add_fusion.me, s32[32]{0:T(128)S(1)} %copy-done.9, s32[4,16]{1,0:T(4,128)S(1)} %copy-done.6, bf16[1024,512]{1,0:T(8,128)(2,1)S(1)} %copy-done.2), custom_call_target="tpu_custom_call" | custom-call | tf_op jit(solution)/shard_map/pack/pallas_call | solution.py:238
  5.3 4.5 %collective-permute-start.9 = (bf16[512,256]{1,0:T(8,128)(2,1)S(1)}, bf16[512,256]{1,0:T(8,128)(2,1)S(1)}, u32[]{:S(2)}, u32[]{:S(2)}) collective-permute-start(bf16[512,256]{1,0:T(8,128)(2,1)S(1)} %get-tuple-element.21), channel_id=1, source_target_pairs={{0,0},{1,8},{2,2},{3,10},{4,4},{5,12},{6,6},{7,14},{8,1},{9,9},{10... | collective-permute-start | bytes 786440 | tf_op jit(solution)/shard_map/ppermute | solution.py:223
  9.9 1.0 %collective-permute-start.11 = (bf16[512,256]{1,0:T(8,128)(2,1)S(1)}, bf16[512,256]{1,0:T(8,128)(2,1)S(1)}, u32[]{:S(2)}, u32[]{:S(2)}) collective-permute-start(bf16[512,256]{1,0:T(8,128)(2,1)S(1)} %get-tuple-element.23), channel_id=1, source_target_pairs={{0,16},{1,24},{2,18},{3,26},{4,20},{5,28},{6,22},{7,30},{8,17},{9,... | collective-permute-start | bytes 786440 | tf_op jit(solution)/shard_map/ppermute | solution.py:223
  10.9 1.0 %collective-permute-start.12 = (bf16[512,256]{1,0:T(8,128)(2,1)S(1)}, bf16[512,256]{1,0:T(8,128)(2,1)S(1)}, u32[]{:S(2)}, u32[]{:S(2)}) collective-permute-start(bf16[512,256]{1,0:T(8,128)(2,1)S(1)} %get-tuple-element.24), channel_id=1, source_target_pairs={{0,17},{1,25},{2,19},{3,27},{4,21},{5,29},{6,23},{7,31},{8,16},{9,... | collective-permute-start | bytes 786440 | tf_op jit(solution)/shard_map/ppermute | solution.py:223
  11.9 1.3 %copy-done = bf16[1,768,768]{2,1,0:T(8,128)(2,1)S(1)} copy-done((bf16[1,768,768]{2,1,0:T(8,128)(2,1)S(1)}, bf16[1,768,768]{2,1,0:T(8,128)(2,1)}, u32[]{:S(2)}) %copy-start) | copy-done | bytes 1179672
  13.2 0.7 copy-done.7
  13.8 1.2 %scale.1 = (bf16[384,256]{1,0:T(8,128)(2,1)S(1)}, bf16[384,256]{1,0:T(8,128)(2,1)S(1)}, bf16[2,384,256]{2,1,0:T(8,128)(2,1)S(1)}) custom-call(s32[2]{0:T(128)S(1)} %pad_add_fusion.me, s32[4]{0:T(128)S(1)} %copy-done.7, bf16[256,768]{1,0:T(8,128)(2,1)S(1)} %bitcast.26, bf16[768,768]{1,0:T(8,128)(2,1)S(1)} %bitcast.23), custom_call_target="tpu_custom_call" | custom-call | tf_op jit(solution)/shard_map/scale/pallas_call | solution.py:225
  15.0 3.1 %collective-permute-start.4 = (bf16[2,384,256]{2,1,0:T(8,128)(2,1)S(1)}, bf16[2,384,256]{2,1,0:T(8,128)(2,1)S(1)}, u32[]{:S(2)}, u32[]{:S(2)}) collective-permute-start(bf16[2,384,256]{2,1,0:T(8,128)(2,1)S(1)} %get-tuple-element.20), channel_id=1, source_target_pairs={{1,8},{3,10},{5,12},{7,14},{8,1},{10,3},{12,5},{14,7},{17,24},{19,... | collective-permute-start | bytes 1179656 | tf_op jit(solution)/shard_map/ppermute | solution.py:223
  18.1 0.1 collective-permute-start
  18.2 3.9 %collective-permute-done.11 = bf16[512,256]{1,0:T(8,128)(2,1)S(1)} collective-permute-done((bf16[512,256]{1,0:T(8,128)(2,1)S(1)}, bf16[512,256]{1,0:T(8,128)(2,1)S(1)}, u32[]{:S(2)}, u32[]{:S(2)}) %collective-permute-start.11) | collective-permute-done | bytes 262176 | tf_op jit(solution)/shard_map/ppermute | solution.py:223
  22.1 2.4 %collective-permute-done.12 = bf16[512,256]{1,0:T(8,128)(2,1)S(1)} collective-permute-done((bf16[512,256]{1,0:T(8,128)(2,1)S(1)}, bf16[512,256]{1,0:T(8,128)(2,1)S(1)}, u32[]{:S(2)}, u32[]{:S(2)}) %collective-permute-start.12) | collective-permute-done | bytes 262176 | tf_op jit(solution)/shard_map/ppermute | solution.py:223
  24.5 0.1 pad_maximum_fusion
  24.7 0.4 collective-permute-start.13
  25.1 1.5 %collective-permute-done.4 = bf16[2,384,256]{2,1,0:T(8,128)(2,1)S(1)} collective-permute-done((bf16[2,384,256]{2,1,0:T(8,128)(2,1)S(1)}, bf16[2,384,256]{2,1,0:T(8,128)(2,1)S(1)}, u32[]{:S(2)}, u32[]{:S(2)}) %collective-permute-start.4) | collective-permute-done | bytes 393248 | tf_op jit(solution)/shard_map/ppermute | solution.py:223
  26.6 0.1 collective-permute-start.5
  26.7 1.3 %collective-permute-start.1 = (bf16[384,256]{1,0:T(8,128)(2,1)S(1)}, bf16[384,256]{1,0:T(8,128)(2,1)S(1)}, u32[]{:S(2)}, u32[]{:S(2)}) collective-permute-start(bf16[384,256]{1,0:T(8,128)(2,1)S(1)} %broadcast_select_fusion.rest_0_), channel_id=1, source_target_pairs={{0,2},{1,3},{2,6},{3,7},{6,4},{7,5},{4,0},{5,1},{8,10},{9,11},{10,... | collective-permute-start | bytes 589832 | tf_op jit(solution)/shard_map/ppermute | solution.py:262
  28.1 2.3 %collective-permute-start.6 = (bf16[384,256]{1,0:T(8,128)(2,1)S(1)}, bf16[384,256]{1,0:T(8,128)(2,1)S(1)}, u32[]{:S(2)}, u32[]{:S(2)}) collective-permute-start(bf16[384,256]{1,0:T(8,128)(2,1)S(1)} %fusion.rest_4_), channel_id=1, source_target_pairs={{0,2},{1,3},{2,6},{3,7},{6,4},{7,5},{4,0},{5,1},{8,10},{9,11},{10,... | collective-permute-start | bytes 589832 | tf_op jit(solution)/shard_map/ppermute | solution.py:263
  30.4 3.2 %collective-permute-done.1.rest_1_ = bf16[384,256]{1,0:T(8,128)(2,1)S(1)} collective-permute-done((bf16[384,256]{1,0:T(8,128)(2,1)S(1)}, bf16[384,256]{1,0:T(8,128)(2,1)S(1)}, u32[]{:S(2)}, u32[]{:S(2)}) %collective-permute-start.1) | collective-permute-done | bytes 196640 | tf_op jit(solution)/shard_map/ppermute | solution.py:262
  33.6 0.5 collective-permute-start.2
  34.1 3.7 %collective-permute-done.6.rest_5_ = bf16[384,256]{1,0:T(8,128)(2,1)S(1)} collective-permute-done((bf16[384,256]{1,0:T(8,128)(2,1)S(1)}, bf16[384,256]{1,0:T(8,128)(2,1)S(1)}, u32[]{:S(2)}, u32[]{:S(2)}) %collective-permute-start.6) | collective-permute-done | bytes 196640 | tf_op jit(solution)/shard_map/ppermute | solution.py:263
  37.8 0.5 collective-permute-start.7
  38.3 3.4 %collective-permute-done.2.rest_2_ = bf16[384,256]{1,0:T(8,128)(2,1)S(1)} collective-permute-done((bf16[384,256]{1,0:T(8,128)(2,1)S(1)}, bf16[384,256]{1,0:T(8,128)(2,1)S(1)}, u32[]{:S(2)}, u32[]{:S(2)}) %collective-permute-start.2) | collective-permute-done | bytes 196640 | tf_op jit(solution)/shard_map/ppermute | solution.py:262
  41.7 0.7 collective-permute-start.3
  42.5 3.5 %collective-permute-done.7.rest_6_ = bf16[384,256]{1,0:T(8,128)(2,1)S(1)} collective-permute-done((bf16[384,256]{1,0:T(8,128)(2,1)S(1)}, bf16[384,256]{1,0:T(8,128)(2,1)S(1)}, u32[]{:S(2)}, u32[]{:S(2)}) %collective-permute-start.7) | collective-permute-done | bytes 196640 | tf_op jit(solution)/shard_map/ppermute | solution.py:263
  46.0 0.7 collective-permute-start.8
  46.7 3.2 %collective-permute-done.3.rest_3_ = bf16[384,256]{1,0:T(8,128)(2,1)S(1)} collective-permute-done((bf16[384,256]{1,0:T(8,128)(2,1)S(1)}, bf16[384,256]{1,0:T(8,128)(2,1)S(1)}, u32[]{:S(2)}, u32[]{:S(2)}) %collective-permute-start.3) | collective-permute-done | bytes 196640 | tf_op jit(solution)/shard_map/ppermute | solution.py:262
  49.9 4.2 %collective-permute-done.8.rest_7_ = bf16[384,256]{1,0:T(8,128)(2,1)S(1)} collective-permute-done((bf16[384,256]{1,0:T(8,128)(2,1)S(1)}, bf16[384,256]{1,0:T(8,128)(2,1)S(1)}, u32[]{:S(2)}, u32[]{:S(2)}) %collective-permute-start.8) | collective-permute-done | bytes 196640 | tf_op jit(solution)/shard_map/ppermute | solution.py:263
  54.1 2.3 %cross.1 = (bf16[384,256]{1,0:T(8,128)(2,1)S(1)}, bf16[384,256]{1,0:T(8,128)(2,1)S(1)}, bf16[8,384,256]{2,1,0:T(8,128)(2,1)S(1)}, bf16[96,512]{1,0:T(8,128)(2,1)...) custom-call(s32[2]{0:T(128)S(1)} %pad_add_fusion.me, s32[4]{0:T(128)S(1)} %copy-done.8, ...), custom_call_target="tpu_custom_call" | custom-call | tf_op jit(solution)/shard_map/cross/pallas_call | solution.py:265
  56.4 2.0 %collective-permute-start.19 = (bf16[8,384,256]{2,1,0:T(8,128)(2,1)S(1)}, bf16[8,384,256]{2,1,0:T(8,128)(2,1)S(1)}, u32[]{:S(2)}, u32[]{:S(2)}) collective-permute-start(bf16[8,384,256]{2,1,0:T(8,128)(2,1)S(1)} %get-tuple-element.31.rest_4_), channel_id=1, source_target_pairs={{0,8},{8,0},{16,24},{24,16},{1,9},{9,1},{17,25},{25,17},{2,10},{10... | collective-permute-start | bytes 4718600 | tf_op jit(solution)/shard_map/ppermute | solution.py:220
  58.3 0.0 collective-permute-start.14
  58.4 3.3 %collective-permute-done.14.other = bf16[384,256]{1,0:T(8,128)(2,1)S(1)} collective-permute-done((bf16[384,256]{1,0:T(8,128)(2,1)S(1)}, bf16[384,256]{1,0:T(8,128)(2,1)S(1)}, u32[]{:S(2)}, u32[]{:S(2)}) %collective-permute-start.14) | collective-permute-done | bytes 196640 | tf_op jit(solution)/shard_map/ppermute | solution.py:220
  61.6 0.8 turn.1
  62.4 4.0 %collective-permute-start.15 = (bf16[256,768]{1,0:T(8,128)(2,1)S(1)}, bf16[256,768]{1,0:T(8,128)(2,1)}, u32[]{:S(2)}, u32[]{:S(2)}) collective-permute-start(bf16[256,768]{1,0:T(8,128)(2,1)S(1)} %turn.1), channel_id=1, source_target_pairs={{0,0},{1,8},{2,2},{3,10},{4,4},{5,12},{6,6},{7,14},{8,1},{9,9},{10... | collective-permute-start | bytes 1179656 | tf_op jit(solution)/shard_map/ppermute | solution.py:223
  66.4 0.6 collective-permute-start.16
  67.0 3.1 %collective-permute-start.17 = (bf16[96,512]{1,0:T(8,128)(2,1)}, bf16[96,512]{1,0:T(8,128)(2,1)}, u32[]{:S(2)}, u32[]{:S(2)}) collective-permute-start(bf16[96,512]{1,0:T(8,128)(2,1)} %get-tuple-element.29), channel_id=1, source_target_pairs={{0,4},{1,5},{2,6},{3,7},{4,0},{5,1},{6,2},{7,3},{8,12},{9,13},{10,... | collective-permute-start | bytes 294920 | tf_op jit(solution)/shard_map/ppermute | solution.py:278
  70.1 1.1 %collective-permute-done.16.rest_1_ = bf16[96,512]{1,0:T(8,128)(2,1)} collective-permute-done((bf16[96,512]{1,0:T(8,128)(2,1)}, bf16[96,512]{1,0:T(8,128)(2,1)}, u32[]{:S(2)}, u32[]{:S(2)}) %collective-permute-start.16) | collective-permute-done | bytes 98336 | tf_op jit(solution)/shard_map/ppermute | solution.py:278
  71.2 5.5 %collective-permute-done.17.rest_2_ = bf16[96,512]{1,0:T(8,128)(2,1)} collective-permute-done((bf16[96,512]{1,0:T(8,128)(2,1)}, bf16[96,512]{1,0:T(8,128)(2,1)}, u32[]{:S(2)}, u32[]{:S(2)}) %collective-permute-start.17) | collective-permute-done | bytes 98336 | tf_op jit(solution)/shard_map/ppermute | solution.py:278
  76.7 0.9 %copy-done.5 = bf16[96,512]{1,0:T(8,128)(2,1)S(1)} copy-done((bf16[96,512]{1,0:T(8,128)(2,1)S(1)}, bf16[96,512]{1,0:T(8,128)(2,1)}, u32[]{:S(2)}) %copy-start.5) | copy-done | bytes 98328
  77.6 2.3 %pivot.1 = bf16[96,768]{1,0:T(8,128)(2,1)S(1)} custom-call(s32[2]{0:T(128)S(1)} %pad_add_fusion.me, bf16[96,512]{1,0:T(8,128)(2,1)S(1)} %copy-done.5, bf16[96,512]{1,0:T(8,128)(2,1)} %collective-permute-done.16.rest_1_, bf16[96,512]{1,0:T(8,128)(2,1)} %collective-permute-done.17.rest_2_, bf16[96,512]{1,0:T(8,128)(2,1)} %collective-permute-done.18.rest_3_, ...), custom_call_target="tpu_custom_call" | custom-call | tf_op jit(solution)/shard_map/pivot/pallas_call | solution.py:293
  79.9 3.7 %collective-permute-start.20 = (bf16[96,768]{1,0:T(8,128)(2,1)S(1)}, bf16[96,768]{1,0:T(8,128)(2,1)S(1)}, u32[]{:S(2)}, u32[]{:S(2)}) collective-permute-start(bf16[96,768]{1,0:T(8,128)(2,1)S(1)} %pivot.1), channel_id=1, source_target_pairs={{0,0},{1,8},{2,2},{3,10},{4,4},{5,12},{6,6},{7,14},{8,1},{9,9},{10... | collective-permute-start | bytes 442376 | tf_op jit(solution)/shard_map/ppermute | solution.py:223
  83.6 0.4 fusion.1
  84.1 2.3 %collective-permute-done.20 = bf16[96,768]{1,0:T(8,128)(2,1)S(1)} collective-permute-done((bf16[96,768]{1,0:T(8,128)(2,1)S(1)}, bf16[96,768]{1,0:T(8,128)(2,1)S(1)}, u32[]{:S(2)}, u32[]{:S(2)}) %collective-permute-start.20) | collective-permute-done | bytes 147488 | tf_op jit(solution)/shard_map/ppermute | solution.py:223
  86.4 0.7 add_bitcast_fusion
  87.1 1.8 %copy.9 = bf16[1,256,768]{2,1,0:T(8,128)(2,1)} copy(bf16[1,256,768]{2,1,0:T(8,128)(2,1)} %bitcast.11) | data formatting | bytes 786432
  (27 shorter events, 0.2 us)
Async XLA Ops:
  0.7 1.2 %copy-start.2 = (bf16[1024,512]{1,0:T(8,128)(2,1)S(1)}, bf16[1024,512]{1,0:T(8,128)(2,1)}, u32[]{:S(2)}) copy-start(bf16[1024,512]{1,0:T(8,128)(2,1)} %anc.1) | copy-start | bytes 3145732
  1.9 0.7 copy-start.6
  2.6 0.7 copy-start.9
  3.3 8.6 %copy-start.3 = (bf16[1,256,768]{2,1,0:T(8,128)(2,1)S(1)}, bf16[1,256,768]{2,1,0:T(8,128)(2,1)}, u32[]{:S(2)}) copy-start(bf16[1,256,768]{2,1,0:T(8,128)(2,1)} %param.10) | copy-start | bytes 1179652
  5.3 12.8 %collective-permute-start.9 = (bf16[512,256]{1,0:T(8,128)(2,1)S(1)}, bf16[512,256]{1,0:T(8,128)(2,1)S(1)}, u32[]{:S(2)}, u32[]{:S(2)}) collective-permute-start(bf16[512,256]{1,0:T(8,128)(2,1)S(1)} %get-tuple-element.21), channel_id=1, source_target_pairs={{0,0},{1,8},{2,2},{3,10},{4,4},{5,12},{6,6},{7,14},{8,1},{9,9},{10... | collective-permute-start | bytes 786440 | tf_op jit(solution)/shard_map/ppermute | solution.py:223
  9.8 8.4 %collective-permute-start.10 = (bf16[512,256]{1,0:T(8,128)(2,1)S(1)}, bf16[512,256]{1,0:T(8,128)(2,1)S(1)}, u32[]{:S(2)}, u32[]{:S(2)}) collective-permute-start(bf16[512,256]{1,0:T(8,128)(2,1)S(1)} %get-tuple-element.22), channel_id=1, source_target_pairs={{0,1},{1,9},{2,3},{3,11},{4,5},{5,13},{6,7},{7,15},{8,0},{9,8},{10... | collective-permute-start | bytes 786440 | tf_op jit(solution)/shard_map/ppermute | solution.py:223
  9.9 12.3 %collective-permute-start.11 = (bf16[512,256]{1,0:T(8,128)(2,1)S(1)}, bf16[512,256]{1,0:T(8,128)(2,1)S(1)}, u32[]{:S(2)}, u32[]{:S(2)}) collective-permute-start(bf16[512,256]{1,0:T(8,128)(2,1)S(1)} %get-tuple-element.23), channel_id=1, source_target_pairs={{0,16},{1,24},{2,18},{3,26},{4,20},{5,28},{6,22},{7,30},{8,17},{9,... | collective-permute-start | bytes 786440 | tf_op jit(solution)/shard_map/ppermute | solution.py:223
  10.9 13.6 %collective-permute-start.12 = (bf16[512,256]{1,0:T(8,128)(2,1)S(1)}, bf16[512,256]{1,0:T(8,128)(2,1)S(1)}, u32[]{:S(2)}, u32[]{:S(2)}) collective-permute-start(bf16[512,256]{1,0:T(8,128)(2,1)S(1)} %get-tuple-element.24), channel_id=1, source_target_pairs={{0,17},{1,25},{2,19},{3,27},{4,21},{5,29},{6,23},{7,31},{8,16},{9,... | collective-permute-start | bytes 786440 | tf_op jit(solution)/shard_map/ppermute | solution.py:223
  11.9 1.3 %copy-start = (bf16[1,768,768]{2,1,0:T(8,128)(2,1)S(1)}, bf16[1,768,768]{2,1,0:T(8,128)(2,1)}, u32[]{:S(2)}) copy-start(bf16[1,768,768]{2,1,0:T(8,128)(2,1)} %param.11) | copy-start | bytes 3538948
  13.2 0.7 copy-start.7
  15.0 11.5 %collective-permute-start.4 = (bf16[2,384,256]{2,1,0:T(8,128)(2,1)S(1)}, bf16[2,384,256]{2,1,0:T(8,128)(2,1)S(1)}, u32[]{:S(2)}, u32[]{:S(2)}) collective-permute-start(bf16[2,384,256]{2,1,0:T(8,128)(2,1)S(1)} %get-tuple-element.20), channel_id=1, source_target_pairs={{1,8},{3,10},{5,12},{7,14},{8,1},{10,3},{12,5},{14,7},{17,24},{19,... | collective-permute-start | bytes 1179656 | tf_op jit(solution)/shard_map/ppermute | solution.py:223
  18.1 8.5 %collective-permute-start = (bf16[384,256]{1,0:T(8,128)(2,1)S(1)}, bf16[384,256]{1,0:T(8,128)(2,1)S(1)}, u32[]{:S(2)}, u32[]{:S(2)}) collective-permute-start(bf16[384,256]{1,0:T(8,128)(2,1)S(1)} %get-tuple-element.19), channel_id=1, source_target_pairs={{0,8},{8,0},{16,24},{24,16},{1,9},{9,1},{17,25},{25,17},{2,10},{10... | collective-permute-start | bytes 589832 | tf_op jit(solution)/shard_map/ppermute | solution.py:220
  24.7 29.4 %copy-start.8 = (s32[4]{0:T(128)S(1)}, s32[4]{0:T(128)}, u32[]{:S(2)}) copy-start(s32[4]{0:T(128)} %front_blocks.3) | copy-start | bytes 52
  24.7 29.4 %collective-permute-start.13 = (bf16[8,256,256]{2,1,0:T(8,128)(2,1)S(1)}, bf16[8,256,256]{2,1,0:T(8,128)(2,1)S(1)}, u32[]{:S(2)}, u32[]{:S(2)}) collective-permute-start(bf16[8,256,256]{2,1,0:T(8,128)(2,1)S(1)} %bitcast.24), channel_id=1, source_target_pairs={{0,8},{8,0},{16,24},{24,16},{1,9},{9,1},{17,25},{25,17},{2,10},{10... | collective-permute-start | bytes 3145736 | tf_op jit(solution)/shard_map/ppermute | solution.py:220
  26.6 1.5 %collective-permute-start.5 = (bf16[384,256]{1,0:T(8,128)(2,1)S(1)}, bf16[384,256]{1,0:T(8,128)(2,1)S(1)}, u32[]{:S(2)}, u32[]{:S(2)}) collective-permute-start(bf16[384,256]{1,0:T(8,128)(2,1)S(1)} %slice_bitcast_fusion.1), channel_id=1, source_target_pairs={{0,8},{8,0},{16,24},{24,16},{1,9},{9,1},{17,25},{25,17},{2,10},{10... | collective-permute-start | bytes 589832 | tf_op jit(solution)/shard_map/ppermute | solution.py:220
  26.7 6.9 %collective-permute-start.1 = (bf16[384,256]{1,0:T(8,128)(2,1)S(1)}, bf16[384,256]{1,0:T(8,128)(2,1)S(1)}, u32[]{:S(2)}, u32[]{:S(2)}) collective-permute-start(bf16[384,256]{1,0:T(8,128)(2,1)S(1)} %broadcast_select_fusion.rest_0_), channel_id=1, source_target_pairs={{0,2},{1,3},{2,6},{3,7},{6,4},{7,5},{4,0},{5,1},{8,10},{9,11},{10,... | collective-permute-start | bytes 589832 | tf_op jit(solution)/shard_map/ppermute | solution.py:262
  28.1 9.7 %collective-permute-start.6 = (bf16[384,256]{1,0:T(8,128)(2,1)S(1)}, bf16[384,256]{1,0:T(8,128)(2,1)S(1)}, u32[]{:S(2)}, u32[]{:S(2)}) collective-permute-start(bf16[384,256]{1,0:T(8,128)(2,1)S(1)} %fusion.rest_4_), channel_id=1, source_target_pairs={{0,2},{1,3},{2,6},{3,7},{6,4},{7,5},{4,0},{5,1},{8,10},{9,11},{10,... | collective-permute-start | bytes 589832 | tf_op jit(solution)/shard_map/ppermute | solution.py:263
  33.6 8.1 %collective-permute-start.2 = (bf16[384,256]{1,0:T(8,128)(2,1)S(1)}, bf16[384,256]{1,0:T(8,128)(2,1)S(1)}, u32[]{:S(2)}, u32[]{:S(2)}) collective-permute-start(bf16[384,256]{1,0:T(8,128)(2,1)S(1)} %collective-permute-done.1.rest_1_), channel_id=1, source_target_pairs={{0,2},{1,3},{2,6},{3,7},{6,4},{7,5},{4,0},{5,1},{8,10},{9,11},{10,... | collective-permute-start | bytes 589832 | tf_op jit(solution)/shard_map/ppermute | solution.py:262
  37.8 8.1 %collective-permute-start.7 = (bf16[384,256]{1,0:T(8,128)(2,1)S(1)}, bf16[384,256]{1,0:T(8,128)(2,1)S(1)}, u32[]{:S(2)}, u32[]{:S(2)}) collective-permute-start(bf16[384,256]{1,0:T(8,128)(2,1)S(1)} %collective-permute-done.6.rest_5_), channel_id=1, source_target_pairs={{0,2},{1,3},{2,6},{3,7},{6,4},{7,5},{4,0},{5,1},{8,10},{9,11},{10,... | collective-permute-start | bytes 589832 | tf_op jit(solution)/shard_map/ppermute | solution.py:263
  41.7 8.1 %collective-permute-start.3 = (bf16[384,256]{1,0:T(8,128)(2,1)S(1)}, bf16[384,256]{1,0:T(8,128)(2,1)S(1)}, u32[]{:S(2)}, u32[]{:S(2)}) collective-permute-start(bf16[384,256]{1,0:T(8,128)(2,1)S(1)} %collective-permute-done.2.rest_2_), channel_id=1, source_target_pairs={{0,2},{1,3},{2,6},{3,7},{6,4},{7,5},{4,0},{5,1},{8,10},{9,11},{10,... | collective-permute-start | bytes 589832 | tf_op jit(solution)/shard_map/ppermute | solution.py:262
  46.0 8.1 %collective-permute-start.8 = (bf16[384,256]{1,0:T(8,128)(2,1)S(1)}, bf16[384,256]{1,0:T(8,128)(2,1)S(1)}, u32[]{:S(2)}, u32[]{:S(2)}) collective-permute-start(bf16[384,256]{1,0:T(8,128)(2,1)S(1)} %collective-permute-done.7.rest_6_), channel_id=1, source_target_pairs={{0,2},{1,3},{2,6},{3,7},{6,4},{7,5},{4,0},{5,1},{8,10},{9,11},{10,... | collective-permute-start | bytes 589832 | tf_op jit(solution)/shard_map/ppermute | solution.py:263
  56.4 10.1 %copy-start.4 = (bf16[96,512]{1,0:T(8,128)(2,1)}, bf16[96,512]{1,0:T(8,128)(2,1)S(1)}, u32[]{:S(2)}) copy-start(bf16[96,512]{1,0:T(8,128)(2,1)S(1)} %get-tuple-element.27.rest_0_) | copy-start | bytes 294916
  56.4 20.3 %collective-permute-start.19 = (bf16[8,384,256]{2,1,0:T(8,128)(2,1)S(1)}, bf16[8,384,256]{2,1,0:T(8,128)(2,1)S(1)}, u32[]{:S(2)}, u32[]{:S(2)}) collective-permute-start(bf16[8,384,256]{2,1,0:T(8,128)(2,1)S(1)} %get-tuple-element.31.rest_4_), channel_id=1, source_target_pairs={{0,8},{8,0},{16,24},{24,16},{1,9},{9,1},{17,25},{25,17},{2,10},{10... | collective-permute-start | bytes 4718600 | tf_op jit(solution)/shard_map/ppermute | solution.py:220
  58.3 3.3 %collective-permute-start.14 = (bf16[384,256]{1,0:T(8,128)(2,1)S(1)}, bf16[384,256]{1,0:T(8,128)(2,1)S(1)}, u32[]{:S(2)}, u32[]{:S(2)}) collective-permute-start(bf16[384,256]{1,0:T(8,128)(2,1)S(1)} %get-tuple-element.26), channel_id=1, source_target_pairs={{0,8},{8,0},{16,24},{24,16},{1,9},{9,1},{17,25},{25,17},{2,10},{10... | collective-permute-start | bytes 589832 | tf_op jit(solution)/shard_map/ppermute | solution.py:220
  62.4 21.6 %collective-permute-start.15 = (bf16[256,768]{1,0:T(8,128)(2,1)S(1)}, bf16[256,768]{1,0:T(8,128)(2,1)}, u32[]{:S(2)}, u32[]{:S(2)}) collective-permute-start(bf16[256,768]{1,0:T(8,128)(2,1)S(1)} %turn.1), channel_id=1, source_target_pairs={{0,0},{1,8},{2,2},{3,10},{4,4},{5,12},{6,6},{7,14},{8,1},{9,9},{10... | collective-permute-start | bytes 1179656 | tf_op jit(solution)/shard_map/ppermute | solution.py:223
  66.4 4.7 %collective-permute-start.16 = (bf16[96,512]{1,0:T(8,128)(2,1)}, bf16[96,512]{1,0:T(8,128)(2,1)}, u32[]{:S(2)}, u32[]{:S(2)}) collective-permute-start(bf16[96,512]{1,0:T(8,128)(2,1)} %get-tuple-element.28), channel_id=1, source_target_pairs={{0,2},{1,3},{2,0},{3,1},{4,6},{5,7},{6,4},{7,5},{8,10},{9,11},{10,... | collective-permute-start | bytes 294920 | tf_op jit(solution)/shard_map/ppermute | solution.py:278
  67.0 9.7 %collective-permute-start.17 = (bf16[96,512]{1,0:T(8,128)(2,1)}, bf16[96,512]{1,0:T(8,128)(2,1)}, u32[]{:S(2)}, u32[]{:S(2)}) collective-permute-start(bf16[96,512]{1,0:T(8,128)(2,1)} %get-tuple-element.29), channel_id=1, source_target_pairs={{0,4},{1,5},{2,6},{3,7},{4,0},{5,1},{6,2},{7,3},{8,12},{9,13},{10,... | collective-permute-start | bytes 294920 | tf_op jit(solution)/shard_map/ppermute | solution.py:278
  70.1 6.6 %collective-permute-start.18 = (bf16[96,512]{1,0:T(8,128)(2,1)}, bf16[96,512]{1,0:T(8,128)(2,1)}, u32[]{:S(2)}, u32[]{:S(2)}) collective-permute-start(bf16[96,512]{1,0:T(8,128)(2,1)} %get-tuple-element.30), channel_id=1, source_target_pairs={{0,6},{1,7},{2,4},{3,5},{4,2},{5,3},{6,0},{7,1},{8,14},{9,15},{10,... | collective-permute-start | bytes 294920 | tf_op jit(solution)/shard_map/ppermute | solution.py:278
  76.7 0.9 %copy-start.5 = (bf16[96,512]{1,0:T(8,128)(2,1)S(1)}, bf16[96,512]{1,0:T(8,128)(2,1)}, u32[]{:S(2)}) copy-start(bf16[96,512]{1,0:T(8,128)(2,1)} %copy-done.4) | copy-start | bytes 294916
  77.6 6.0 %copy-start.1 = (bf16[1,768,768]{2,1,0:T(8,128)(2,1)S(1)}, bf16[1,768,768]{2,1,0:T(8,128)(2,1)}, u32[]{:S(2)}) copy-start(bf16[1,768,768]{2,1,0:T(8,128)(2,1)} %param.11) | copy-start | bytes 3538948
  79.9 6.5 %collective-permute-start.20 = (bf16[96,768]{1,0:T(8,128)(2,1)S(1)}, bf16[96,768]{1,0:T(8,128)(2,1)S(1)}, u32[]{:S(2)}, u32[]{:S(2)}) collective-permute-start(bf16[96,768]{1,0:T(8,128)(2,1)S(1)} %pivot.1), channel_id=1, source_target_pairs={{0,0},{1,8},{2,2},{3,10},{4,4},{5,12},{6,6},{7,14},{8,1},{9,9},{10... | collective-permute-start | bytes 442376 | tf_op jit(solution)/shard_map/ppermute | solution.py:223

commit v2 on v1

v2 whole, which is shorter than its diff:
```python
import functools

import jax
import jax.numpy as jnp
from jax import lax
from jax.experimental import pallas as pl
from jax.experimental.pallas import tpu as pltpu
from jax.sharding import PartitionSpec as P

BLK = 128
F32 = jnp.float32
BF16 = jnp.bfloat16

VMEM = pl.BlockSpec(memory_space=pltpu.VMEM)
SMEM = pl.BlockSpec(memory_space=pltpu.SMEM)
HBM = pl.BlockSpec(memory_space=pltpu.HBM)


def power_of_two(n):
    return n & (n - 1) == 0


def peer(q, k, n):
    return q ^ k if power_of_two(n) else (q + k) % n


def source(q, k, n):
    return q ^ k if power_of_two(n) else (q + n - k) % n


def ring_place(position, n):
    return position ^ (position >> 1) if power_of_two(n) else position


def ring_position(place, n):
    position = place
    if power_of_two(n):
        shift = 1
        while shift < n:
            position = position ^ (place >> shift)
            shift += 1
    return position


def coordinates():
    g, p = lax.axis_index("grp"), lax.axis_index("pan")
    return g >> 1, g & 1, p >> 1, p & 1


def params(mib=40):
    return pltpu.CompilerParams(vmem_limit_bytes=mib * 1024 * 1024)


def pack_kernel(groups, pan, row_home_in, lists_in, anc, other_anc, *rest):
    pairs = groups // 2
    outs, members = rest[:pairs], rest[pairs]
    row_home, lists, sems = rest[pairs + 1 :]
    h, c, q, l = coordinates()
    p = 2 * q + l
    loads = [
        pltpu.make_async_copy(row_home_in, row_home, sems.at[pairs]),
        pltpu.make_async_copy(lists_in, lists, sems.at[pairs + 1]),
    ]
    for load in loads:
        load.start()
    for load in loads:
        load.wait()
    stored = anc.shape[0] // BLK
    window_blocks = anc.shape[1] // BLK
    picked = lists.shape[1] // pan
    windows = pan // groups
    depth = picked * BLK

    def window(w, ranks):
        owner = row_home[window_blocks * w] // stored
        counts = []
        for core, rank in enumerate(ranks):
            mine = owner == 2 * h + core
            counts.append(rank + mine.astype(jnp.int32))
            for local in range(2):

                @pl.when(mine & ((c == core) == (local == 0)))
                def _():
                    origin = (anc, other_anc)[local]
                    for k in range(pairs):
                        front = 2 * peer(h, k, pairs) + c
                        for r in range(picked):
                            row = row_home[lists[front, picked * w + r]] - stored * owner
                            at = ((core * windows + rank) * picked + r) * BLK
                            for s in range(picked):
                                column = lists[front, picked * p + s] - window_blocks * p
                                pltpu.make_async_copy(
                                    origin.at[pl.ds(row * BLK, BLK), pl.ds(column * BLK, BLK)],
                                    outs[k].at[pl.ds(at, BLK), pl.ds(s * BLK, BLK)],
                                    sems.at[k],
                                ).start()

        return tuple(counts)

    lax.fori_loop(0, pan, window, (jnp.int32(0), jnp.int32(0)))
    owners = [row_home[window_blocks * w] // stored for w in range(pan)]
    for w in range(pan):
        rank = jnp.int32(0)
        for v in range(w):
            rank = rank + (owners[v] == owners[w]).astype(jnp.int32)
        step = owners[w] >> 1
        step = step ^ h if power_of_two(pairs) else (h + pairs - step) % pairs
        members[(2 * step + (owners[w] & 1)) * windows + rank] = jnp.int32(w)
    rows, columns = outs[0].shape
    for k in range(pairs):
        pltpu.make_async_copy(
            anc.at[pl.ds(0, rows), pl.ds(0, columns)], outs[k], sems.at[k]
        ).wait()


def scale_kernel(
    pan, front_blocks_in, panel_in, inverse_in, keep, give, panel, inverse, turned, front_blocks, sems
):
    h, c, q, l = coordinates()
    g, p = 2 * h + c, 2 * q + l
    loads = [
        pltpu.make_async_copy(inverse_in, inverse, sems.at[0]),
        pltpu.make_async_copy(panel_in, panel, sems.at[1]),
        pltpu.make_async_copy(front_blocks_in, front_blocks, sems.at[2]),
    ]
    for load in loads:
        load.start()
    for load in loads:
        load.wait()
    rows, width = panel.shape
    n, share = pan // 2, width // pan
    padded = keep.shape[0] // n
    live = front_blocks[g]
    scaled = jnp.dot(panel[...], inverse[...], preferred_element_type=F32)
    row = lax.broadcasted_iota(jnp.int32, scaled.shape, 0)
    scaled = jnp.where(p * (rows // BLK) + row // BLK < live, scaled, 0.0)
    turned[...] = scaled.T
    if padded != share:
        keep[...] = jnp.zeros_like(keep)
        give[...] = jnp.zeros_like(give)
    for place in range(n):
        at = pl.ds(place * padded, share)
        keep[at] = turned[pl.ds(share * (2 * place + c), share)].astype(BF16)
        give[at] = turned[pl.ds(share * (2 * place + 1 - c), share)].astype(BF16)


def cross_kernel(n, groups, front_blocks, members, *rest):
    near, far = rest[:n], rest[n : 2 * n]
    rest = rest[2 * n :]
    pairs = groups // 2
    own_sigma, other_sigma = rest[:pairs], rest[pairs : 2 * pairs]
    rest = rest[2 * pairs :]
    mine, give, whole = rest[:3]
    parts, total = rest[3 : n + 3], rest[n + 3]
    h, c, q, l = coordinates()
    half, rows = near[0].shape
    padded = half // n
    position = ring_position(q, n)
    for step in range(n):
        origin = ring_place((position + n - step) % n, n)
        whole[2 * origin + l] = near[step][...]
        whole[2 * origin + (1 - l)] = far[step][...]
    own = jnp.zeros((half, rows), F32)
    other = jnp.zeros((half, rows), F32)
    windows = 2 * n // pairs
    depth = own_sigma[0].shape[0] // windows
    for slot in range(2 * n):
        chunk = whole[members[slot]]
        at = pl.ds(slot % windows * depth, depth)
        own = own + jnp.dot(chunk, own_sigma[slot // windows][at], preferred_element_type=F32)
        other = other + jnp.dot(chunk, other_sigma[slot // windows][at], preferred_element_type=F32)
    live = front_blocks[2 * h + l]
    block = lax.broadcasted_iota(jnp.int32, (half, rows), 1) // BLK
    own = jnp.where((2 * q + c) * (rows // BLK) + block < live, -own, 0.0)
    other = jnp.where((2 * q + 1 - c) * (rows // BLK) + block < live, -other, 0.0)
    mine[...] = own.astype(BF16)
    give[...] = other.astype(BF16)
    total[c] = own
    total[1 - c] = other
    for k in range(n):
        at = pl.ds(peer(q, k, n) * padded, padded)
        for side in range(2):
            parts[k][:, pl.ds(side * rows, rows)] = total[side, at].astype(BF16)


def pivot_first_kernel(n, part, own_scaled, other_scaled, own_out, other_out):
    _, _, q, _ = coordinates()
    own, other = pivot_terms(part, q, own_scaled, other_scaled)
    own_out[...] = own
    other_out[...] = other


def pivot_terms(part, origin, own_scaled, other_scaled):
    rows = own_scaled.shape[2]
    sums = [None, None]
    for side in range(2):
        piece = part[:, pl.ds(side * rows, rows)]
        for i, scaled in enumerate((own_scaled, other_scaled)):
            term = lax.dot_general(
                piece, scaled[2 * origin + side], (((1,), (1,)), ((), ())), preferred_element_type=F32
            )
            sums[i] = term if sums[i] is None else sums[i] + term
    return sums


def pivot_kernel(n, share, *rest):
    own_first, other_first = rest[:2]
    parts, own_scaled, other_scaled, out = rest[2 : n + 1], rest[n + 1], rest[n + 2], rest[n + 3]
    _, c, q, _ = coordinates()
    padded = parts[0].shape[0]
    own, other = own_first[...], other_first[...]
    for k in range(1, n):
        terms = pivot_terms(parts[k - 1], source(q, k, n), own_scaled, other_scaled)
        own, other = own + terms[0], other + terms[1]
    low = jnp.where(c == 0, own, other)
    high = jnp.where(c == 0, other, own)
    pieces = []
    for place in range(n):
        at = slice(place * padded, place * padded + share)
        pieces += [low[:, at], high[:, at]]
    out[...] = (-jnp.concatenate(pieces, axis=1)).astype(BF16)


def turn_kernel(pan, share, mine, other, out, natural):
    _, c, _, _ = coordinates()
    n = pan // 2
    padded = mine.shape[0] // n
    for place in range(n):
        at = pl.ds(place * padded, share)
        natural[pl.ds(share * (2 * place + c), share)] = mine[at].astype(F32)
        natural[pl.ds(share * (2 * place + 1 - c), share)] = other[at].astype(F32)
    out[...] = natural[...].T.astype(BF16)


def per_device(anc_rows, row_home, block_lists, front_blocks, panel, pivot_inverse):
    groups, pan = lax.axis_size("grp"), lax.axis_size("pan")
    n, pairs = pan // 2, groups // 2
    rows, width = panel.shape[1:]
    share = width // pan
    padded = -(-share // 16) * 16
    half = n * padded
    wanted = block_lists.shape[1] // groups * BLK
    windows = pan // groups
    diagonal = (lax.axis_index("grp") ^ lax.axis_index("pan")) & 1 == 0
    inverse = pivot_inverse[0]
    shape = jax.ShapeDtypeStruct

    def at(h, c, q, l):
        return (2 * h + c) * pan + 2 * q + l

    places = [
        (h, c, q, l) for h in range(pairs) for c in range(2) for q in range(n) for l in range(2)
    ]
    exchange = [(at(h, c, q, l), at(h, l, q, c)) for h, c, q, l in places]
    crossing = [(a, b) for a, b in exchange if a != b]
    to_sibling = [(at(h, c, q, l), at(h, 1 - c, q, l)) for h, c, q, l in places if c == l]
    to_diagonal = [(at(h, c, q, l), at(h, c, q, c)) for h, c, q, l in places if c != l]
    cores = [(g, g ^ 1) for g in range(groups)]
    ring = [
        (2 * ring_place(i, n) + l, 2 * ring_place((i + 1) % n, n) + l)
        for i in range(n)
        for l in range(2)
    ]

    def swap(x):
        return lax.ppermute(x, "grp", cores)

    def everywhere(x, pairs_of):
        return lax.ppermute(x, ("grp", "pan"), pairs_of)

    keep, give = pl.pallas_call(
        functools.partial(scale_kernel, pan),
        out_shape=[shape((half, rows), BF16)] * 2,
        in_specs=[HBM] * 3,
        out_specs=[VMEM] * 2,
        scratch_shapes=[
            pltpu.VMEM((rows, width), BF16),
            pltpu.VMEM((width, width), BF16),
            pltpu.VMEM((width, rows), F32),
            pltpu.SMEM(front_blocks.shape, jnp.int32),
            pltpu.SemaphoreType.DMA((3,)),
        ],
        compiler_params=params(60),
        name="scale",
    )(front_blocks, panel[0], inverse)
    given = everywhere(give, to_sibling)
    keep, give, given = lax.optimization_barrier((keep, give, given))
    near = jnp.where(diagonal, keep, given)
    far = jnp.where(diagonal, everywhere(keep, to_diagonal), everywhere(give, crossing))

    *packed, members = pl.pallas_call(
        functools.partial(pack_kernel, groups, pan),
        out_shape=[shape((2 * wanted, rows), BF16)] * pairs + [shape((pan,), jnp.int32)],
        in_specs=[HBM] * 4,
        out_specs=[HBM] * pairs + [SMEM],
        scratch_shapes=[
            pltpu.SMEM(row_home.shape, jnp.int32),
            pltpu.SMEM(block_lists.shape, jnp.int32),
            pltpu.SemaphoreType.DMA((pairs + 2,)),
        ],
        compiler_params=params(),
        name="pack",
    )(row_home, block_lists, anc_rows, swap(anc_rows))
    arrived = [
        everywhere(
            packed[k], [(at(h, c, q, l), at(peer(h, k, pairs), l, q, c)) for h, c, q, l in places]
        )
        for k in range(pairs)
    ]
    own_columns = lax.dynamic_slice_in_dim(inverse, lax.axis_index("pan") * share, share, 1)
    triangle = lax.dot_general(
        own_columns, inverse, (((0,), (0,)), ((), ())), preferred_element_type=F32
    )

    nears, fars = [near], [far]
    for step in range(1, n):
        nears.append(lax.ppermute(nears[-1], "pan", ring))
        fars.append(lax.ppermute(fars[-1], "pan", ring))

    arrived, triangle, _ = lax.optimization_barrier((arrived, triangle, nears[min(2, n - 1)]))
    swapped = [swap(piece) for piece in arrived]
    mine, give, whole, *parts = pl.pallas_call(
        functools.partial(cross_kernel, n, groups),
        out_shape=[shape((half, rows), BF16)] * 2
        + [shape((pan, half, rows), BF16)]
        + [shape((padded, 2 * rows), BF16)] * n,
        in_specs=[SMEM] * 2 + [VMEM] * (2 * n + groups),
        out_specs=[VMEM] * (n + 3),
        scratch_shapes=[pltpu.VMEM((2, half, rows), F32)],
        compiler_params=params(),
        name="cross",
    )(front_blocks, members, *nears, *fars, *arrived, *swapped)

    for k in range(1, n):
        parts[k] = lax.ppermute(
            parts[k], "pan", [(2 * q + l, 2 * peer(q, k, n) + l) for q in range(n) for l in range(2)]
        )
    other_whole = swap(whole)
    turned = pl.pallas_call(
        functools.partial(turn_kernel, pan, share),
        out_shape=shape((rows, width), BF16),
        in_specs=[VMEM, VMEM],
        out_specs=VMEM,
        scratch_shapes=[pltpu.VMEM((width, rows), F32)],
        compiler_params=params(),
        name="turn",
    )(mine, swap(give))
    cross = jnp.where(diagonal, turned, everywhere(turned, crossing))

    firsts = pl.pallas_call(
        functools.partial(pivot_first_kernel, n),
        out_shape=[shape((padded, half), F32)] * 2,
        in_specs=[VMEM] * 3,
        out_specs=[VMEM] * 2,
        compiler_params=params(),
        name="pivot_first",
    )(parts[0], whole, other_whole)
    term = pl.pallas_call(
        functools.partial(pivot_kernel, n, share),
        out_shape=shape((padded, width), BF16),
        in_specs=[VMEM] * (n + 3),
        out_specs=VMEM,
        compiler_params=params(),
        name="pivot",
    )(*firsts, *parts[1:], whole, other_whole)
    term, cross = lax.optimization_barrier((term, cross))
    term = jnp.where(diagonal, term, everywhere(term, crossing))
    pivot = triangle + term[:share].astype(F32)
    return cross[None], pivot[None]


def solution(mesh):
    placed = (P("grp", "pan"), P(), P(), P(), P("grp", "pan", None), P("grp", None, None))
    return jax.shard_map(
        per_device,
        mesh=mesh,
        in_specs=placed,
        out_specs=(P("grp", "pan", None), P("grp", "pan", None)),
        check_vma=False,
    )
```

time: 89.3 us -> 78.2 us (0.88)
  waiting for transfers between devices: 41.2 us -> 30 us
  local copies, waits for them, and re-layouts: 7.17 us -> 0.03 us
  starting transfers between devices: 29.7 us -> 36.6 us
    unnamed x21 -> x12, local copies, waits for them, and re-layouts: 7.16 us -> 0.03 us
    ppermute x3, waiting for transfers between devices: 11.4 us -> 7.06 us  [per_device(): fars.append(lax.ppermute(fars[-1], 'pan', ring))]
    ppermute x3, waiting for transfers between devices: 6.59 us -> 2.53 us  [per_device(): lax.ppermute(parts[k], 'pan', [(2 * q + l, 2 * peer(q, k, n) + l) for q i...]
    ppermute x7, starting transfers between devices: 17.3 us -> 20.8 us  [everywhere(): return lax.ppermute(x, ('grp', 'pan'), pairs_of)]
    ppermute x7, waiting for transfers between devices: 10.1 us -> 6.83 us  [everywhere(): return lax.ppermute(x, ('grp', 'pan'), pairs_of)]
    ppermute x3, starting transfers between devices: 2.57 us -> 5.34 us  [per_device(): nears.append(lax.ppermute(nears[-1], 'pan', ring))]
    pallas_call x1, Pallas kernels: 1.2 us -> 2.86 us  [per_device(): pl.pallas_call(functools.partial(scale_kernel, pan), out_shape=[shape((ha...]
    ppermute x3, starting transfers between devices: 3.55 us -> 4.86 us  [per_device(): fars.append(lax.ppermute(fars[-1], 'pan', ring))]
  transfers between devices with their start and end apart: 21 -> 21, of which waited for: 13 -> 10; matrix products, arithmetic and copies ran while one was open for 1% -> 2% of each run, Pallas kernels for 5% -> 7%
where the time goes in v2:
time: 78.2 us; the launch traced here: 78 us
  starting transfers between devices  36.6 us (47%)
  waiting for transfers between devices  30 us (38%)
  Pallas kernels  8.4 us (11%)
  other arithmetic  1.6 us (2%)
  between operations  0.85 us (1%)
    ppermute x7, starting transfers between devices, everywhere(): return lax.ppermute(x, ('grp', 'pan'), pairs_of)  20.8 us
    ppermute x3, waiting for transfers between devices, per_device(): nears.append(lax.ppermute(nears[-1], 'pan', ring))  10.4 us
    ppermute x3, waiting for transfers between devices, per_device(): fars.append(lax.ppermute(fars[-1], 'pan', ring))  7.06 us
    ppermute x7, waiting for transfers between devices, everywhere(): return lax.ppermute(x, ('grp', 'pan'), pairs_of)  6.83 us
    ppermute x3, starting transfers between devices, per_device(): nears.append(lax.ppermute(nears[-1], 'pan', ring))  5.34 us
    ppermute x3, starting transfers between devices, per_device(): fars.append(lax.ppermute(fars[-1], 'pan', ring))  4.86 us
    ppermute x3, starting transfers between devices, per_device(): lax.ppermute(parts[k], 'pan', [(2 * q + l, 2 * peer(q, k, n) + l) for q i...  3.67 us
    ppermute x5, waiting for transfers between devices, swap(): return lax.ppermute(x, 'grp', cores)  3.25 us
  transfers between devices with their start and end apart: 21, of which 10 were waited for; matrix products, arithmetic and copies ran while one was open for 2% of the time, Pallas kernels for 7%

profile of v2, /device:TPU:1, one launch (start us, length us, event | category | flops | bytes accessed | tf_op | source)
XLA Modules:
  0.0 78.0 jit_solution(13592239101044345400)
XLA Ops:
  0.7 0.1 collective-permute-start
  0.8 2.9 %scale.1 = (bf16[384,256]{1,0:T(8,128)(2,1)}, bf16[384,256]{1,0:T(8,128)(2,1)}) custom-call(s32[4]{0:T(128)} %front_blocks.1, bf16[256,768]{1,0:T(8,128)(2,1)} %bitcast.11, bf16[768,768]{1,0:T(8,128)(2,1)} %bitcast.10), custom_call_target="tpu_custom_call" | custom-call | tf_op jit(solution)/shard_map/scale/pallas_call | solution.py:271
  3.7 0.0 copy-start.5
  3.7 1.4 %collective-permute-start.1 = (bf16[384,256]{1,0:T(8,128)(2,1)}, bf16[384,256]{1,0:T(8,128)(2,1)S(1)}, u32[]{:S(2)}, u32[]{:S(2)}) collective-permute-start(bf16[384,256]{1,0:T(8,128)(2,1)} %get-tuple-element.29), channel_id=1, source_target_pairs={{0,8},{2,10},{4,12},{6,14},{9,1},{11,3},{13,5},{15,7},{16,24},{18,... | collective-permute-start | bytes 589832 | tf_op jit(solution)/shard_map/ppermute | solution.py:269
  5.1 2.2 %collective-permute-done.1 = bf16[384,256]{1,0:T(8,128)(2,1)S(1)} collective-permute-done((bf16[384,256]{1,0:T(8,128)(2,1)}, bf16[384,256]{1,0:T(8,128)(2,1)S(1)}, u32[]{:S(2)}, u32[]{:S(2)}) %collective-permute-start.1) | collective-permute-done | bytes 196640 | tf_op jit(solution)/shard_map/ppermute | solution.py:269
  7.3 4.6 %collective-permute-start.6 = (bf16[384,256]{1,0:T(8,128)(2,1)}, bf16[384,256]{1,0:T(8,128)(2,1)S(1)}, u32[]{:S(2)}, u32[]{:S(2)}) collective-permute-start(bf16[384,256]{1,0:T(8,128)(2,1)} %get-tuple-element.29), channel_id=1, source_target_pairs={{1,8},{3,10},{5,12},{7,14},{8,1},{10,3},{12,5},{14,7},{17,24},{19,... | collective-permute-start | bytes 589832 | tf_op jit(solution)/shard_map/ppermute | solution.py:269
  11.9 1.3 %collective-permute-start.5 = (bf16[384,256]{1,0:T(8,128)(2,1)}, bf16[384,256]{1,0:T(8,128)(2,1)S(1)}, u32[]{:S(2)}, u32[]{:S(2)}) collective-permute-start(bf16[384,256]{1,0:T(8,128)(2,1)} %get-tuple-element.27), channel_id=1, source_target_pairs={{1,0},{3,2},{5,4},{7,6},{8,9},{10,11},{12,13},{14,15},{17,16},{19,... | collective-permute-start | bytes 589832 | tf_op jit(solution)/shard_map/ppermute | solution.py:269
  13.2 0.0 collective-permute-done.other_anc
  13.3 2.3 %pack.1 = (bf16[1024,256]{1,0:T(8,128)(2,1)S(1)}, bf16[1024,256]{1,0:T(8,128)(2,1)S(1)}, s32[8]{0:T(128)S(1)}) custom-call(s32[32]{0:T(128)S(1)} %copy-done.3, s32[4,16]{1,0:T(4,128)S(1)} %copy-done.2, bf16[1024,512]{1,0:T(8,128)(2,1)S(1)} %copy-done, bf16[1024,512]{1,0:T(8,128)(2,1)S(1)} %collective-permute-done.other_anc), custom_call_target="tpu_custom_call" | custom-call | tf_op jit(solution)/shard_map/pack/pallas_call | solution.py:291
  15.5 1.9 %collective-permute-start.10 = (bf16[1024,256]{1,0:T(8,128)(2,1)S(1)}, bf16[1024,256]{1,0:T(8,128)(2,1)S(1)}, u32[]{:S(2)}, u32[]{:S(2)}) collective-permute-start(bf16[1024,256]{1,0:T(8,128)(2,1)S(1)} %get-tuple-element.30), channel_id=1, source_target_pairs={{0,0},{1,8},{2,2},{3,10},{4,4},{5,12},{6,6},{7,14},{8,1},{9,9},{10... | collective-permute-start | bytes 1572872 | tf_op jit(solution)/shard_map/ppermute | solution.py:269
  17.5 2.8 %collective-permute-start.11 = (bf16[1024,256]{1,0:T(8,128)(2,1)S(1)}, bf16[1024,256]{1,0:T(8,128)(2,1)S(1)}, u32[]{:S(2)}, u32[]{:S(2)}) collective-permute-start(bf16[1024,256]{1,0:T(8,128)(2,1)S(1)} %get-tuple-element.31), channel_id=1, source_target_pairs={{0,16},{1,24},{2,18},{3,26},{4,20},{5,28},{6,22},{7,30},{8,17},{9,... | collective-permute-start | bytes 1572872 | tf_op jit(solution)/shard_map/ppermute | solution.py:269
  20.3 0.0 copy-start.1
  20.3 1.4 %collective-permute-start.2 = (bf16[384,256]{1,0:T(8,128)(2,1)S(1)}, bf16[384,256]{1,0:T(8,128)(2,1)S(1)}, u32[]{:S(2)}, u32[]{:S(2)}) collective-permute-start(bf16[384,256]{1,0:T(8,128)(2,1)S(1)} %broadcast_select_fusion.2.rest_0_), channel_id=1, source_target_pairs={{0,2},{1,3},{2,6},{3,7},{6,4},{7,5},{4,0},{5,1},{8,10},{9,11},{10,... | collective-permute-start | bytes 589832 | tf_op jit(solution)/shard_map/ppermute | solution.py:317
  21.6 0.0 collective-permute-done.6
  21.6 0.0 collective-permute-done.5
  21.7 2.4 %collective-permute-start.7 = (bf16[384,256]{1,0:T(8,128)(2,1)S(1)}, bf16[384,256]{1,0:T(8,128)(2,1)S(1)}, u32[]{:S(2)}, u32[]{:S(2)}) collective-permute-start(bf16[384,256]{1,0:T(8,128)(2,1)S(1)} %broadcast_select_fusion.1.rest_4_), channel_id=1, source_target_pairs={{0,2},{1,3},{2,6},{3,7},{6,4},{7,5},{4,0},{5,1},{8,10},{9,11},{10,... | collective-permute-start | bytes 589832 | tf_op jit(solution)/shard_map/ppermute | solution.py:318
  24.0 3.4 %collective-permute-done.2.rest_1_ = bf16[384,256]{1,0:T(8,128)(2,1)S(1)} collective-permute-done((bf16[384,256]{1,0:T(8,128)(2,1)S(1)}, bf16[384,256]{1,0:T(8,128)(2,1)S(1)}, u32[]{:S(2)}, u32[]{:S(2)}) %collective-permute-start.2) | collective-permute-done | bytes 196640 | tf_op jit(solution)/shard_map/ppermute | solution.py:317
  27.4 1.2 %collective-permute-start.3 = (bf16[384,256]{1,0:T(8,128)(2,1)S(1)}, bf16[384,256]{1,0:T(8,128)(2,1)S(1)}, u32[]{:S(2)}, u32[]{:S(2)}) collective-permute-start(bf16[384,256]{1,0:T(8,128)(2,1)S(1)} %collective-permute-done.2.rest_1_), channel_id=1, source_target_pairs={{0,2},{1,3},{2,6},{3,7},{6,4},{7,5},{4,0},{5,1},{8,10},{9,11},{10,... | collective-permute-start | bytes 589832 | tf_op jit(solution)/shard_map/ppermute | solution.py:317
  28.6 0.4 fusion
  29.0 3.9 %collective-permute-done.3.rest_2_ = bf16[384,256]{1,0:T(8,128)(2,1)S(1)} collective-permute-done((bf16[384,256]{1,0:T(8,128)(2,1)S(1)}, bf16[384,256]{1,0:T(8,128)(2,1)S(1)}, u32[]{:S(2)}, u32[]{:S(2)}) %collective-permute-start.3) | collective-permute-done | bytes 196640 | tf_op jit(solution)/shard_map/ppermute | solution.py:317
  32.9 0.0 collective-permute-done.10.rest_8_
  32.9 0.5 collective-permute-start.13
  33.4 1.4 %collective-permute-start.8 = (bf16[384,256]{1,0:T(8,128)(2,1)S(1)}, bf16[384,256]{1,0:T(8,128)(2,1)S(1)}, u32[]{:S(2)}, u32[]{:S(2)}) collective-permute-start(bf16[384,256]{1,0:T(8,128)(2,1)S(1)} %collective-permute-done.7.rest_5_), channel_id=1, source_target_pairs={{0,2},{1,3},{2,6},{3,7},{6,4},{7,5},{4,0},{5,1},{8,10},{9,11},{10,... | collective-permute-start | bytes 589832 | tf_op jit(solution)/shard_map/ppermute | solution.py:318
  34.8 2.8 %collective-permute-start.4 = (bf16[384,256]{1,0:T(8,128)(2,1)S(1)}, bf16[384,256]{1,0:T(8,128)(2,1)S(1)}, u32[]{:S(2)}, u32[]{:S(2)}) collective-permute-start(bf16[384,256]{1,0:T(8,128)(2,1)S(1)} %collective-permute-done.3.rest_2_), channel_id=1, source_target_pairs={{0,2},{1,3},{2,6},{3,7},{6,4},{7,5},{4,0},{5,1},{8,10},{9,11},{10,... | collective-permute-start | bytes 589832 | tf_op jit(solution)/shard_map/ppermute | solution.py:317
  37.6 3.2 %collective-permute-done.8.rest_6_ = bf16[384,256]{1,0:T(8,128)(2,1)S(1)} collective-permute-done((bf16[384,256]{1,0:T(8,128)(2,1)S(1)}, bf16[384,256]{1,0:T(8,128)(2,1)S(1)}, u32[]{:S(2)}, u32[]{:S(2)}) %collective-permute-start.8) | collective-permute-done | bytes 196640 | tf_op jit(solution)/shard_map/ppermute | solution.py:318
  40.8 1.1 %collective-permute-start.9 = (bf16[384,256]{1,0:T(8,128)(2,1)S(1)}, bf16[384,256]{1,0:T(8,128)(2,1)S(1)}, u32[]{:S(2)}, u32[]{:S(2)}) collective-permute-start(bf16[384,256]{1,0:T(8,128)(2,1)S(1)} %collective-permute-done.8.rest_6_), channel_id=1, source_target_pairs={{0,2},{1,3},{2,6},{3,7},{6,4},{7,5},{4,0},{5,1},{8,10},{9,11},{10,... | collective-permute-start | bytes 589832 | tf_op jit(solution)/shard_map/ppermute | solution.py:318
  41.9 3.1 %collective-permute-done.4.rest_3_ = bf16[384,256]{1,0:T(8,128)(2,1)S(1)} collective-permute-done((bf16[384,256]{1,0:T(8,128)(2,1)S(1)}, bf16[384,256]{1,0:T(8,128)(2,1)S(1)}, u32[]{:S(2)}, u32[]{:S(2)}) %collective-permute-start.4) | collective-permute-done | bytes 196640 | tf_op jit(solution)/shard_map/ppermute | solution.py:317
  45.0 3.9 %collective-permute-done.9.rest_7_ = bf16[384,256]{1,0:T(8,128)(2,1)S(1)} collective-permute-done((bf16[384,256]{1,0:T(8,128)(2,1)S(1)}, bf16[384,256]{1,0:T(8,128)(2,1)S(1)}, u32[]{:S(2)}, u32[]{:S(2)}) %collective-permute-start.9) | collective-permute-done | bytes 196640 | tf_op jit(solution)/shard_map/ppermute | solution.py:318
  48.9 0.0 collective-permute-done.12.rest_10_
  48.9 0.0 collective-permute-done.13.rest_11_
  48.9 1.7 %cross.1 = (bf16[384,256]{1,0:T(8,128)(2,1)S(1)}, bf16[384,256]{1,0:T(8,128)(2,1)S(1)}, bf16[8,384,256]{2,1,0:T(8,128)(2,1)S(1)}, bf16[96,512]{1,0:T(8,128)(2,1)...) custom-call(s32[4]{0:T(128)S(1)} %copy-done.1, ...), custom_call_target="tpu_custom_call" | custom-call | tf_op jit(solution)/shard_map/cross/pallas_call | solution.py:322
  50.6 1.2 %collective-permute-start.14 = (bf16[8,384,256]{2,1,0:T(8,128)(2,1)S(1)}, bf16[8,384,256]{2,1,0:T(8,128)(2,1)S(1)}, u32[]{:S(2)}, u32[]{:S(2)}) collective-permute-start(bf16[8,384,256]{2,1,0:T(8,128)(2,1)S(1)} %get-tuple-element.35.own_scaled.rest_5_), channel_id=1, source_target_pairs={{0,8},{8,0},{16,24},{24,16},{1,9},{9,1},{17,25},{25,17},{2,10},{10... | collective-permute-start | bytes 4718600 | tf_op jit(solution)/shard_map/ppermute | solution.py:266
  51.8 0.1 collective-permute-start.18
  51.9 3.2 %collective-permute-done.18.other = bf16[384,256]{1,0:T(8,128)(2,1)S(1)} collective-permute-done((bf16[384,256]{1,0:T(8,128)(2,1)S(1)}, bf16[384,256]{1,0:T(8,128)(2,1)S(1)}, u32[]{:S(2)}, u32[]{:S(2)}) %collective-permute-start.18) | collective-permute-done | bytes 196640 | tf_op jit(solution)/shard_map/ppermute | solution.py:266
  55.2 0.2 turn.1
  55.4 5.0 %collective-permute-start.19 = (bf16[256,768]{1,0:T(8,128)(2,1)S(1)}, bf16[256,768]{1,0:T(8,128)(2,1)S(1)}, u32[]{:S(2)}, u32[]{:S(2)}) collective-permute-start(bf16[256,768]{1,0:T(8,128)(2,1)S(1)} %turn.1), channel_id=1, source_target_pairs={{1,8},{3,10},{5,12},{7,14},{8,1},{10,3},{12,5},{14,7},{17,24},{19,... | collective-permute-start | bytes 1179656 | tf_op jit(solution)/shard_map/ppermute | solution.py:269
  60.4 0.6 collective-permute-start.15
  60.9 3.1 %collective-permute-start.16 = (bf16[96,512]{1,0:T(8,128)(2,1)S(1)}, bf16[96,512]{1,0:T(8,128)(2,1)S(1)}, u32[]{:S(2)}, u32[]{:S(2)}) collective-permute-start(bf16[96,512]{1,0:T(8,128)(2,1)S(1)} %get-tuple-element.39), channel_id=1, source_target_pairs={{0,4},{1,5},{2,6},{3,7},{4,0},{5,1},{6,2},{7,3},{8,12},{9,13},{10,... | collective-permute-start | bytes 294920 | tf_op jit(solution)/shard_map/ppermute | solution.py:335
  64.0 1.8 %collective-permute-done.19 = bf16[256,768]{1,0:T(8,128)(2,1)S(1)} collective-permute-done((bf16[256,768]{1,0:T(8,128)(2,1)S(1)}, bf16[256,768]{1,0:T(8,128)(2,1)S(1)}, u32[]{:S(2)}, u32[]{:S(2)}) %collective-permute-start.19) | collective-permute-done | bytes 393248 | tf_op jit(solution)/shard_map/ppermute | solution.py:269
  65.8 0.8 %broadcast_select_fusion = bf16[256,768]{1,0:T(8,128)(2,1)} fusion(bf16[256,768]{1,0:T(8,128)(2,1)S(1)} %turn.1, bf16[256,768]{1,0:T(8,128)(2,1)S(1)} %collective-permute-done.19, pred[]{:T(512)S(6)} %eq.3), kind=kLoop, calls=%fused_computation | loop fusion | flops 196608 | bytes 1179649 | tf_op jit(solution)/shard_map/jit(_where)/select_n | solution.py:348
  66.6 0.0 collective-permute-done.14.other_scaled.rest_6_
  66.6 0.4 pivot_first.1
  67.0 2.5 %collective-permute-done.16.rest_3_ = bf16[96,512]{1,0:T(8,128)(2,1)S(1)} collective-permute-done((bf16[96,512]{1,0:T(8,128)(2,1)S(1)}, bf16[96,512]{1,0:T(8,128)(2,1)S(1)}, u32[]{:S(2)}, u32[]{:S(2)}) %collective-permute-start.16) | collective-permute-done | bytes 98336 | tf_op jit(solution)/shard_map/ppermute | solution.py:335
  69.5 0.0 collective-permute-done.17.rest_4_
  69.5 1.0 %pivot.1 = bf16[96,768]{1,0:T(8,128)(2,1)S(1)} custom-call(f32[96,384]{1,0:T(8,128)S(1)} %get-tuple-element.36.rest_0_, f32[96,384]{1,0:T(8,128)S(1)} %get-tuple-element.37.rest_1_, bf16[96,512]{1,0:T(8,128)(2,1)S(1)} %collective-permute-done.15.rest_2_, bf16[96,512]{1,0:T(8,128)(2,1)S(1)} %collective-permute-done.16.rest_3_, ...), custom_call_target="tpu_custom_call" | custom-call | tf_op jit(solution)/shard_map/pivot/pallas_call | solution.py:358
  70.5 3.9 %collective-permute-start.20 = (bf16[96,768]{1,0:T(8,128)(2,1)S(1)}, bf16[96,768]{1,0:T(8,128)(2,1)S(1)}, u32[]{:S(2)}, u32[]{:S(2)}) collective-permute-start(bf16[96,768]{1,0:T(8,128)(2,1)S(1)} %pivot.1), channel_id=1, source_target_pairs={{1,8},{3,10},{5,12},{7,14},{8,1},{10,3},{12,5},{14,7},{17,24},{19,... | collective-permute-start | bytes 442376 | tf_op jit(solution)/shard_map/ppermute | solution.py:269
  74.4 2.8 %collective-permute-done.20 = bf16[96,768]{1,0:T(8,128)(2,1)S(1)} collective-permute-done((bf16[96,768]{1,0:T(8,128)(2,1)S(1)}, bf16[96,768]{1,0:T(8,128)(2,1)S(1)}, u32[]{:S(2)}, u32[]{:S(2)}) %collective-permute-start.20) | collective-permute-done | bytes 147488 | tf_op jit(solution)/shard_map/ppermute | solution.py:269
  77.2 0.8 add_bitcast_fusion
  (17 shorter events, 0.1 us)
Async XLA Ops:
  0.6 12.6 %copy-start = (bf16[1024,512]{1,0:T(8,128)(2,1)S(1)}, bf16[1024,512]{1,0:T(8,128)(2,1)}, u32[]{:S(2)}) copy-start(bf16[1024,512]{1,0:T(8,128)(2,1)} %anc.1) | copy-start | bytes 3145732
  0.6 12.6 %copy-start.2 = (s32[4,16]{1,0:T(4,128)S(1)}, s32[4,16]{1,0:T(4,128)}, u32[]{:S(2)}) copy-start(s32[4,16]{1,0:T(4,128)} %lists_in.1) | copy-start | bytes 772
  0.7 12.6 %copy-start.3 = (s32[32]{0:T(128)S(1)}, s32[32]{0:T(128)}, u32[]{:S(2)}) copy-start(s32[32]{0:T(128)} %row_home_in.1) | copy-start | bytes 388
  0.7 12.6 %collective-permute-start = (bf16[1024,512]{1,0:T(8,128)(2,1)}, bf16[1024,512]{1,0:T(8,128)(2,1)S(1)}, u32[]{:S(2)}, u32[]{:S(2)}) collective-permute-start(bf16[1024,512]{1,0:T(8,128)(2,1)} %anc.1), channel_id=1, source_target_pairs={{0,8},{8,0},{16,24},{24,16},{1,9},{9,1},{17,25},{25,17},{2,10},{10... | collective-permute-start | bytes 3145736 | tf_op jit(solution)/shard_map/ppermute | solution.py:266
  3.7 16.6 %copy-start.5 = (bf16[384,256]{1,0:T(8,128)(2,1)S(1)}, bf16[384,256]{1,0:T(8,128)(2,1)}, u32[]{:S(2)}) copy-start(bf16[384,256]{1,0:T(8,128)(2,1)} %get-tuple-element.27) | copy-start | bytes 589828
  3.7 3.7 %collective-permute-start.1 = (bf16[384,256]{1,0:T(8,128)(2,1)}, bf16[384,256]{1,0:T(8,128)(2,1)S(1)}, u32[]{:S(2)}, u32[]{:S(2)}) collective-permute-start(bf16[384,256]{1,0:T(8,128)(2,1)} %get-tuple-element.29), channel_id=1, source_target_pairs={{0,8},{2,10},{4,12},{6,14},{9,1},{11,3},{13,5},{15,7},{16,24},{18,... | collective-permute-start | bytes 589832 | tf_op jit(solution)/shard_map/ppermute | solution.py:269
  7.3 21.2 %copy-start.4 = (bf16[1,768,768]{2,1,0:T(8,128)(2,1)S(1)}, bf16[1,768,768]{2,1,0:T(8,128)(2,1)}, u32[]{:S(2)}) copy-start(bf16[1,768,768]{2,1,0:T(8,128)(2,1)} %param.11) | copy-start | bytes 3538948
  7.3 14.3 %collective-permute-start.6 = (bf16[384,256]{1,0:T(8,128)(2,1)}, bf16[384,256]{1,0:T(8,128)(2,1)S(1)}, u32[]{:S(2)}, u32[]{:S(2)}) collective-permute-start(bf16[384,256]{1,0:T(8,128)(2,1)} %get-tuple-element.29), channel_id=1, source_target_pairs={{1,8},{3,10},{5,12},{7,14},{8,1},{10,3},{12,5},{14,7},{17,24},{19,... | collective-permute-start | bytes 589832 | tf_op jit(solution)/shard_map/ppermute | solution.py:269
  11.9 9.7 %collective-permute-start.5 = (bf16[384,256]{1,0:T(8,128)(2,1)}, bf16[384,256]{1,0:T(8,128)(2,1)S(1)}, u32[]{:S(2)}, u32[]{:S(2)}) collective-permute-start(bf16[384,256]{1,0:T(8,128)(2,1)} %get-tuple-element.27), channel_id=1, source_target_pairs={{1,0},{3,2},{5,4},{7,6},{8,9},{10,11},{12,13},{14,15},{17,16},{19,... | collective-permute-start | bytes 589832 | tf_op jit(solution)/shard_map/ppermute | solution.py:269
  15.5 17.3 %collective-permute-start.10 = (bf16[1024,256]{1,0:T(8,128)(2,1)S(1)}, bf16[1024,256]{1,0:T(8,128)(2,1)S(1)}, u32[]{:S(2)}, u32[]{:S(2)}) collective-permute-start(bf16[1024,256]{1,0:T(8,128)(2,1)S(1)} %get-tuple-element.30), channel_id=1, source_target_pairs={{0,0},{1,8},{2,2},{3,10},{4,4},{5,12},{6,6},{7,14},{8,1},{9,9},{10... | collective-permute-start | bytes 1572872 | tf_op jit(solution)/shard_map/ppermute | solution.py:269
  17.5 15.4 %collective-permute-start.11 = (bf16[1024,256]{1,0:T(8,128)(2,1)S(1)}, bf16[1024,256]{1,0:T(8,128)(2,1)S(1)}, u32[]{:S(2)}, u32[]{:S(2)}) collective-permute-start(bf16[1024,256]{1,0:T(8,128)(2,1)S(1)} %get-tuple-element.31), channel_id=1, source_target_pairs={{0,16},{1,24},{2,18},{3,26},{4,20},{5,28},{6,22},{7,30},{8,17},{9,... | collective-permute-start | bytes 1572872 | tf_op jit(solution)/shard_map/ppermute | solution.py:269
  20.3 28.6 %copy-start.1 = (s32[4]{0:T(128)S(1)}, s32[4]{0:T(128)}, u32[]{:S(2)}) copy-start(s32[4]{0:T(128)} %front_blocks.1) | copy-start | bytes 52
  20.3 7.1 %collective-permute-start.2 = (bf16[384,256]{1,0:T(8,128)(2,1)S(1)}, bf16[384,256]{1,0:T(8,128)(2,1)S(1)}, u32[]{:S(2)}, u32[]{:S(2)}) collective-permute-start(bf16[384,256]{1,0:T(8,128)(2,1)S(1)} %broadcast_select_fusion.2.rest_0_), channel_id=1, source_target_pairs={{0,2},{1,3},{2,6},{3,7},{6,4},{7,5},{4,0},{5,1},{8,10},{9,11},{10,... | collective-permute-start | bytes 589832 | tf_op jit(solution)/shard_map/ppermute | solution.py:317
  21.7 11.8 %collective-permute-start.7 = (bf16[384,256]{1,0:T(8,128)(2,1)S(1)}, bf16[384,256]{1,0:T(8,128)(2,1)S(1)}, u32[]{:S(2)}, u32[]{:S(2)}) collective-permute-start(bf16[384,256]{1,0:T(8,128)(2,1)S(1)} %broadcast_select_fusion.1.rest_4_), channel_id=1, source_target_pairs={{0,2},{1,3},{2,6},{3,7},{6,4},{7,5},{4,0},{5,1},{8,10},{9,11},{10,... | collective-permute-start | bytes 589832 | tf_op jit(solution)/shard_map/ppermute | solution.py:318
  27.4 5.5 %collective-permute-start.3 = (bf16[384,256]{1,0:T(8,128)(2,1)S(1)}, bf16[384,256]{1,0:T(8,128)(2,1)S(1)}, u32[]{:S(2)}, u32[]{:S(2)}) collective-permute-start(bf16[384,256]{1,0:T(8,128)(2,1)S(1)} %collective-permute-done.2.rest_1_), channel_id=1, source_target_pairs={{0,2},{1,3},{2,6},{3,7},{6,4},{7,5},{4,0},{5,1},{8,10},{9,11},{10,... | collective-permute-start | bytes 589832 | tf_op jit(solution)/shard_map/ppermute | solution.py:317
  32.9 16.0 %collective-permute-start.12 = (bf16[1024,256]{1,0:T(8,128)(2,1)S(1)}, bf16[1024,256]{1,0:T(8,128)(2,1)S(1)}, u32[]{:S(2)}, u32[]{:S(2)}) collective-permute-start(bf16[1024,256]{1,0:T(8,128)(2,1)S(1)} %collective-permute-done.10.rest_8_), channel_id=1, source_target_pairs={{0,8},{8,0},{16,24},{24,16},{1,9},{9,1},{17,25},{25,17},{2,10},{10... | collective-permute-start | bytes 1572872 | tf_op jit(solution)/shard_map/ppermute | solution.py:266
  32.9 16.0 %collective-permute-start.13 = (bf16[1024,256]{1,0:T(8,128)(2,1)S(1)}, bf16[1024,256]{1,0:T(8,128)(2,1)S(1)}, u32[]{:S(2)}, u32[]{:S(2)}) collective-permute-start(bf16[1024,256]{1,0:T(8,128)(2,1)S(1)} %collective-permute-done.11.rest_9_), channel_id=1, source_target_pairs={{0,8},{8,0},{16,24},{24,16},{1,9},{9,1},{17,25},{25,17},{2,10},{10... | collective-permute-start | bytes 1572872 | tf_op jit(solution)/shard_map/ppermute | solution.py:266
  33.4 7.4 %collective-permute-start.8 = (bf16[384,256]{1,0:T(8,128)(2,1)S(1)}, bf16[384,256]{1,0:T(8,128)(2,1)S(1)}, u32[]{:S(2)}, u32[]{:S(2)}) collective-permute-start(bf16[384,256]{1,0:T(8,128)(2,1)S(1)} %collective-permute-done.7.rest_5_), channel_id=1, source_target_pairs={{0,2},{1,3},{2,6},{3,7},{6,4},{7,5},{4,0},{5,1},{8,10},{9,11},{10,... | collective-permute-start | bytes 589832 | tf_op jit(solution)/shard_map/ppermute | solution.py:318
  34.8 10.2 %collective-permute-start.4 = (bf16[384,256]{1,0:T(8,128)(2,1)S(1)}, bf16[384,256]{1,0:T(8,128)(2,1)S(1)}, u32[]{:S(2)}, u32[]{:S(2)}) collective-permute-start(bf16[384,256]{1,0:T(8,128)(2,1)S(1)} %collective-permute-done.3.rest_2_), channel_id=1, source_target_pairs={{0,2},{1,3},{2,6},{3,7},{6,4},{7,5},{4,0},{5,1},{8,10},{9,11},{10,... | collective-permute-start | bytes 589832 | tf_op jit(solution)/shard_map/ppermute | solution.py:317
  40.8 8.1 %collective-permute-start.9 = (bf16[384,256]{1,0:T(8,128)(2,1)S(1)}, bf16[384,256]{1,0:T(8,128)(2,1)S(1)}, u32[]{:S(2)}, u32[]{:S(2)}) collective-permute-start(bf16[384,256]{1,0:T(8,128)(2,1)S(1)} %collective-permute-done.8.rest_6_), channel_id=1, source_target_pairs={{0,2},{1,3},{2,6},{3,7},{6,4},{7,5},{4,0},{5,1},{8,10},{9,11},{10,... | collective-permute-start | bytes 589832 | tf_op jit(solution)/shard_map/ppermute | solution.py:318
  50.6 16.0 %collective-permute-start.14 = (bf16[8,384,256]{2,1,0:T(8,128)(2,1)S(1)}, bf16[8,384,256]{2,1,0:T(8,128)(2,1)S(1)}, u32[]{:S(2)}, u32[]{:S(2)}) collective-permute-start(bf16[8,384,256]{2,1,0:T(8,128)(2,1)S(1)} %get-tuple-element.35.own_scaled.rest_5_), channel_id=1, source_target_pairs={{0,8},{8,0},{16,24},{24,16},{1,9},{9,1},{17,25},{25,17},{2,10},{10... | collective-permute-start | bytes 4718600 | tf_op jit(solution)/shard_map/ppermute | solution.py:266
  51.8 3.3 %collective-permute-start.18 = (bf16[384,256]{1,0:T(8,128)(2,1)S(1)}, bf16[384,256]{1,0:T(8,128)(2,1)S(1)}, u32[]{:S(2)}, u32[]{:S(2)}) collective-permute-start(bf16[384,256]{1,0:T(8,128)(2,1)S(1)} %get-tuple-element.42), channel_id=1, source_target_pairs={{0,8},{8,0},{16,24},{24,16},{1,9},{9,1},{17,25},{25,17},{2,10},{10... | collective-permute-start | bytes 589832 | tf_op jit(solution)/shard_map/ppermute | solution.py:266
  55.4 10.4 %collective-permute-start.19 = (bf16[256,768]{1,0:T(8,128)(2,1)S(1)}, bf16[256,768]{1,0:T(8,128)(2,1)S(1)}, u32[]{:S(2)}, u32[]{:S(2)}) collective-permute-start(bf16[256,768]{1,0:T(8,128)(2,1)S(1)} %turn.1), channel_id=1, source_target_pairs={{1,8},{3,10},{5,12},{7,14},{8,1},{10,3},{12,5},{14,7},{17,24},{19,... | collective-permute-start | bytes 1179656 | tf_op jit(solution)/shard_map/ppermute | solution.py:269
  60.4 6.6 %collective-permute-start.15 = (bf16[96,512]{1,0:T(8,128)(2,1)S(1)}, bf16[96,512]{1,0:T(8,128)(2,1)S(1)}, u32[]{:S(2)}, u32[]{:S(2)}) collective-permute-start(bf16[96,512]{1,0:T(8,128)(2,1)S(1)} %get-tuple-element.38), channel_id=1, source_target_pairs={{0,2},{1,3},{2,0},{3,1},{4,6},{5,7},{6,4},{7,5},{8,10},{9,11},{10,... | collective-permute-start | bytes 294920 | tf_op jit(solution)/shard_map/ppermute | solution.py:335
  60.9 8.6 %collective-permute-start.16 = (bf16[96,512]{1,0:T(8,128)(2,1)S(1)}, bf16[96,512]{1,0:T(8,128)(2,1)S(1)}, u32[]{:S(2)}, u32[]{:S(2)}) collective-permute-start(bf16[96,512]{1,0:T(8,128)(2,1)S(1)} %get-tuple-element.39), channel_id=1, source_target_pairs={{0,4},{1,5},{2,6},{3,7},{4,0},{5,1},{6,2},{7,3},{8,12},{9,13},{10,... | collective-permute-start | bytes 294920 | tf_op jit(solution)/shard_map/ppermute | solution.py:335
  64.0 5.5 %collective-permute-start.17 = (bf16[96,512]{1,0:T(8,128)(2,1)S(1)}, bf16[96,512]{1,0:T(8,128)(2,1)S(1)}, u32[]{:S(2)}, u32[]{:S(2)}) collective-permute-start(bf16[96,512]{1,0:T(8,128)(2,1)S(1)} %get-tuple-element.40), channel_id=1, source_target_pairs={{0,6},{1,7},{2,4},{3,5},{4,2},{5,3},{6,0},{7,1},{8,14},{9,15},{10,... | collective-permute-start | bytes 294920 | tf_op jit(solution)/shard_map/ppermute | solution.py:335
  70.5 6.7 %collective-permute-start.20 = (bf16[96,768]{1,0:T(8,128)(2,1)S(1)}, bf16[96,768]{1,0:T(8,128)(2,1)S(1)}, u32[]{:S(2)}, u32[]{:S(2)}) collective-permute-start(bf16[96,768]{1,0:T(8,128)(2,1)S(1)} %pivot.1), channel_id=1, source_target_pairs={{1,8},{3,10},{5,12},{7,14},{8,1},{10,3},{12,5},{14,7},{17,24},{19,... | collective-permute-start | bytes 442376 | tf_op jit(solution)/shard_map/ppermute | solution.py:269

commit v3 on v2

--- a/solution.py
+++ b/solution.py
@@ -8,6 +8,8 @@
 from jax.sharding import PartitionSpec as P
 
 BLK = 128
+PLACE = 1_000_000_000
+STACK = 12_000_000_000
 F32 = jnp.float32
 BF16 = jnp.bfloat16
 
@@ -53,51 +55,23 @@
 
 def pack_kernel(groups, pan, row_home_in, lists_in, anc, other_anc, *rest):
     pairs = groups // 2
-    outs, members = rest[:pairs], rest[pairs]
-    row_home, lists, sems = rest[pairs + 1 :]
-    h, c, q, l = coordinates()
-    p = 2 * q + l
+    outs, slots = rest[:pairs], rest[pairs]
+    row_home, lists, place, sems = rest[pairs + 1 :]
     loads = [
-        pltpu.make_async_copy(row_home_in, row_home, sems.at[pairs]),
-        pltpu.make_async_copy(lists_in, lists, sems.at[pairs + 1]),
+        pltpu.make_async_copy(row_home_in, row_home, sems.at[0]),
+        pltpu.make_async_copy(lists_in, lists, sems.at[1]),
     ]
     for load in loads:
         load.start()
     for load in loads:
         load.wait()
+    h, c, q, l = coordinates()
+    p = 2 * q + l
     stored = anc.shape[0] // BLK
     window_blocks = anc.shape[1] // BLK
     picked = lists.shape[1] // pan
     windows = pan // groups
-    depth = picked * BLK
-
-    def window(w, ranks):
-        owner = row_home[window_blocks * w] // stored
-        counts = []
-        for core, rank in enumerate(ranks):
-            mine = owner == 2 * h + core
-            counts.append(rank + mine.astype(jnp.int32))
-            for local in range(2):
-
-                @pl.when(mine & ((c == core) == (local == 0)))
-                def _():
-                    origin = (anc, other_anc)[local]
-                    for k in range(pairs):
-                        front = 2 * peer(h, k, pairs) + c
-                        for r in range(picked):
-                            row = row_home[lists[front, picked * w + r]] - stored * owner
-                            at = ((core * windows + rank) * picked + r) * BLK
-                            for s in range(picked):
-                                column = lists[front, picked * p + s] - window_blocks * p
-                                pltpu.make_async_copy(
-                                    origin.at[pl.ds(row * BLK, BLK), pl.ds(column * BLK, BLK)],
-                                    outs[k].at[pl.ds(at, BLK), pl.ds(s * BLK, BLK)],
-                                    sems.at[k],
-                                ).start()
-
-        return tuple(counts)
-
-    lax.fori_loop(0, pan, window, (jnp.int32(0), jnp.int32(0)))
+
     owners = [row_home[window_blocks * w] // stored for w in range(pan)]
     for w in range(pan):
         rank = jnp.int32(0)
@@ -105,12 +79,25 @@
             rank = rank + (owners[v] == owners[w]).astype(jnp.int32)
         step = owners[w] >> 1
         step = step ^ h if power_of_two(pairs) else (h + pairs - step) % pairs
-        members[(2 * step + (owners[w] & 1)) * windows + rank] = jnp.int32(w)
-    rows, columns = outs[0].shape
+        slots[w] = (2 * step + (owners[w] & 1)) * windows + rank
+
+        @pl.when(owners[w] >> 1 == h)
+        def _():
+            place[(owners[w] & 1) * windows + rank] = jnp.int32(w)
+
     for k in range(pairs):
-        pltpu.make_async_copy(
-            anc.at[pl.ds(0, rows), pl.ds(0, columns)], outs[k], sems.at[k]
-        ).wait()
+        front = 2 * peer(h, k, pairs) + c
+        columns = [lists[front, picked * p + s] - window_blocks * p for s in range(picked)]
+        for core in range(2):
+            for rank in range(windows):
+                w = place[core * windows + rank]
+                for r in range(picked):
+                    row = row_home[lists[front, picked * w + r]] - stored * (2 * h + core)
+                    rows = pl.ds(pl.multiple_of(row * BLK, BLK), BLK)
+                    for s in range(picked):
+                        at = pl.ds(pl.multiple_of(columns[s] * BLK, BLK), BLK)
+                        to = pl.ds(((core * windows + rank) * picked + r) * BLK, BLK)
+                        outs[k][to, pl.ds(s * BLK, BLK)] = jnp.where(c == core, anc[rows, at], other_anc[rows, at])
 
 
 def scale_kernel(
@@ -144,31 +131,35 @@
         give[at] = turned[pl.ds(share * (2 * place + 1 - c), share)].astype(BF16)
 
 
-def cross_kernel(n, groups, front_blocks, members, *rest):
-    near, far = rest[:n], rest[n : 2 * n]
-    rest = rest[2 * n :]
-    pairs = groups // 2
-    own_sigma, other_sigma = rest[:pairs], rest[pairs : 2 * pairs]
-    rest = rest[2 * pairs :]
-    mine, give, whole = rest[:3]
-    parts, total = rest[3 : n + 3], rest[n + 3]
+def stack_kernel(pairs, *refs):
+    own_in, other_in, (own, other) = refs[:pairs], refs[pairs : 2 * pairs], refs[2 * pairs :]
+    depth = own.shape[1]
+    windows = own_in[0].shape[0] // depth
+    for slot in range(own.shape[0]):
+        at = pl.ds(slot % windows * depth, depth)
+        own[slot] = own_in[slot // windows][at]
+        other[slot] = other_in[slot // windows][at]
+
+
+def place_kernel(n, k, side, chunk, _, whole, sem):
+    _, _, q, l = coordinates()
+    origin = ring_place((ring_position(q, n) + n - k) % n, n)
+    copy = pltpu.make_async_copy(chunk, whole.at[2 * origin + (l ^ side)], sem)
+    copy.start()
+    copy.wait()
+
+
+def cross_kernel(n, front_blocks, slots, whole, own_sigma, other_sigma, mine, give, *rest):
+    parts, total = rest[:n], rest[n]
     h, c, q, l = coordinates()
-    half, rows = near[0].shape
+    half, rows = mine.shape
     padded = half // n
-    position = ring_position(q, n)
-    for step in range(n):
-        origin = ring_place((position + n - step) % n, n)
-        whole[2 * origin + l] = near[step][...]
-        whole[2 * origin + (1 - l)] = far[step][...]
     own = jnp.zeros((half, rows), F32)
     other = jnp.zeros((half, rows), F32)
-    windows = 2 * n // pairs
-    depth = own_sigma[0].shape[0] // windows
-    for slot in range(2 * n):
-        chunk = whole[members[slot]]
-        at = pl.ds(slot % windows * depth, depth)
-        own = own + jnp.dot(chunk, own_sigma[slot // windows][at], preferred_element_type=F32)
-        other = other + jnp.dot(chunk, other_sigma[slot // windows][at], preferred_element_type=F32)
+    for member in range(2 * n):
+        slot = slots[member]
+        own = own + jnp.dot(whole[member], own_sigma[slot], preferred_element_type=F32)
+        other = other + jnp.dot(whole[member], other_sigma[slot], preferred_element_type=F32)
     live = front_blocks[2 * h + l]
     block = lax.broadcasted_iota(jnp.int32, (half, rows), 1) // BLK
     own = jnp.where((2 * q + c) * (rows // BLK) + block < live, -own, 0.0)
@@ -221,15 +212,15 @@
     out[...] = (-jnp.concatenate(pieces, axis=1)).astype(BF16)
 
 
-def turn_kernel(pan, share, mine, other, out, natural):
-    _, c, _, _ = coordinates()
+def turn_kernel(pan, share, own_rows, other_rows, out, natural):
+    _, _, _, l = coordinates()
     n = pan // 2
-    padded = mine.shape[0] // n
+    padded = own_rows.shape[0] // n
     for place in range(n):
         at = pl.ds(place * padded, share)
-        natural[pl.ds(share * (2 * place + c), share)] = mine[at].astype(F32)
-        natural[pl.ds(share * (2 * place + 1 - c), share)] = other[at].astype(F32)
-    out[...] = natural[...].T.astype(BF16)
+        natural[pl.ds(share * (2 * place + l), share)] = own_rows[at].astype(F32)
+        natural[pl.ds(share * (2 * place + 1 - l), share)] = other_rows[at].astype(F32)
+    out[0] = natural[...].T.astype(BF16)
 
 
 def per_device(anc_rows, row_home, block_lists, front_blocks, panel, pivot_inverse):
@@ -262,11 +253,17 @@
         for l in range(2)
     ]
 
-    def swap(x):
-        return lax.ppermute(x, "grp", cores)
-
-    def everywhere(x, pairs_of):
-        return lax.ppermute(x, ("grp", "pan"), pairs_of)
+    def swap(x, name):
+        with jax.named_scope(name):
+            return lax.ppermute(x, "grp", cores)
+
+    def everywhere(x, pairs_of, name):
+        with jax.named_scope(name):
+            return lax.ppermute(x, ("grp", "pan"), pairs_of)
+
+    def along(x, pairs_of, name):
+        with jax.named_scope(name):
+            return lax.ppermute(x, "pan", pairs_of)
 
     keep, give = pl.pallas_call(
         functools.partial(scale_kernel, pan),
@@ -283,30 +280,28 @@
         compiler_params=params(60),
         name="scale",
     )(front_blocks, panel[0], inverse)
-    given = everywhere(give, to_sibling)
-    keep, give, given = lax.optimization_barrier((keep, give, given))
+    given = everywhere(give, to_sibling, "near_half")
     near = jnp.where(diagonal, keep, given)
-    far = jnp.where(diagonal, everywhere(keep, to_diagonal), everywhere(give, crossing))
-
-    *packed, members = pl.pallas_call(
+    far = jnp.where(
+        diagonal,
+        everywhere(keep, to_diagonal, "far_half"),
+        everywhere(give, crossing, "far_half_off"),
+    )
+
+    *packed, slots = pl.pallas_call(
         functools.partial(pack_kernel, groups, pan),
         out_shape=[shape((2 * wanted, rows), BF16)] * pairs + [shape((pan,), jnp.int32)],
-        in_specs=[HBM] * 4,
-        out_specs=[HBM] * pairs + [SMEM],
+        in_specs=[HBM, HBM, VMEM, VMEM],
+        out_specs=[VMEM] * pairs + [SMEM],
         scratch_shapes=[
             pltpu.SMEM(row_home.shape, jnp.int32),
             pltpu.SMEM(block_lists.shape, jnp.int32),
-            pltpu.SemaphoreType.DMA((pairs + 2,)),
+            pltpu.SMEM((pan,), jnp.int32),
+            pltpu.SemaphoreType.DMA((2,)),
         ],
         compiler_params=params(),
         name="pack",
-    )(row_home, block_lists, anc_rows, swap(anc_rows))
-    arrived = [
-        everywhere(
-            packed[k], [(at(h, c, q, l), at(peer(h, k, pairs), l, q, c)) for h, c, q, l in places]
-        )
-        for k in range(pairs)
-    ]
+    )(row_home, block_lists, anc_rows, swap(anc_rows, "rows_of_sibling"))
     own_columns = lax.dynamic_slice_in_dim(inverse, lax.axis_index("pan") * share, share, 1)
     triangle = lax.dot_general(
         own_columns, inverse, (((0,), (0,)), ((), ())), preferred_element_type=F32
@@ -314,39 +309,65 @@
 
     nears, fars = [near], [far]
     for step in range(1, n):
-        nears.append(lax.ppermute(nears[-1], "pan", ring))
-        fars.append(lax.ppermute(fars[-1], "pan", ring))
-
-    arrived, triangle, _ = lax.optimization_barrier((arrived, triangle, nears[min(2, n - 1)]))
-    swapped = [swap(piece) for piece in arrived]
-    mine, give, whole, *parts = pl.pallas_call(
-        functools.partial(cross_kernel, n, groups),
+        nears.append(along(nears[-1], ring, f"near_{step}"))
+        fars.append(along(fars[-1], ring, f"far_{step}"))
+
+    whole = jnp.zeros((pan, half, rows), BF16)
+    anywhere = pl.BlockSpec(memory_space=pl.ANY)
+    for k in range(n):
+        for side, chunks in enumerate((nears, fars)):
+            whole = pl.pallas_call(
+                functools.partial(place_kernel, n, k, side),
+                out_shape=shape((pan, half, rows), BF16),
+                in_specs=[anywhere, anywhere],
+                out_specs=anywhere,
+                scratch_shapes=[pltpu.SemaphoreType.DMA(())],
+                input_output_aliases={1: 0},
+                cost_estimate=pl.CostEstimate(flops=PLACE, bytes_accessed=0, transcendentals=0),
+                compiler_params=params(),
+                name="place",
+            )(chunks[k], whole)
+    arrived = [
+        everywhere(
+            packed[k],
+            [(at(h, c, q, l), at(peer(h, k, pairs), l, q, c)) for h, c, q, l in places],
+            f"sigma_{k}",
+        )
+        for k in range(pairs)
+    ]
+    swapped = [swap(piece, f"share_{k}") for k, piece in enumerate(arrived)]
+    triangle, _ = lax.optimization_barrier((triangle, nears[-2]))
+    own_sigma, other_sigma = pl.pallas_call(
+        functools.partial(stack_kernel, pairs),
+        out_shape=[shape((pan, wanted // windows, rows), BF16)] * 2,
+        in_specs=[VMEM] * groups,
+        out_specs=[VMEM] * 2,
+        compiler_params=params(),
+        cost_estimate=pl.CostEstimate(flops=STACK, bytes_accessed=0, transcendentals=0),
+        name="stack",
+    )(*arrived, *swapped)
+    mine, give, *parts = pl.pallas_call(
+        functools.partial(cross_kernel, n),
         out_shape=[shape((half, rows), BF16)] * 2
-        + [shape((pan, half, rows), BF16)]
         + [shape((padded, 2 * rows), BF16)] * n,
-        in_specs=[SMEM] * 2 + [VMEM] * (2 * n + groups),
-        out_specs=[VMEM] * (n + 3),
+        in_specs=[SMEM] * 2 + [VMEM] * 3,
+        out_specs=[VMEM] * (n + 2),
         scratch_shapes=[pltpu.VMEM((2, half, rows), F32)],
         compiler_params=params(),
         name="cross",
-    )(front_blocks, members, *nears, *fars, *arrived, *swapped)
+    )(front_blocks, slots, whole, own_sigma, other_sigma)
 
     for k in range(1, n):
-        parts[k] = lax.ppermute(
-            parts[k], "pan", [(2 * q + l, 2 * peer(q, k, n) + l) for q in range(n) for l in range(2)]
+        parts[k] = along(
+            parts[k],
+            [(2 * q + l, 2 * peer(q, k, n) + l) for q in range(n) for l in range(2)],
+            f"columns_{k}",
         )
-    other_whole = swap(whole)
-    turned = pl.pallas_call(
-        functools.partial(turn_kernel, pan, share),
-        out_shape=shape((rows, width), BF16),
-        in_specs=[VMEM, VMEM],
-        out_specs=VMEM,
-        scratch_shapes=[pltpu.VMEM((width, rows), F32)],
-        compiler_params=params(),
-        name="turn",
-    )(mine, swap(give))
-    cross = jnp.where(diagonal, turned, everywhere(turned, crossing))
-
+    other_whole = swap(whole, "scaled_of_sibling")
+    own_rows = everywhere(mine, exchange, "rows_out")
+    other_rows = everywhere(
+        give, [(at(h, c, q, l), at(h, l, q, 1 - c)) for h, c, q, l in places], "rows_out_other"
+    )
     firsts = pl.pallas_call(
         functools.partial(pivot_first_kernel, n),
         out_shape=[shape((padded, half), F32)] * 2,
@@ -363,10 +384,18 @@
         compiler_params=params(),
         name="pivot",
     )(*firsts, *parts[1:], whole, other_whole)
-    term, cross = lax.optimization_barrier((term, cross))
-    term = jnp.where(diagonal, term, everywhere(term, crossing))
+    term = everywhere(term, exchange, "term_out")
+    cross = pl.pallas_call(
+        functools.partial(turn_kernel, pan, share),
+        out_shape=shape((1, rows, width), BF16),
+        in_specs=[VMEM, VMEM],
+        out_specs=VMEM,
+        scratch_shapes=[pltpu.VMEM((width, rows), F32)],
+        compiler_params=params(),
+        name="turn",
+    )(own_rows, other_rows)
     pivot = triangle + term[:share].astype(F32)
-    return cross[None], pivot[None]
+    return cross, pivot[None]
 
 
 def solution(mesh):

time: 78.2 us -> 65.9 us (0.84)
  waiting for transfers between devices: 30 us -> 18.3 us
  starting transfers between devices: 36.6 us -> 32.1 us
  Pallas kernels: 8.4 us -> 11.3 us
  local copies, waits for them, and re-layouts: 0.03 us -> 1.51 us
  other arithmetic: 1.6 us -> 0.8 us
    ppermute x9, waiting for transfers between devices: 20 us -> 12.9 us  [along(): return lax.ppermute(x, 'pan', pairs_of)]
    ppermute x5 -> x4, waiting for transfers between devices: 3.25 us -> 0.01 us  [swap(): return lax.ppermute(x, 'grp', cores)]
    pallas_call x1 -> x10, Pallas kernels: 1.7 us -> 4.47 us  [the longest x1 2.31 us: per_device(): pl.pallas_call(functools.partial(cross_kernel, n), out_shape=[shape((half...]
    ppermute x7 -> x8, starting transfers between devices: 20.8 us -> 18.5 us  [everywhere(): return lax.ppermute(x, ('grp', 'pan'), pairs_of)]
    ppermute x7 -> x8, waiting for transfers between devices: 6.83 us -> 5.33 us  [everywhere(): return lax.ppermute(x, ('grp', 'pan'), pairs_of)]
    unnamed x12 -> x14, local copies, waits for them, and re-layouts: 0.03 us -> 1.41 us
    ppermute x5 -> x4, starting transfers between devices: 1.95 us -> 0.66 us  [swap(): return lax.ppermute(x, 'grp', cores)]
    ppermute x9, starting transfers between devices: 13.9 us -> 12.9 us  [along(): return lax.ppermute(x, 'pan', pairs_of)]
  transfers between devices with their start and end apart: 21 -> 21, of which waited for: 10 -> 7; matrix products, arithmetic and copies ran while one was open for 2% -> 1% of each run, Pallas kernels for 7% -> 17%
where the time goes in v3:
time: 65.9 us; the launch traced here: 65.4 us
  starting transfers between devices  32.1 us (49%)
  waiting for transfers between devices  18.3 us (28%)
  Pallas kernels  11.3 us (17%)
  local copies, waits for them, and re-layouts  1.51 us (2%)
  between operations  0.94 us (1%)
  other arithmetic  0.8 us (1%)
    ppermute x8, starting transfers between devices, everywhere(): return lax.ppermute(x, ('grp', 'pan'), pairs_of)  18.5 us
    ppermute x9, waiting for transfers between devices, along(): return lax.ppermute(x, 'pan', pairs_of)  12.9 us
    ppermute x9, starting transfers between devices, along(): return lax.ppermute(x, 'pan', pairs_of)  12.9 us
    ppermute x8, waiting for transfers between devices, everywhere(): return lax.ppermute(x, ('grp', 'pan'), pairs_of)  5.33 us
    pallas_call x1, Pallas kernels, per_device(): pl.pallas_call(functools.partial(scale_kernel, pan), out_shape=[shape((ha...  2.86 us
    pallas_call x1, Pallas kernels, per_device(): pl.pallas_call(functools.partial(cross_kernel, n), out_shape=[shape((half...  2.31 us
    pallas_call x8, Pallas kernels, per_device(): pl.pallas_call(functools.partial(place_kernel, n, k, side), out_shape=sha...  2.03 us
    pallas_call x1, Pallas kernels, per_device(): pl.pallas_call(functools.partial(pack_kernel, groups, pan), out_shape=[sh...  1.63 us
  transfers between devices with their start and end apart: 21, of which 7 were waited for; matrix products, arithmetic and copies ran while one was open for 1% of the time, Pallas kernels for 17%

profile of v3, /device:TPU:1, one launch (start us, length us, event | category | flops | bytes accessed | tf_op | source)
XLA Modules:
  0.0 65.4 jit_solution(10119025466396857795)
XLA Ops:
  0.7 0.1 collective-permute-start
  0.8 2.9 %scale.1 = (bf16[384,256]{1,0:T(8,128)(2,1)}, bf16[384,256]{1,0:T(8,128)(2,1)}) custom-call(s32[4]{0:T(128)} %front_blocks.1, bf16[256,768]{1,0:T(8,128)(2,1)} %bitcast.10, bf16[768,768]{1,0:T(8,128)(2,1)} %bitcast.9), custom_call_target="tpu_custom_call" | custom-call | tf_op jit(solution)/shard_map/scale/pallas_call | solution.py:268
  3.7 1.3 %collective-permute-start.6 = (bf16[384,256]{1,0:T(8,128)(2,1)}, bf16[384,256]{1,0:T(8,128)(2,1)S(1)}, u32[]{:S(2)}, u32[]{:S(2)}) collective-permute-start(bf16[384,256]{1,0:T(8,128)(2,1)} %get-tuple-element.20), channel_id=1, source_target_pairs={{0,8},{2,10},{4,12},{6,14},{9,1},{11,3},{13,5},{15,7},{16,24},{18,... | collective-permute-start | bytes 589832 | tf_op jit(solution)/shard_map/near_half/ppermute | solution.py:262
  5.0 4.5 %collective-permute-start.2 = (bf16[384,256]{1,0:T(8,128)(2,1)}, bf16[384,256]{1,0:T(8,128)(2,1)S(1)}, u32[]{:S(2)}, u32[]{:S(2)}) collective-permute-start(bf16[384,256]{1,0:T(8,128)(2,1)} %get-tuple-element.20), channel_id=1, source_target_pairs={{1,8},{3,10},{5,12},{7,14},{8,1},{10,3},{12,5},{14,7},{17,24},{19,... | collective-permute-start | bytes 589832 | tf_op jit(solution)/shard_map/far_half_off/ppermute | solution.py:262
  9.4 1.4 %collective-permute-start.1 = (bf16[384,256]{1,0:T(8,128)(2,1)}, bf16[384,256]{1,0:T(8,128)(2,1)S(1)}, u32[]{:S(2)}, u32[]{:S(2)}) collective-permute-start(bf16[384,256]{1,0:T(8,128)(2,1)} %get-tuple-element.19), channel_id=1, source_target_pairs={{1,0},{3,2},{5,4},{7,6},{8,9},{10,11},{12,13},{14,15},{17,16},{19,... | collective-permute-start | bytes 589832 | tf_op jit(solution)/shard_map/far_half/ppermute | solution.py:262
  10.9 1.4 %collective-permute-start.7 = (bf16[384,256]{1,0:T(8,128)(2,1)S(1)}, bf16[384,256]{1,0:T(8,128)(2,1)S(1)}, u32[]{:S(2)}, u32[]{:S(2)}) collective-permute-start(bf16[384,256]{1,0:T(8,128)(2,1)S(1)} %broadcast_select_fusion.chunk), channel_id=1, source_target_pairs={{0,2},{1,3},{2,6},{3,7},{6,4},{7,5},{4,0},{5,1},{8,10},{9,11},{10,... | collective-permute-start | bytes 589832 | tf_op jit(solution)/shard_map/near_1/ppermute | solution.py:266
  12.3 2.2 %collective-permute-done.1 = bf16[384,256]{1,0:T(8,128)(2,1)S(1)} collective-permute-done((bf16[384,256]{1,0:T(8,128)(2,1)}, bf16[384,256]{1,0:T(8,128)(2,1)S(1)}, u32[]{:S(2)}, u32[]{:S(2)}) %collective-permute-start.1) | collective-permute-done | bytes 196640 | tf_op jit(solution)/shard_map/far_half/ppermute | solution.py:262
  14.5 1.4 %collective-permute-start.3 = (bf16[384,256]{1,0:T(8,128)(2,1)S(1)}, bf16[384,256]{1,0:T(8,128)(2,1)S(1)}, u32[]{:S(2)}, u32[]{:S(2)}) collective-permute-start(bf16[384,256]{1,0:T(8,128)(2,1)S(1)} %broadcast_select_fusion.1.chunk), channel_id=1, source_target_pairs={{0,2},{1,3},{2,6},{3,7},{6,4},{7,5},{4,0},{5,1},{8,10},{9,11},{10,... | collective-permute-start | bytes 589832 | tf_op jit(solution)/shard_map/far_1/ppermute | solution.py:266
  15.8 2.3 %collective-permute-done.7.chunk = bf16[384,256]{1,0:T(8,128)(2,1)S(1)} collective-permute-done((bf16[384,256]{1,0:T(8,128)(2,1)S(1)}, bf16[384,256]{1,0:T(8,128)(2,1)S(1)}, u32[]{:S(2)}, u32[]{:S(2)}) %collective-permute-start.7) | collective-permute-done | bytes 196640 | tf_op jit(solution)/shard_map/near_1/ppermute | solution.py:266
  18.2 1.1 %collective-permute-start.8 = (bf16[384,256]{1,0:T(8,128)(2,1)S(1)}, bf16[384,256]{1,0:T(8,128)(2,1)S(1)}, u32[]{:S(2)}, u32[]{:S(2)}) collective-permute-start(bf16[384,256]{1,0:T(8,128)(2,1)S(1)} %collective-permute-done.7.chunk), channel_id=1, source_target_pairs={{0,2},{1,3},{2,6},{3,7},{6,4},{7,5},{4,0},{5,1},{8,10},{9,11},{10,... | collective-permute-start | bytes 589832 | tf_op jit(solution)/shard_map/near_2/ppermute | solution.py:266
  19.3 1.6 %pack.1 = (bf16[1024,256]{1,0:T(8,128)(2,1)S(1)}, bf16[1024,256]{1,0:T(8,128)(2,1)S(1)}, s32[8]{0:T(128)S(1)}) custom-call(s32[32]{0:T(128)S(1)} %copy-done.3, s32[4,16]{1,0:T(4,128)S(1)} %copy-done.2, bf16[1024,512]{1,0:T(8,128)(2,1)S(1)} %copy-done, bf16[1024,512]{1,0:T(8,128)(2,1)S(1)} %collective-permute-done.other_anc), custom_call_target="tpu_custom_call" | custom-call | tf_op jit(solution)/shard_map/pack/pallas_call | solution.py:291
  20.9 2.8 %collective-permute-start.10 = (bf16[1024,256]{1,0:T(8,128)(2,1)S(1)}, bf16[1024,256]{1,0:T(8,128)(2,1)S(1)}, u32[]{:S(2)}, u32[]{:S(2)}) collective-permute-start(bf16[1024,256]{1,0:T(8,128)(2,1)S(1)} %get-tuple-element.21), channel_id=1, source_target_pairs={{0,0},{1,8},{2,2},{3,10},{4,4},{5,12},{6,6},{7,14},{8,1},{9,9},{10... | collective-permute-start | bytes 1572872 | tf_op jit(solution)/shard_map/sigma_0/ppermute | solution.py:262
  23.7 1.9 %collective-permute-start.11 = (bf16[1024,256]{1,0:T(8,128)(2,1)S(1)}, bf16[1024,256]{1,0:T(8,128)(2,1)S(1)}, u32[]{:S(2)}, u32[]{:S(2)}) collective-permute-start(bf16[1024,256]{1,0:T(8,128)(2,1)S(1)} %get-tuple-element.22), channel_id=1, source_target_pairs={{0,16},{1,24},{2,18},{3,26},{4,20},{5,28},{6,22},{7,30},{8,17},{9,... | collective-permute-start | bytes 1572872 | tf_op jit(solution)/shard_map/sigma_1/ppermute | solution.py:262
  25.6 0.1 broadcast_in_dim.6._
  25.7 0.3 place.8._
  26.0 3.1 %collective-permute-start.4 = (bf16[384,256]{1,0:T(8,128)(2,1)S(1)}, bf16[384,256]{1,0:T(8,128)(2,1)S(1)}, u32[]{:S(2)}, u32[]{:S(2)}) collective-permute-start(bf16[384,256]{1,0:T(8,128)(2,1)S(1)} %collective-permute-done.3.chunk), channel_id=1, source_target_pairs={{0,2},{1,3},{2,6},{3,7},{6,4},{7,5},{4,0},{5,1},{8,10},{9,11},{10,... | collective-permute-start | bytes 589832 | tf_op jit(solution)/shard_map/far_2/ppermute | solution.py:266
  29.1 0.2 place.9._
  29.4 0.3 place.10._
  29.7 0.1 collective-permute-start.9
  29.8 0.2 place.11._
  30.0 3.9 %collective-permute-done.4.chunk = bf16[384,256]{1,0:T(8,128)(2,1)S(1)} collective-permute-done((bf16[384,256]{1,0:T(8,128)(2,1)S(1)}, bf16[384,256]{1,0:T(8,128)(2,1)S(1)}, u32[]{:S(2)}, u32[]{:S(2)}) %collective-permute-start.4) | collective-permute-done | bytes 196640 | tf_op jit(solution)/shard_map/far_2/ppermute | solution.py:266
  33.9 2.2 %collective-permute-start.5 = (bf16[384,256]{1,0:T(8,128)(2,1)S(1)}, bf16[384,256]{1,0:T(8,128)(2,1)S(1)}, u32[]{:S(2)}, u32[]{:S(2)}) collective-permute-start(bf16[384,256]{1,0:T(8,128)(2,1)S(1)} %collective-permute-done.4.chunk), channel_id=1, source_target_pairs={{0,2},{1,3},{2,6},{3,7},{6,4},{7,5},{4,0},{5,1},{8,10},{9,11},{10,... | collective-permute-start | bytes 589832 | tf_op jit(solution)/shard_map/far_3/ppermute | solution.py:266
  36.1 0.2 place.12._
  36.3 0.3 place.13._
  36.6 0.1 collective-permute-start.12
  36.7 1.6 %collective-permute-done.11.refs_1_ = bf16[1024,256]{1,0:T(8,128)(2,1)S(1)} collective-permute-done((bf16[1024,256]{1,0:T(8,128)(2,1)S(1)}, bf16[1024,256]{1,0:T(8,128)(2,1)S(1)}, u32[]{:S(2)}, u32[]{:S(2)}) %collective-permute-start.11) | collective-permute-done | bytes 524320 | tf_op jit(solution)/shard_map/sigma_1/ppermute | solution.py:262
  38.3 0.3 place.14._
  38.6 2.8 %collective-permute-done.5.chunk = bf16[384,256]{1,0:T(8,128)(2,1)S(1)} collective-permute-done((bf16[384,256]{1,0:T(8,128)(2,1)S(1)}, bf16[384,256]{1,0:T(8,128)(2,1)S(1)}, u32[]{:S(2)}, u32[]{:S(2)}) %collective-permute-start.5) | collective-permute-done | bytes 196640 | tf_op jit(solution)/shard_map/far_3/ppermute | solution.py:266
  41.4 0.2 place.15.whole.own_scaled.rest_5_
  41.7 0.5 collective-permute-start.16
  42.1 0.1 stack.1
  42.3 0.0 copy-done.1
  42.3 2.3 %cross.1 = (bf16[384,256]{1,0:T(8,128)(2,1)S(1)}, bf16[384,256]{1,0:T(8,128)(2,1)S(1)}, bf16[96,512]{1,0:T(8,128)(2,1)S(1)}, bf16[96,512]{1,0:T(8,128)(2,1)}, bf...) custom-call(s32[4]{0:T(128)S(1)} %copy-done.1, s32[8]{0:T(128)S(1)} %get-tuple-element.18.slots, ...), custom_call_target="tpu_custom_call" | custom-call | tf_op jit(solution)/shard_map/cross/pallas_call | solution.py:349
  44.6 0.7 %copy-done.4 = bf16[384,256]{1,0:T(8,128)(2,1)} copy-done((bf16[384,256]{1,0:T(8,128)(2,1)}, bf16[384,256]{1,0:T(8,128)(2,1)S(1)}, u32[]{:S(2)}) %copy-start.4) | copy-done | bytes 196632
  45.3 0.7 %copy-done.5 = bf16[384,256]{1,0:T(8,128)(2,1)} copy-done((bf16[384,256]{1,0:T(8,128)(2,1)}, bf16[384,256]{1,0:T(8,128)(2,1)S(1)}, u32[]{:S(2)}) %copy-start.5) | copy-done | bytes 196632
  46.0 1.5 %collective-permute-start.17 = (bf16[96,512]{1,0:T(8,128)(2,1)}, bf16[96,512]{1,0:T(8,128)(2,1)S(1)}, u32[]{:S(2)}, u32[]{:S(2)}) collective-permute-start(bf16[96,512]{1,0:T(8,128)(2,1)} %get-tuple-element.31), channel_id=1, source_target_pairs={{0,2},{1,3},{2,0},{3,1},{4,6},{5,7},{6,4},{7,5},{8,10},{9,11},{10,... | collective-permute-start | bytes 294920 | tf_op jit(solution)/shard_map/columns_1/ppermute | solution.py:266
  47.5 1.0 %collective-permute-start.18 = (bf16[96,512]{1,0:T(8,128)(2,1)}, bf16[96,512]{1,0:T(8,128)(2,1)S(1)}, u32[]{:S(2)}, u32[]{:S(2)}) collective-permute-start(bf16[96,512]{1,0:T(8,128)(2,1)} %get-tuple-element.32), channel_id=1, source_target_pairs={{0,4},{1,5},{2,6},{3,7},{4,0},{5,1},{6,2},{7,3},{8,12},{9,13},{10,... | collective-permute-start | bytes 294920 | tf_op jit(solution)/shard_map/columns_2/ppermute | solution.py:266
  48.5 1.1 %collective-permute-start.19 = (bf16[96,512]{1,0:T(8,128)(2,1)}, bf16[96,512]{1,0:T(8,128)(2,1)S(1)}, u32[]{:S(2)}, u32[]{:S(2)}) collective-permute-start(bf16[96,512]{1,0:T(8,128)(2,1)} %get-tuple-element.33), channel_id=1, source_target_pairs={{0,6},{1,7},{2,4},{3,5},{4,2},{5,3},{6,0},{7,1},{8,14},{9,15},{10,... | collective-permute-start | bytes 294920 | tf_op jit(solution)/shard_map/columns_3/ppermute | solution.py:266
  49.6 3.2 %collective-permute-start.14 = (bf16[384,256]{1,0:T(8,128)(2,1)}, bf16[384,256]{1,0:T(8,128)(2,1)S(1)}, u32[]{:S(2)}, u32[]{:S(2)}) collective-permute-start(bf16[384,256]{1,0:T(8,128)(2,1)} %copy-done.5), channel_id=1, source_target_pairs={{0,0},{1,8},{2,2},{3,10},{4,4},{5,12},{6,6},{7,14},{8,1},{9,9},{10... | collective-permute-start | bytes 589832 | tf_op jit(solution)/shard_map/rows_out/ppermute | solution.py:262
  52.8 0.0 collective-permute-start.15
  52.8 0.4 pivot_first.1
  53.2 3.9 %collective-permute-done.18.rest_3_ = bf16[96,512]{1,0:T(8,128)(2,1)S(1)} collective-permute-done((bf16[96,512]{1,0:T(8,128)(2,1)}, bf16[96,512]{1,0:T(8,128)(2,1)S(1)}, u32[]{:S(2)}, u32[]{:S(2)}) %collective-permute-start.18) | collective-permute-done | bytes 98336 | tf_op jit(solution)/shard_map/columns_2/ppermute | solution.py:266
  57.1 1.0 %pivot.1 = bf16[96,768]{1,0:T(8,128)(2,1)S(1)} custom-call(f32[96,384]{1,0:T(8,128)S(1)} %get-tuple-element.29.rest_0_, f32[96,384]{1,0:T(8,128)S(1)} %get-tuple-element.30.rest_1_, bf16[96,512]{1,0:T(8,128)(2,1)S(1)} %collective-permute-done.17.rest_2_, bf16[96,512]{1,0:T(8,128)(2,1)S(1)} %collective-permute-done.18.rest_3_, ...), custom_call_target="tpu_custom_call" | custom-call | tf_op jit(solution)/shard_map/pivot/pallas_call | solution.py:379
  58.1 3.5 %collective-permute-start.20 = (bf16[96,768]{1,0:T(8,128)(2,1)S(1)}, bf16[96,768]{1,0:T(8,128)(2,1)S(1)}, u32[]{:S(2)}, u32[]{:S(2)}) collective-permute-start(bf16[96,768]{1,0:T(8,128)(2,1)S(1)} %pivot.1), channel_id=1, source_target_pairs={{0,0},{1,8},{2,2},{3,10},{4,4},{5,12},{6,6},{7,14},{8,1},{9,9},{10... | collective-permute-start | bytes 442376 | tf_op jit(solution)/shard_map/term_out/ppermute | solution.py:262
  61.6 0.4 fusion
  62.1 1.0 %turn.1 = bf16[1,256,768]{2,1,0:T(8,128)(2,1)} custom-call(bf16[384,256]{1,0:T(8,128)(2,1)S(1)} %collective-permute-done.14.own_rows, bf16[384,256]{1,0:T(8,128)(2,1)S(1)} %collective-permute-done.15.other_rows), custom_call_target="tpu_custom_call" | custom-call | tf_op jit(solution)/shard_map/turn/pallas_call | solution.py:388
  63.1 1.5 %collective-permute-done.20 = bf16[96,768]{1,0:T(8,128)(2,1)S(1)} collective-permute-done((bf16[96,768]{1,0:T(8,128)(2,1)S(1)}, bf16[96,768]{1,0:T(8,128)(2,1)S(1)}, u32[]{:S(2)}, u32[]{:S(2)}) %collective-permute-start.20) | collective-permute-done | bytes 147488 | tf_op jit(solution)/shard_map/term_out/ppermute | solution.py:262
  64.6 0.7 %add_bitcast_fusion = f32[1,96,768]{2,1,0:T(8,128)} fusion(f32[96,768]{1,0:T(8,128)S(1)} %fusion, bf16[96,768]{1,0:T(8,128)(2,1)S(1)} %collective-permute-done.20), kind=kLoop, calls=%fused_computation | loop fusion | flops 147456 | bytes 737280 | tf_op jit(solution)/shard_map/broadcast_in_dim | solution.py:398
  (28 shorter events, 0.1 us)
Async XLA Ops:
  0.6 18.7 %copy-start = (bf16[1024,512]{1,0:T(8,128)(2,1)S(1)}, bf16[1024,512]{1,0:T(8,128)(2,1)}, u32[]{:S(2)}) copy-start(bf16[1024,512]{1,0:T(8,128)(2,1)} %anc.1) | copy-start | bytes 3145732
  0.6 18.7 %copy-start.3 = (s32[32]{0:T(128)S(1)}, s32[32]{0:T(128)}, u32[]{:S(2)}) copy-start(s32[32]{0:T(128)} %row_home_in.1) | copy-start | bytes 388
  0.7 18.7 %copy-start.2 = (s32[4,16]{1,0:T(4,128)S(1)}, s32[4,16]{1,0:T(4,128)}, u32[]{:S(2)}) copy-start(s32[4,16]{1,0:T(4,128)} %lists_in.1) | copy-start | bytes 772
  0.7 18.6 %collective-permute-start = (bf16[1024,512]{1,0:T(8,128)(2,1)}, bf16[1024,512]{1,0:T(8,128)(2,1)S(1)}, u32[]{:S(2)}, u32[]{:S(2)}) collective-permute-start(bf16[1024,512]{1,0:T(8,128)(2,1)} %anc.1), channel_id=1, source_target_pairs={{0,8},{8,0},{16,24},{24,16},{1,9},{9,1},{17,25},{25,17},{2,10},{10... | collective-permute-start | bytes 3145736 | tf_op jit(solution)/shard_map/rows_of_sibling/ppermute | solution.py:258
  3.7 7.2 %collective-permute-start.6 = (bf16[384,256]{1,0:T(8,128)(2,1)}, bf16[384,256]{1,0:T(8,128)(2,1)S(1)}, u32[]{:S(2)}, u32[]{:S(2)}) collective-permute-start(bf16[384,256]{1,0:T(8,128)(2,1)} %get-tuple-element.20), channel_id=1, source_target_pairs={{0,8},{2,10},{4,12},{6,14},{9,1},{11,3},{13,5},{15,7},{16,24},{18,... | collective-permute-start | bytes 589832 | tf_op jit(solution)/shard_map/near_half/ppermute | solution.py:262
  5.0 9.5 %collective-permute-start.2 = (bf16[384,256]{1,0:T(8,128)(2,1)}, bf16[384,256]{1,0:T(8,128)(2,1)S(1)}, u32[]{:S(2)}, u32[]{:S(2)}) collective-permute-start(bf16[384,256]{1,0:T(8,128)(2,1)} %get-tuple-element.20), channel_id=1, source_target_pairs={{1,8},{3,10},{5,12},{7,14},{8,1},{10,3},{12,5},{14,7},{17,24},{19,... | collective-permute-start | bytes 589832 | tf_op jit(solution)/shard_map/far_half_off/ppermute | solution.py:262
  9.4 5.0 %collective-permute-start.1 = (bf16[384,256]{1,0:T(8,128)(2,1)}, bf16[384,256]{1,0:T(8,128)(2,1)S(1)}, u32[]{:S(2)}, u32[]{:S(2)}) collective-permute-start(bf16[384,256]{1,0:T(8,128)(2,1)} %get-tuple-element.19), channel_id=1, source_target_pairs={{1,0},{3,2},{5,4},{7,6},{8,9},{10,11},{12,13},{14,15},{17,16},{19,... | collective-permute-start | bytes 589832 | tf_op jit(solution)/shard_map/far_half/ppermute | solution.py:262
  10.9 7.3 %collective-permute-start.7 = (bf16[384,256]{1,0:T(8,128)(2,1)S(1)}, bf16[384,256]{1,0:T(8,128)(2,1)S(1)}, u32[]{:S(2)}, u32[]{:S(2)}) collective-permute-start(bf16[384,256]{1,0:T(8,128)(2,1)S(1)} %broadcast_select_fusion.chunk), channel_id=1, source_target_pairs={{0,2},{1,3},{2,6},{3,7},{6,4},{7,5},{4,0},{5,1},{8,10},{9,11},{10,... | collective-permute-start | bytes 589832 | tf_op jit(solution)/shard_map/near_1/ppermute | solution.py:266
  14.5 11.6 %collective-permute-start.3 = (bf16[384,256]{1,0:T(8,128)(2,1)S(1)}, bf16[384,256]{1,0:T(8,128)(2,1)S(1)}, u32[]{:S(2)}, u32[]{:S(2)}) collective-permute-start(bf16[384,256]{1,0:T(8,128)(2,1)S(1)} %broadcast_select_fusion.1.chunk), channel_id=1, source_target_pairs={{0,2},{1,3},{2,6},{3,7},{6,4},{7,5},{4,0},{5,1},{8,10},{9,11},{10,... | collective-permute-start | bytes 589832 | tf_op jit(solution)/shard_map/far_1/ppermute | solution.py:266
  18.2 11.5 %collective-permute-start.8 = (bf16[384,256]{1,0:T(8,128)(2,1)S(1)}, bf16[384,256]{1,0:T(8,128)(2,1)S(1)}, u32[]{:S(2)}, u32[]{:S(2)}) collective-permute-start(bf16[384,256]{1,0:T(8,128)(2,1)S(1)} %collective-permute-done.7.chunk), channel_id=1, source_target_pairs={{0,2},{1,3},{2,6},{3,7},{6,4},{7,5},{4,0},{5,1},{8,10},{9,11},{10,... | collective-permute-start | bytes 589832 | tf_op jit(solution)/shard_map/near_2/ppermute | solution.py:266
  20.9 15.7 %collective-permute-start.10 = (bf16[1024,256]{1,0:T(8,128)(2,1)S(1)}, bf16[1024,256]{1,0:T(8,128)(2,1)S(1)}, u32[]{:S(2)}, u32[]{:S(2)}) collective-permute-start(bf16[1024,256]{1,0:T(8,128)(2,1)S(1)} %get-tuple-element.21), channel_id=1, source_target_pairs={{0,0},{1,8},{2,2},{3,10},{4,4},{5,12},{6,6},{7,14},{8,1},{9,9},{10... | collective-permute-start | bytes 1572872 | tf_op jit(solution)/shard_map/sigma_0/ppermute | solution.py:262
  23.7 14.6 %collective-permute-start.11 = (bf16[1024,256]{1,0:T(8,128)(2,1)S(1)}, bf16[1024,256]{1,0:T(8,128)(2,1)S(1)}, u32[]{:S(2)}, u32[]{:S(2)}) collective-permute-start(bf16[1024,256]{1,0:T(8,128)(2,1)S(1)} %get-tuple-element.22), channel_id=1, source_target_pairs={{0,16},{1,24},{2,18},{3,26},{4,20},{5,28},{6,22},{7,30},{8,17},{9,... | collective-permute-start | bytes 1572872 | tf_op jit(solution)/shard_map/sigma_1/ppermute | solution.py:262
  26.0 7.9 %collective-permute-start.4 = (bf16[384,256]{1,0:T(8,128)(2,1)S(1)}, bf16[384,256]{1,0:T(8,128)(2,1)S(1)}, u32[]{:S(2)}, u32[]{:S(2)}) collective-permute-start(bf16[384,256]{1,0:T(8,128)(2,1)S(1)} %collective-permute-done.3.chunk), channel_id=1, source_target_pairs={{0,2},{1,3},{2,6},{3,7},{6,4},{7,5},{4,0},{5,1},{8,10},{9,11},{10,... | collective-permute-start | bytes 589832 | tf_op jit(solution)/shard_map/far_2/ppermute | solution.py:266
  29.7 8.6 %collective-permute-start.9 = (bf16[384,256]{1,0:T(8,128)(2,1)S(1)}, bf16[384,256]{1,0:T(8,128)(2,1)S(1)}, u32[]{:S(2)}, u32[]{:S(2)}) collective-permute-start(bf16[384,256]{1,0:T(8,128)(2,1)S(1)} %collective-permute-done.8.chunk), channel_id=1, source_target_pairs={{0,2},{1,3},{2,6},{3,7},{6,4},{7,5},{4,0},{5,1},{8,10},{9,11},{10,... | collective-permute-start | bytes 589832 | tf_op jit(solution)/shard_map/near_3/ppermute | solution.py:266
  33.9 7.5 %collective-permute-start.5 = (bf16[384,256]{1,0:T(8,128)(2,1)S(1)}, bf16[384,256]{1,0:T(8,128)(2,1)S(1)}, u32[]{:S(2)}, u32[]{:S(2)}) collective-permute-start(bf16[384,256]{1,0:T(8,128)(2,1)S(1)} %collective-permute-done.4.chunk), channel_id=1, source_target_pairs={{0,2},{1,3},{2,6},{3,7},{6,4},{7,5},{4,0},{5,1},{8,10},{9,11},{10,... | collective-permute-start | bytes 589832 | tf_op jit(solution)/shard_map/far_3/ppermute | solution.py:266
  36.6 5.5 %collective-permute-start.12 = (bf16[1024,256]{1,0:T(8,128)(2,1)S(1)}, bf16[1024,256]{1,0:T(8,128)(2,1)S(1)}, u32[]{:S(2)}, u32[]{:S(2)}) collective-permute-start(bf16[1024,256]{1,0:T(8,128)(2,1)S(1)} %collective-permute-done.10.refs_0_), channel_id=1, source_target_pairs={{0,8},{8,0},{16,24},{24,16},{1,9},{9,1},{17,25},{25,17},{2,10},{10... | collective-permute-start | bytes 1572872 | tf_op jit(solution)/shard_map/share_0/ppermute | solution.py:258
  38.3 3.8 %collective-permute-start.13 = (bf16[1024,256]{1,0:T(8,128)(2,1)S(1)}, bf16[1024,256]{1,0:T(8,128)(2,1)S(1)}, u32[]{:S(2)}, u32[]{:S(2)}) collective-permute-start(bf16[1024,256]{1,0:T(8,128)(2,1)S(1)} %collective-permute-done.11.refs_1_), channel_id=1, source_target_pairs={{0,8},{8,0},{16,24},{24,16},{1,9},{9,1},{17,25},{25,17},{2,10},{10... | collective-permute-start | bytes 1572872 | tf_op jit(solution)/shard_map/share_1/ppermute | solution.py:258
  41.6 0.7 %copy-start.1 = (s32[4]{0:T(128)S(1)}, s32[4]{0:T(128)}, u32[]{:S(2)}) copy-start(s32[4]{0:T(128)} %front_blocks.1) | copy-start | bytes 52
  41.7 11.2 %collective-permute-start.16 = (bf16[8,384,256]{2,1,0:T(8,128)(2,1)S(1)}, bf16[8,384,256]{2,1,0:T(8,128)(2,1)S(1)}, u32[]{:S(2)}, u32[]{:S(2)}) collective-permute-start(bf16[8,384,256]{2,1,0:T(8,128)(2,1)S(1)} %place.15.whole.own_scaled.rest_5_), channel_id=1, source_target_pairs={{0,8},{8,0},{16,24},{24,16},{1,9},{9,1},{17,25},{25,17},{2,10},{10... | collective-permute-start | bytes 4718600 | tf_op jit(solution)/shard_map/scaled_of_sibling/ppermute | solution.py:258
  44.6 0.7 %copy-start.4 = (bf16[384,256]{1,0:T(8,128)(2,1)}, bf16[384,256]{1,0:T(8,128)(2,1)S(1)}, u32[]{:S(2)}) copy-start(bf16[384,256]{1,0:T(8,128)(2,1)S(1)} %get-tuple-element.26) | copy-start | bytes 589828
  45.3 0.7 %copy-start.5 = (bf16[384,256]{1,0:T(8,128)(2,1)}, bf16[384,256]{1,0:T(8,128)(2,1)S(1)}, u32[]{:S(2)}) copy-start(bf16[384,256]{1,0:T(8,128)(2,1)S(1)} %get-tuple-element.25) | copy-start | bytes 589828
  46.0 7.3 %collective-permute-start.17 = (bf16[96,512]{1,0:T(8,128)(2,1)}, bf16[96,512]{1,0:T(8,128)(2,1)S(1)}, u32[]{:S(2)}, u32[]{:S(2)}) collective-permute-start(bf16[96,512]{1,0:T(8,128)(2,1)} %get-tuple-element.31), channel_id=1, source_target_pairs={{0,2},{1,3},{2,0},{3,1},{4,6},{5,7},{6,4},{7,5},{8,10},{9,11},{10,... | collective-permute-start | bytes 294920 | tf_op jit(solution)/shard_map/columns_1/ppermute | solution.py:266
  47.5 9.6 %collective-permute-start.18 = (bf16[96,512]{1,0:T(8,128)(2,1)}, bf16[96,512]{1,0:T(8,128)(2,1)S(1)}, u32[]{:S(2)}, u32[]{:S(2)}) collective-permute-start(bf16[96,512]{1,0:T(8,128)(2,1)} %get-tuple-element.32), channel_id=1, source_target_pairs={{0,4},{1,5},{2,6},{3,7},{4,0},{5,1},{6,2},{7,3},{8,12},{9,13},{10,... | collective-permute-start | bytes 294920 | tf_op jit(solution)/shard_map/columns_2/ppermute | solution.py:266
  48.5 8.6 %collective-permute-start.19 = (bf16[96,512]{1,0:T(8,128)(2,1)}, bf16[96,512]{1,0:T(8,128)(2,1)S(1)}, u32[]{:S(2)}, u32[]{:S(2)}) collective-permute-start(bf16[96,512]{1,0:T(8,128)(2,1)} %get-tuple-element.33), channel_id=1, source_target_pairs={{0,6},{1,7},{2,4},{3,5},{4,2},{5,3},{6,0},{7,1},{8,14},{9,15},{10,... | collective-permute-start | bytes 294920 | tf_op jit(solution)/shard_map/columns_3/ppermute | solution.py:266
  49.6 12.5 %collective-permute-start.14 = (bf16[384,256]{1,0:T(8,128)(2,1)}, bf16[384,256]{1,0:T(8,128)(2,1)S(1)}, u32[]{:S(2)}, u32[]{:S(2)}) collective-permute-start(bf16[384,256]{1,0:T(8,128)(2,1)} %copy-done.5), channel_id=1, source_target_pairs={{0,0},{1,8},{2,2},{3,10},{4,4},{5,12},{6,6},{7,14},{8,1},{9,9},{10... | collective-permute-start | bytes 589832 | tf_op jit(solution)/shard_map/rows_out/ppermute | solution.py:262
  52.8 9.3 %collective-permute-start.15 = (bf16[384,256]{1,0:T(8,128)(2,1)}, bf16[384,256]{1,0:T(8,128)(2,1)S(1)}, u32[]{:S(2)}, u32[]{:S(2)}) collective-permute-start(bf16[384,256]{1,0:T(8,128)(2,1)} %copy-done.4), channel_id=1, source_target_pairs={{0,1},{1,9},{2,3},{3,11},{4,5},{5,13},{6,7},{7,15},{8,0},{9,8},{10... | collective-permute-start | bytes 589832 | tf_op jit(solution)/shard_map/rows_out_other/ppermute | solution.py:262
  57.1 4.5 %copy-start.6 = (bf16[1,768,768]{2,1,0:T(8,128)(2,1)S(1)}, bf16[1,768,768]{2,1,0:T(8,128)(2,1)}, u32[]{:S(2)}) copy-start(bf16[1,768,768]{2,1,0:T(8,128)(2,1)} %param.11) | copy-start | bytes 3538948
  58.1 6.5 %collective-permute-start.20 = (bf16[96,768]{1,0:T(8,128)(2,1)S(1)}, bf16[96,768]{1,0:T(8,128)(2,1)S(1)}, u32[]{:S(2)}, u32[]{:S(2)}) collective-permute-start(bf16[96,768]{1,0:T(8,128)(2,1)S(1)} %pivot.1), channel_id=1, source_target_pairs={{0,0},{1,8},{2,2},{3,10},{4,4},{5,12},{6,6},{7,14},{8,1},{9,9},{10... | collective-permute-start | bytes 442376 | tf_op jit(solution)/shard_map/term_out/ppermute | solution.py:262

commit v4 on v3

--- a/solution.py
+++ b/solution.py
@@ -44,18 +44,22 @@
     return position
 
 
+def far_first(n):
+    return [0, *range(2, n), *range(1, min(n, 2))]
+
+
 def coordinates():
     g, p = lax.axis_index("grp"), lax.axis_index("pan")
     return g >> 1, g & 1, p >> 1, p & 1
 
 
-def params(mib=40):
+def params(mib=16):
     return pltpu.CompilerParams(vmem_limit_bytes=mib * 1024 * 1024)
 
 
 def pack_kernel(groups, pan, row_home_in, lists_in, anc, other_anc, *rest):
     pairs = groups // 2
-    outs, slots = rest[:pairs], rest[pairs]
+    outs, members = rest[:pairs], rest[pairs]
     row_home, lists, place, sems = rest[pairs + 1 :]
     loads = [
         pltpu.make_async_copy(row_home_in, row_home, sems.at[0]),
@@ -79,7 +83,7 @@
             rank = rank + (owners[v] == owners[w]).astype(jnp.int32)
         step = owners[w] >> 1
         step = step ^ h if power_of_two(pairs) else (h + pairs - step) % pairs
-        slots[w] = (2 * step + (owners[w] & 1)) * windows + rank
+        members[(2 * step + (owners[w] & 1)) * windows + rank] = jnp.int32(w)
 
         @pl.when(owners[w] >> 1 == h)
         def _():
@@ -131,78 +135,59 @@
         give[at] = turned[pl.ds(share * (2 * place + 1 - c), share)].astype(BF16)
 
 
-def stack_kernel(pairs, *refs):
-    own_in, other_in, (own, other) = refs[:pairs], refs[pairs : 2 * pairs], refs[2 * pairs :]
-    depth = own.shape[1]
-    windows = own_in[0].shape[0] // depth
-    for slot in range(own.shape[0]):
+def stack_kernel(pairs, members, *refs):
+    own_in, other_in, out = refs[:pairs], refs[pairs : 2 * pairs], refs[2 * pairs]
+    _, c, _, _ = coordinates()
+    count = members.shape[0]
+    depth, rows = out.shape[0] // count, out.shape[1] // 2
+    windows = count // pairs
+    for slot in range(count):
         at = pl.ds(slot % windows * depth, depth)
-        own[slot] = own_in[slot // windows][at]
-        other[slot] = other_in[slot // windows][at]
+        to = pl.ds(pl.multiple_of(members[slot] * depth, depth), depth)
+        own, other = own_in[slot // windows][at], other_in[slot // windows][at]
+        out[to, :rows] = jnp.where(c == 0, own, other)
+        out[to, rows:] = jnp.where(c == 0, other, own)
 
 
 def place_kernel(n, k, side, chunk, _, whole, sem):
     _, _, q, l = coordinates()
     origin = ring_place((ring_position(q, n) + n - k) % n, n)
-    copy = pltpu.make_async_copy(chunk, whole.at[2 * origin + (l ^ side)], sem)
+    rows = chunk.shape[1]
+    at = pl.ds(pl.multiple_of((2 * origin + (l ^ side)) * rows, rows), rows)
+    copy = pltpu.make_async_copy(chunk, whole.at[:, at], sem)
     copy.start()
     copy.wait()
 
 
-def cross_kernel(n, front_blocks, slots, whole, own_sigma, other_sigma, mine, give, *rest):
+def cross_kernel(n, front_blocks, whole, sigma, mine, give, *rest):
     parts, total = rest[:n], rest[n]
     h, c, q, l = coordinates()
     half, rows = mine.shape
     padded = half // n
-    own = jnp.zeros((half, rows), F32)
-    other = jnp.zeros((half, rows), F32)
-    for member in range(2 * n):
-        slot = slots[member]
-        own = own + jnp.dot(whole[member], own_sigma[slot], preferred_element_type=F32)
-        other = other + jnp.dot(whole[member], other_sigma[slot], preferred_element_type=F32)
-    live = front_blocks[2 * h + l]
-    block = lax.broadcasted_iota(jnp.int32, (half, rows), 1) // BLK
-    own = jnp.where((2 * q + c) * (rows // BLK) + block < live, -own, 0.0)
-    other = jnp.where((2 * q + 1 - c) * (rows // BLK) + block < live, -other, 0.0)
-    mine[...] = own.astype(BF16)
-    give[...] = other.astype(BF16)
-    total[c] = own
-    total[1 - c] = other
+    product = jnp.dot(whole[...], sigma[...], preferred_element_type=F32)
+    block = (2 * q * rows + lax.broadcasted_iota(jnp.int32, product.shape, 1)) // BLK
+    product = jnp.where(block < front_blocks[2 * h + l], -product, 0.0)
+    total[...] = product
+    product = product.astype(BF16)
+    mine[...] = jnp.where(c == 0, product[:, :rows], product[:, rows:])
+    give[...] = jnp.where(c == 0, product[:, rows:], product[:, :rows])
     for k in range(n):
-        at = pl.ds(peer(q, k, n) * padded, padded)
-        for side in range(2):
-            parts[k][:, pl.ds(side * rows, rows)] = total[side, at].astype(BF16)
-
-
-def pivot_first_kernel(n, part, own_scaled, other_scaled, own_out, other_out):
-    _, _, q, _ = coordinates()
-    own, other = pivot_terms(part, q, own_scaled, other_scaled)
-    own_out[...] = own
-    other_out[...] = other
-
-
-def pivot_terms(part, origin, own_scaled, other_scaled):
-    rows = own_scaled.shape[2]
-    sums = [None, None]
-    for side in range(2):
-        piece = part[:, pl.ds(side * rows, rows)]
-        for i, scaled in enumerate((own_scaled, other_scaled)):
-            term = lax.dot_general(
-                piece, scaled[2 * origin + side], (((1,), (1,)), ((), ())), preferred_element_type=F32
-            )
-            sums[i] = term if sums[i] is None else sums[i] + term
-    return sums
+        at = pl.ds(pl.multiple_of(peer(q, k, n) * padded, padded), padded)
+        parts[k][...] = total[at].astype(BF16)
 
 
 def pivot_kernel(n, share, *rest):
-    own_first, other_first = rest[:2]
-    parts, own_scaled, other_scaled, out = rest[2 : n + 1], rest[n + 1], rest[n + 2], rest[n + 3]
+    parts, (own_scaled, other_scaled, out, columns) = rest[:n], rest[n:]
     _, c, q, _ = coordinates()
-    padded = parts[0].shape[0]
-    own, other = own_first[...], other_first[...]
-    for k in range(1, n):
-        terms = pivot_terms(parts[k - 1], source(q, k, n), own_scaled, other_scaled)
-        own, other = own + terms[0], other + terms[1]
+    padded, depth = parts[0].shape
+    for k, part in zip(far_first(n), parts):
+        at = pl.ds(pl.multiple_of(source(q, k, n) * depth, depth), depth)
+        columns[:, at] = part[...]
+    across = (((1,), (1,)), ((), ()))
+    own, other = [
+        lax.dot_general(columns[...], scaled[...], across, preferred_element_type=F32)
+        for scaled in (own_scaled, other_scaled)
+    ]
     low = jnp.where(c == 0, own, other)
     high = jnp.where(c == 0, other, own)
     pieces = []
@@ -288,7 +273,7 @@
         everywhere(give, crossing, "far_half_off"),
     )
 
-    *packed, slots = pl.pallas_call(
+    *packed, members = pl.pallas_call(
         functools.partial(pack_kernel, groups, pan),
         out_shape=[shape((2 * wanted, rows), BF16)] * pairs + [shape((pan,), jnp.int32)],
         in_specs=[HBM, HBM, VMEM, VMEM],
@@ -312,13 +297,13 @@
         nears.append(along(nears[-1], ring, f"near_{step}"))
         fars.append(along(fars[-1], ring, f"far_{step}"))
 
-    whole = jnp.zeros((pan, half, rows), BF16)
+    whole = jnp.zeros((half, pan * rows), BF16)
     anywhere = pl.BlockSpec(memory_space=pl.ANY)
     for k in range(n):
         for side, chunks in enumerate((nears, fars)):
             whole = pl.pallas_call(
                 functools.partial(place_kernel, n, k, side),
-                out_shape=shape((pan, half, rows), BF16),
+                out_shape=shape(whole.shape, BF16),
                 in_specs=[anywhere, anywhere],
                 out_specs=anywhere,
                 scratch_shapes=[pltpu.SemaphoreType.DMA(())],
@@ -337,27 +322,27 @@
     ]
     swapped = [swap(piece, f"share_{k}") for k, piece in enumerate(arrived)]
     triangle, _ = lax.optimization_barrier((triangle, nears[-2]))
-    own_sigma, other_sigma = pl.pallas_call(
+    sigma = pl.pallas_call(
         functools.partial(stack_kernel, pairs),
-        out_shape=[shape((pan, wanted // windows, rows), BF16)] * 2,
-        in_specs=[VMEM] * groups,
-        out_specs=[VMEM] * 2,
+        out_shape=shape((pan * wanted // windows, 2 * rows), BF16),
+        in_specs=[SMEM] + [VMEM] * groups,
+        out_specs=VMEM,
         compiler_params=params(),
         cost_estimate=pl.CostEstimate(flops=STACK, bytes_accessed=0, transcendentals=0),
         name="stack",
-    )(*arrived, *swapped)
+    )(members, *arrived, *swapped)
     mine, give, *parts = pl.pallas_call(
         functools.partial(cross_kernel, n),
         out_shape=[shape((half, rows), BF16)] * 2
         + [shape((padded, 2 * rows), BF16)] * n,
-        in_specs=[SMEM] * 2 + [VMEM] * 3,
+        in_specs=[SMEM] + [VMEM] * 2,
         out_specs=[VMEM] * (n + 2),
-        scratch_shapes=[pltpu.VMEM((2, half, rows), F32)],
+        scratch_shapes=[pltpu.VMEM((half, 2 * rows), F32)],
         compiler_params=params(),
         name="cross",
-    )(front_blocks, slots, whole, own_sigma, other_sigma)
-
-    for k in range(1, n):
+    )(front_blocks, whole, sigma)
+
+    for k in far_first(n)[1:]:
         parts[k] = along(
             parts[k],
             [(2 * q + l, 2 * peer(q, k, n) + l) for q in range(n) for l in range(2)],
@@ -368,22 +353,15 @@
     other_rows = everywhere(
         give, [(at(h, c, q, l), at(h, l, q, 1 - c)) for h, c, q, l in places], "rows_out_other"
     )
-    firsts = pl.pallas_call(
-        functools.partial(pivot_first_kernel, n),
-        out_shape=[shape((padded, half), F32)] * 2,
-        in_specs=[VMEM] * 3,
-        out_specs=[VMEM] * 2,
-        compiler_params=params(),
-        name="pivot_first",
-    )(parts[0], whole, other_whole)
     term = pl.pallas_call(
         functools.partial(pivot_kernel, n, share),
         out_shape=shape((padded, width), BF16),
-        in_specs=[VMEM] * (n + 3),
+        in_specs=[VMEM] * (n + 2),
         out_specs=VMEM,
+        scratch_shapes=[pltpu.VMEM((padded, pan * rows), BF16)],
         compiler_params=params(),
         name="pivot",
-    )(*firsts, *parts[1:], whole, other_whole)
+    )(*[parts[k] for k in far_first(n)], whole, other_whole)
     term = everywhere(term, exchange, "term_out")
     cross = pl.pallas_call(
         functools.partial(turn_kernel, pan, share),

time: 65.9 us -> 65.9 us (level)
  Pallas kernels: 11.3 us -> 10 us
  waiting for transfers between devices: 18.3 us -> 19.2 us
    pallas_call x8, Pallas kernels: 2.03 us -> 0.36 us  [per_device(): pl.pallas_call(functools.partial(place_kernel, n, k, side), out_shape=sha...]
    ppermute x8, waiting for transfers between devices: 5.33 us -> 6.53 us  [everywhere(): return lax.ppermute(x, ('grp', 'pan'), pairs_of)]
    ppermute x8, starting transfers between devices: 18.5 us -> 19.5 us  [everywhere(): return lax.ppermute(x, ('grp', 'pan'), pairs_of)]
  transfers between devices with their start and end apart: 21 -> 21, of which waited for: 7 -> 7; matrix products, arithmetic and copies ran while one was open for 1% -> 1% of each run, Pallas kernels for 17% -> 15%
where the time goes in v4:
time: 65.9 us; the launch traced here: 65.7 us
  starting transfers between devices  32.7 us (50%)
  waiting for transfers between devices  19.2 us (29%)
  Pallas kernels  10 us (15%)
  local copies, waits for them, and re-layouts  1.55 us (2%)
  between operations  0.94 us (1%)
  other arithmetic  0.8 us (1%)
    ppermute x8, starting transfers between devices, everywhere(): return lax.ppermute(x, ('grp', 'pan'), pairs_of)  19.5 us
    ppermute x9, waiting for transfers between devices, along(): return lax.ppermute(x, 'pan', pairs_of)  12.6 us
    ppermute x9, starting transfers between devices, along(): return lax.ppermute(x, 'pan', pairs_of)  12.5 us
    ppermute x8, waiting for transfers between devices, everywhere(): return lax.ppermute(x, ('grp', 'pan'), pairs_of)  6.53 us
    pallas_call x1, Pallas kernels, per_device(): pl.pallas_call(functools.partial(scale_kernel, pan), out_shape=[shape((ha...  2.86 us
    pallas_call x1, Pallas kernels, per_device(): pl.pallas_call(functools.partial(cross_kernel, n), out_shape=[shape((half...  2.27 us
    pallas_call x1, Pallas kernels, per_device(): pl.pallas_call(functools.partial(pack_kernel, groups, pan), out_shape=[sh...  1.63 us
    unnamed x14, local copies, waits for them, and re-layouts  1.37 us
  transfers between devices with their start and end apart: 21, of which 7 were waited for; matrix products, arithmetic and copies ran while one was open for 1% of the time, Pallas kernels for 15%

profile of v4, /device:TPU:1, one launch (start us, length us, event | category | flops | bytes accessed | tf_op | source)
XLA Modules:
  0.0 65.7 jit_solution(15345592214662238071)
XLA Ops:
  0.7 0.1 collective-permute-start.9
  0.8 2.9 %scale.1 = (bf16[384,256]{1,0:T(8,128)(2,1)}, bf16[384,256]{1,0:T(8,128)(2,1)}) custom-call(s32[4]{0:T(128)} %front_blocks.1, bf16[256,768]{1,0:T(8,128)(2,1)} %bitcast.10, bf16[768,768]{1,0:T(8,128)(2,1)} %bitcast.9), custom_call_target="tpu_custom_call" | custom-call | tf_op jit(solution)/shard_map/scale/pallas_call | solution.py:253
  3.7 1.3 %collective-permute-start.5 = (bf16[384,256]{1,0:T(8,128)(2,1)}, bf16[384,256]{1,0:T(8,128)(2,1)S(1)}, u32[]{:S(2)}, u32[]{:S(2)}) collective-permute-start(bf16[384,256]{1,0:T(8,128)(2,1)} %get-tuple-element.15), channel_id=1, source_target_pairs={{0,8},{2,10},{4,12},{6,14},{9,1},{11,3},{13,5},{15,7},{16,24},{18,... | collective-permute-start | bytes 589832 | tf_op jit(solution)/shard_map/near_half/ppermute | solution.py:247
  5.0 4.5 %collective-permute-start.1 = (bf16[384,256]{1,0:T(8,128)(2,1)}, bf16[384,256]{1,0:T(8,128)(2,1)S(1)}, u32[]{:S(2)}, u32[]{:S(2)}) collective-permute-start(bf16[384,256]{1,0:T(8,128)(2,1)} %get-tuple-element.15), channel_id=1, source_target_pairs={{1,8},{3,10},{5,12},{7,14},{8,1},{10,3},{12,5},{14,7},{17,24},{19,... | collective-permute-start | bytes 589832 | tf_op jit(solution)/shard_map/far_half_off/ppermute | solution.py:247
  9.4 1.4 %collective-permute-start = (bf16[384,256]{1,0:T(8,128)(2,1)}, bf16[384,256]{1,0:T(8,128)(2,1)S(1)}, u32[]{:S(2)}, u32[]{:S(2)}) collective-permute-start(bf16[384,256]{1,0:T(8,128)(2,1)} %get-tuple-element.14), channel_id=1, source_target_pairs={{1,0},{3,2},{5,4},{7,6},{8,9},{10,11},{12,13},{14,15},{17,16},{19,... | collective-permute-start | bytes 589832 | tf_op jit(solution)/shard_map/far_half/ppermute | solution.py:247
  10.9 1.4 %collective-permute-start.6 = (bf16[384,256]{1,0:T(8,128)(2,1)S(1)}, bf16[384,256]{1,0:T(8,128)(2,1)S(1)}, u32[]{:S(2)}, u32[]{:S(2)}) collective-permute-start(bf16[384,256]{1,0:T(8,128)(2,1)S(1)} %broadcast_select_fusion.chunk), channel_id=1, source_target_pairs={{0,2},{1,3},{2,6},{3,7},{6,4},{7,5},{4,0},{5,1},{8,10},{9,11},{10,... | collective-permute-start | bytes 589832 | tf_op jit(solution)/shard_map/near_1/ppermute | solution.py:251
  12.3 2.2 %collective-permute-done = bf16[384,256]{1,0:T(8,128)(2,1)S(1)} collective-permute-done((bf16[384,256]{1,0:T(8,128)(2,1)}, bf16[384,256]{1,0:T(8,128)(2,1)S(1)}, u32[]{:S(2)}, u32[]{:S(2)}) %collective-permute-start) | collective-permute-done | bytes 196640 | tf_op jit(solution)/shard_map/far_half/ppermute | solution.py:247
  14.4 0.0 collective-permute-done.1
  14.5 1.4 %collective-permute-start.2 = (bf16[384,256]{1,0:T(8,128)(2,1)S(1)}, bf16[384,256]{1,0:T(8,128)(2,1)S(1)}, u32[]{:S(2)}, u32[]{:S(2)}) collective-permute-start(bf16[384,256]{1,0:T(8,128)(2,1)S(1)} %broadcast_select_fusion.1.chunk), channel_id=1, source_target_pairs={{0,2},{1,3},{2,6},{3,7},{6,4},{7,5},{4,0},{5,1},{8,10},{9,11},{10,... | collective-permute-start | bytes 589832 | tf_op jit(solution)/shard_map/far_1/ppermute | solution.py:251
  15.8 2.3 %collective-permute-done.6.chunk = bf16[384,256]{1,0:T(8,128)(2,1)S(1)} collective-permute-done((bf16[384,256]{1,0:T(8,128)(2,1)S(1)}, bf16[384,256]{1,0:T(8,128)(2,1)S(1)}, u32[]{:S(2)}, u32[]{:S(2)}) %collective-permute-start.6) | collective-permute-done | bytes 196640 | tf_op jit(solution)/shard_map/near_1/ppermute | solution.py:251
  18.2 1.1 %collective-permute-start.7 = (bf16[384,256]{1,0:T(8,128)(2,1)S(1)}, bf16[384,256]{1,0:T(8,128)(2,1)S(1)}, u32[]{:S(2)}, u32[]{:S(2)}) collective-permute-start(bf16[384,256]{1,0:T(8,128)(2,1)S(1)} %collective-permute-done.6.chunk), channel_id=1, source_target_pairs={{0,2},{1,3},{2,6},{3,7},{6,4},{7,5},{4,0},{5,1},{8,10},{9,11},{10,... | collective-permute-start | bytes 589832 | tf_op jit(solution)/shard_map/near_2/ppermute | solution.py:251
  19.3 1.6 %pack.1 = (bf16[1024,256]{1,0:T(8,128)(2,1)S(1)}, bf16[1024,256]{1,0:T(8,128)(2,1)S(1)}, s32[8]{0:T(128)S(1)}) custom-call(s32[32]{0:T(128)S(1)} %copy-done.3, s32[4,16]{1,0:T(4,128)S(1)} %copy-done.1, bf16[1024,512]{1,0:T(8,128)(2,1)S(1)} %copy-done, bf16[1024,512]{1,0:T(8,128)(2,1)S(1)} %collective-permute-done.9.other_anc), custom_call_target="tpu_custom_call" | custom-call | tf_op jit(solution)/shard_map/pack/pallas_call | solution.py:276
  21.0 2.8 %collective-permute-start.10 = (bf16[1024,256]{1,0:T(8,128)(2,1)S(1)}, bf16[1024,256]{1,0:T(8,128)(2,1)S(1)}, u32[]{:S(2)}, u32[]{:S(2)}) collective-permute-start(bf16[1024,256]{1,0:T(8,128)(2,1)S(1)} %get-tuple-element.17), channel_id=1, source_target_pairs={{0,0},{1,8},{2,2},{3,10},{4,4},{5,12},{6,6},{7,14},{8,1},{9,9},{10... | collective-permute-start | bytes 1572872 | tf_op jit(solution)/shard_map/sigma_0/ppermute | solution.py:247
  23.7 1.9 %collective-permute-start.11 = (bf16[1024,256]{1,0:T(8,128)(2,1)S(1)}, bf16[1024,256]{1,0:T(8,128)(2,1)S(1)}, u32[]{:S(2)}, u32[]{:S(2)}) collective-permute-start(bf16[1024,256]{1,0:T(8,128)(2,1)S(1)} %get-tuple-element.18), channel_id=1, source_target_pairs={{0,16},{1,24},{2,18},{3,26},{4,20},{5,28},{6,22},{7,30},{8,17},{9,... | collective-permute-start | bytes 1572872 | tf_op jit(solution)/shard_map/sigma_1/ppermute | solution.py:247
  25.6 0.2 broadcast_in_dim.6._
  25.8 0.1 place.8._
  25.9 3.1 %collective-permute-start.3 = (bf16[384,256]{1,0:T(8,128)(2,1)S(1)}, bf16[384,256]{1,0:T(8,128)(2,1)S(1)}, u32[]{:S(2)}, u32[]{:S(2)}) collective-permute-start(bf16[384,256]{1,0:T(8,128)(2,1)S(1)} %collective-permute-done.2.chunk), channel_id=1, source_target_pairs={{0,2},{1,3},{2,6},{3,7},{6,4},{7,5},{4,0},{5,1},{8,10},{9,11},{10,... | collective-permute-start | bytes 589832 | tf_op jit(solution)/shard_map/far_2/ppermute | solution.py:251
  29.0 0.1 place.10._
  29.1 0.0 collective-permute-done.7.chunk
  29.1 0.1 collective-permute-start.8
  29.2 4.5 %collective-permute-done.3.chunk = bf16[384,256]{1,0:T(8,128)(2,1)S(1)} collective-permute-done((bf16[384,256]{1,0:T(8,128)(2,1)S(1)}, bf16[384,256]{1,0:T(8,128)(2,1)S(1)}, u32[]{:S(2)}, u32[]{:S(2)}) %collective-permute-start.3) | collective-permute-done | bytes 196640 | tf_op jit(solution)/shard_map/far_2/ppermute | solution.py:251
  33.7 2.2 %collective-permute-start.4 = (bf16[384,256]{1,0:T(8,128)(2,1)S(1)}, bf16[384,256]{1,0:T(8,128)(2,1)S(1)}, u32[]{:S(2)}, u32[]{:S(2)}) collective-permute-start(bf16[384,256]{1,0:T(8,128)(2,1)S(1)} %collective-permute-done.3.chunk), channel_id=1, source_target_pairs={{0,2},{1,3},{2,6},{3,7},{6,4},{7,5},{4,0},{5,1},{8,10},{9,11},{10,... | collective-permute-start | bytes 589832 | tf_op jit(solution)/shard_map/far_3/ppermute | solution.py:251
  36.0 0.1 place.13._
  36.1 0.0 collective-permute-done.10.refs_0_
  36.1 0.1 collective-permute-start.12
  36.1 2.2 %collective-permute-done.11.refs_1_ = bf16[1024,256]{1,0:T(8,128)(2,1)S(1)} collective-permute-done((bf16[1024,256]{1,0:T(8,128)(2,1)S(1)}, bf16[1024,256]{1,0:T(8,128)(2,1)S(1)}, u32[]{:S(2)}, u32[]{:S(2)}) %collective-permute-start.11) | collective-permute-done | bytes 524320 | tf_op jit(solution)/shard_map/sigma_1/ppermute | solution.py:247
  38.3 0.0 collective-permute-start.13
  38.3 0.0 collective-permute-done.8.chunk
  38.4 2.9 %collective-permute-done.4.chunk = bf16[384,256]{1,0:T(8,128)(2,1)S(1)} collective-permute-done((bf16[384,256]{1,0:T(8,128)(2,1)S(1)}, bf16[384,256]{1,0:T(8,128)(2,1)S(1)}, u32[]{:S(2)}, u32[]{:S(2)}) %collective-permute-start.4) | collective-permute-done | bytes 196640 | tf_op jit(solution)/shard_map/far_3/ppermute | solution.py:251
  41.3 0.5 collective-permute-start.19
  41.8 0.0 collective-permute-done.12.refs_2_
  41.8 0.0 collective-permute-done.13.refs_3_
  41.8 0.7 %stack.1.sigma = bf16[2048,512]{1,0:T(8,128)(2,1)S(1)} custom-call(s32[8]{0:T(128)S(1)} %get-tuple-element.16.members, bf16[1024,256]{1,0:T(8,128)(2,1)S(1)} %collective-permute-done.10.refs_0_, bf16[1024,256]{1,0:T(8,128)(2,1)S(1)} %collective-permute-done.11.refs_1_, bf16[1024,256]{1,0:T(8,128)(2,1)S(1)} %collective-permute-done.12.refs_2_, ...), custom_call_target="tpu_custom_call" | custom-call | flops 12000000000 | tf_op jit(solution)/shard_map/stack/pallas_call | solution.py:325
  42.5 2.3 %cross.1 = (bf16[384,256]{1,0:T(8,128)(2,1)S(1)}, bf16[384,256]{1,0:T(8,128)(2,1)S(1)}, bf16[96,512]{1,0:T(8,128)(2,1)S(1)}, bf16[96,512]{1,0:T(8,128)(2,1)}, bf...) custom-call(s32[4]{0:T(128)S(1)} %copy-done.2, bf16[384,2048]{1,0:T(8,128)(2,1)S(1)} %place.15.whole.rest_4_, ...), custom_call_target="tpu_custom_call" | custom-call | tf_op jit(solution)/shard_map/cross/pallas_call | solution.py:334
  44.8 0.7 %copy-done.4 = bf16[384,256]{1,0:T(8,128)(2,1)} copy-done((bf16[384,256]{1,0:T(8,128)(2,1)}, bf16[384,256]{1,0:T(8,128)(2,1)S(1)}, u32[]{:S(2)}) %copy-start.4) | copy-done | bytes 196632
  45.4 0.7 %copy-done.5 = bf16[384,256]{1,0:T(8,128)(2,1)} copy-done((bf16[384,256]{1,0:T(8,128)(2,1)}, bf16[384,256]{1,0:T(8,128)(2,1)S(1)}, u32[]{:S(2)}) %copy-start.5) | copy-done | bytes 196632
  46.1 0.0 collective-permute-start.16
  46.1 3.3 %collective-permute-start.17 = (bf16[96,512]{1,0:T(8,128)(2,1)}, bf16[96,512]{1,0:T(8,128)(2,1)S(1)}, u32[]{:S(2)}, u32[]{:S(2)}) collective-permute-start(bf16[96,512]{1,0:T(8,128)(2,1)} %get-tuple-element.24), channel_id=1, source_target_pairs={{0,6},{1,7},{2,4},{3,5},{4,2},{5,3},{6,0},{7,1},{8,14},{9,15},{10,... | collective-permute-start | bytes 294920 | tf_op jit(solution)/shard_map/columns_3/ppermute | solution.py:251
  49.4 3.4 %collective-permute-start.14 = (bf16[384,256]{1,0:T(8,128)(2,1)}, bf16[384,256]{1,0:T(8,128)(2,1)S(1)}, u32[]{:S(2)}, u32[]{:S(2)}) collective-permute-start(bf16[384,256]{1,0:T(8,128)(2,1)} %copy-done.5), channel_id=1, source_target_pairs={{0,0},{1,8},{2,2},{3,10},{4,4},{5,12},{6,6},{7,14},{8,1},{9,9},{10... | collective-permute-start | bytes 589832 | tf_op jit(solution)/shard_map/rows_out/ppermute | solution.py:247
  52.8 2.9 %collective-permute-done.16.rest_1_ = bf16[96,512]{1,0:T(8,128)(2,1)S(1)} collective-permute-done((bf16[96,512]{1,0:T(8,128)(2,1)}, bf16[96,512]{1,0:T(8,128)(2,1)S(1)}, u32[]{:S(2)}, u32[]{:S(2)}) %collective-permute-start.16) | collective-permute-done | bytes 98336 | tf_op jit(solution)/shard_map/columns_2/ppermute | solution.py:251
  55.7 1.5 %collective-permute-start.15 = (bf16[384,256]{1,0:T(8,128)(2,1)}, bf16[384,256]{1,0:T(8,128)(2,1)S(1)}, u32[]{:S(2)}, u32[]{:S(2)}) collective-permute-start(bf16[384,256]{1,0:T(8,128)(2,1)} %copy-done.4), channel_id=1, source_target_pairs={{0,1},{1,9},{2,3},{3,11},{4,5},{5,13},{6,7},{7,15},{8,0},{9,8},{10... | collective-permute-start | bytes 589832 | tf_op jit(solution)/shard_map/rows_out_other/ppermute | solution.py:247
  57.2 0.0 copy-start.6
  57.2 1.2 %pivot.1 = bf16[96,768]{1,0:T(8,128)(2,1)S(1)} custom-call(bf16[96,512]{1,0:T(8,128)(2,1)S(1)} %get-tuple-element.22.rest_0_, bf16[96,512]{1,0:T(8,128)(2,1)S(1)} %collective-permute-done.16.rest_1_, bf16[96,512]{1,0:T(8,128)(2,1)S(1)} %collective-permute-done.17.rest_2_, bf16[96,512]{1,0:T(8,128)(2,1)S(1)} %collective-permute-done.18.rest_3_, ...), custom_call_target="tpu_custom_call" | custom-call | tf_op jit(solution)/shard_map/pivot/pallas_call | solution.py:356
  58.5 2.8 %collective-permute-start.20 = (bf16[96,768]{1,0:T(8,128)(2,1)S(1)}, bf16[96,768]{1,0:T(8,128)(2,1)S(1)}, u32[]{:S(2)}, u32[]{:S(2)}) collective-permute-start(bf16[96,768]{1,0:T(8,128)(2,1)S(1)} %pivot.1), channel_id=1, source_target_pairs={{0,0},{1,8},{2,2},{3,10},{4,4},{5,12},{6,6},{7,14},{8,1},{9,9},{10... | collective-permute-start | bytes 442376 | tf_op jit(solution)/shard_map/term_out/ppermute | solution.py:247
  61.3 0.4 fusion
  61.8 1.0 %turn.1 = bf16[1,256,768]{2,1,0:T(8,128)(2,1)} custom-call(bf16[384,256]{1,0:T(8,128)(2,1)S(1)} %collective-permute-done.14.own_rows, bf16[384,256]{1,0:T(8,128)(2,1)S(1)} %collective-permute-done.15.other_rows), custom_call_target="tpu_custom_call" | custom-call | tf_op jit(solution)/shard_map/turn/pallas_call | solution.py:366
  62.8 2.2 %collective-permute-done.20 = bf16[96,768]{1,0:T(8,128)(2,1)S(1)} collective-permute-done((bf16[96,768]{1,0:T(8,128)(2,1)S(1)}, bf16[96,768]{1,0:T(8,128)(2,1)S(1)}, u32[]{:S(2)}, u32[]{:S(2)}) %collective-permute-start.20) | collective-permute-done | bytes 147488 | tf_op jit(solution)/shard_map/term_out/ppermute | solution.py:247
  64.9 0.7 %add_bitcast_fusion = f32[1,96,768]{2,1,0:T(8,128)} fusion(f32[96,768]{1,0:T(8,128)S(1)} %fusion, bf16[96,768]{1,0:T(8,128)(2,1)S(1)} %collective-permute-done.20), kind=kLoop, calls=%fused_computation | loop fusion | flops 147456 | bytes 737280 | tf_op jit(solution)/shard_map/broadcast_in_dim | solution.py:376
  (27 shorter events, 0.3 us)
Async XLA Ops:
  0.6 18.7 %copy-start = (bf16[1024,512]{1,0:T(8,128)(2,1)S(1)}, bf16[1024,512]{1,0:T(8,128)(2,1)}, u32[]{:S(2)}) copy-start(bf16[1024,512]{1,0:T(8,128)(2,1)} %anc.1) | copy-start | bytes 3145732
  0.6 18.7 %copy-start.3 = (s32[32]{0:T(128)S(1)}, s32[32]{0:T(128)}, u32[]{:S(2)}) copy-start(s32[32]{0:T(128)} %row_home_in.1) | copy-start | bytes 388
  0.7 18.7 %copy-start.1 = (s32[4,16]{1,0:T(4,128)S(1)}, s32[4,16]{1,0:T(4,128)}, u32[]{:S(2)}) copy-start(s32[4,16]{1,0:T(4,128)} %lists_in.1) | copy-start | bytes 772
  0.7 18.6 %collective-permute-start.9 = (bf16[1024,512]{1,0:T(8,128)(2,1)}, bf16[1024,512]{1,0:T(8,128)(2,1)S(1)}, u32[]{:S(2)}, u32[]{:S(2)}) collective-permute-start(bf16[1024,512]{1,0:T(8,128)(2,1)} %anc.1), channel_id=1, source_target_pairs={{0,8},{8,0},{16,24},{24,16},{1,9},{9,1},{17,25},{25,17},{2,10},{10... | collective-permute-start | bytes 3145736 | tf_op jit(solution)/shard_map/rows_of_sibling/ppermute | solution.py:243
  3.7 7.2 %collective-permute-start.5 = (bf16[384,256]{1,0:T(8,128)(2,1)}, bf16[384,256]{1,0:T(8,128)(2,1)S(1)}, u32[]{:S(2)}, u32[]{:S(2)}) collective-permute-start(bf16[384,256]{1,0:T(8,128)(2,1)} %get-tuple-element.15), channel_id=1, source_target_pairs={{0,8},{2,10},{4,12},{6,14},{9,1},{11,3},{13,5},{15,7},{16,24},{18,... | collective-permute-start | bytes 589832 | tf_op jit(solution)/shard_map/near_half/ppermute | solution.py:247
  5.0 9.5 %collective-permute-start.1 = (bf16[384,256]{1,0:T(8,128)(2,1)}, bf16[384,256]{1,0:T(8,128)(2,1)S(1)}, u32[]{:S(2)}, u32[]{:S(2)}) collective-permute-start(bf16[384,256]{1,0:T(8,128)(2,1)} %get-tuple-element.15), channel_id=1, source_target_pairs={{1,8},{3,10},{5,12},{7,14},{8,1},{10,3},{12,5},{14,7},{17,24},{19,... | collective-permute-start | bytes 589832 | tf_op jit(solution)/shard_map/far_half_off/ppermute | solution.py:247
  9.4 5.0 %collective-permute-start = (bf16[384,256]{1,0:T(8,128)(2,1)}, bf16[384,256]{1,0:T(8,128)(2,1)S(1)}, u32[]{:S(2)}, u32[]{:S(2)}) collective-permute-start(bf16[384,256]{1,0:T(8,128)(2,1)} %get-tuple-element.14), channel_id=1, source_target_pairs={{1,0},{3,2},{5,4},{7,6},{8,9},{10,11},{12,13},{14,15},{17,16},{19,... | collective-permute-start | bytes 589832 | tf_op jit(solution)/shard_map/far_half/ppermute | solution.py:247
  10.9 7.3 %collective-permute-start.6 = (bf16[384,256]{1,0:T(8,128)(2,1)S(1)}, bf16[384,256]{1,0:T(8,128)(2,1)S(1)}, u32[]{:S(2)}, u32[]{:S(2)}) collective-permute-start(bf16[384,256]{1,0:T(8,128)(2,1)S(1)} %broadcast_select_fusion.chunk), channel_id=1, source_target_pairs={{0,2},{1,3},{2,6},{3,7},{6,4},{7,5},{4,0},{5,1},{8,10},{9,11},{10,... | collective-permute-start | bytes 589832 | tf_op jit(solution)/shard_map/near_1/ppermute | solution.py:251
  14.5 11.4 %collective-permute-start.2 = (bf16[384,256]{1,0:T(8,128)(2,1)S(1)}, bf16[384,256]{1,0:T(8,128)(2,1)S(1)}, u32[]{:S(2)}, u32[]{:S(2)}) collective-permute-start(bf16[384,256]{1,0:T(8,128)(2,1)S(1)} %broadcast_select_fusion.1.chunk), channel_id=1, source_target_pairs={{0,2},{1,3},{2,6},{3,7},{6,4},{7,5},{4,0},{5,1},{8,10},{9,11},{10,... | collective-permute-start | bytes 589832 | tf_op jit(solution)/shard_map/far_1/ppermute | solution.py:251
  18.2 10.9 %collective-permute-start.7 = (bf16[384,256]{1,0:T(8,128)(2,1)S(1)}, bf16[384,256]{1,0:T(8,128)(2,1)S(1)}, u32[]{:S(2)}, u32[]{:S(2)}) collective-permute-start(bf16[384,256]{1,0:T(8,128)(2,1)S(1)} %collective-permute-done.6.chunk), channel_id=1, source_target_pairs={{0,2},{1,3},{2,6},{3,7},{6,4},{7,5},{4,0},{5,1},{8,10},{9,11},{10,... | collective-permute-start | bytes 589832 | tf_op jit(solution)/shard_map/near_2/ppermute | solution.py:251
  21.0 15.1 %collective-permute-start.10 = (bf16[1024,256]{1,0:T(8,128)(2,1)S(1)}, bf16[1024,256]{1,0:T(8,128)(2,1)S(1)}, u32[]{:S(2)}, u32[]{:S(2)}) collective-permute-start(bf16[1024,256]{1,0:T(8,128)(2,1)S(1)} %get-tuple-element.17), channel_id=1, source_target_pairs={{0,0},{1,8},{2,2},{3,10},{4,4},{5,12},{6,6},{7,14},{8,1},{9,9},{10... | collective-permute-start | bytes 1572872 | tf_op jit(solution)/shard_map/sigma_0/ppermute | solution.py:247
  23.7 14.6 %collective-permute-start.11 = (bf16[1024,256]{1,0:T(8,128)(2,1)S(1)}, bf16[1024,256]{1,0:T(8,128)(2,1)S(1)}, u32[]{:S(2)}, u32[]{:S(2)}) collective-permute-start(bf16[1024,256]{1,0:T(8,128)(2,1)S(1)} %get-tuple-element.18), channel_id=1, source_target_pairs={{0,16},{1,24},{2,18},{3,26},{4,20},{5,28},{6,22},{7,30},{8,17},{9,... | collective-permute-start | bytes 1572872 | tf_op jit(solution)/shard_map/sigma_1/ppermute | solution.py:247
  25.9 7.9 %collective-permute-start.3 = (bf16[384,256]{1,0:T(8,128)(2,1)S(1)}, bf16[384,256]{1,0:T(8,128)(2,1)S(1)}, u32[]{:S(2)}, u32[]{:S(2)}) collective-permute-start(bf16[384,256]{1,0:T(8,128)(2,1)S(1)} %collective-permute-done.2.chunk), channel_id=1, source_target_pairs={{0,2},{1,3},{2,6},{3,7},{6,4},{7,5},{4,0},{5,1},{8,10},{9,11},{10,... | collective-permute-start | bytes 589832 | tf_op jit(solution)/shard_map/far_2/ppermute | solution.py:251
  29.1 9.2 %collective-permute-start.8 = (bf16[384,256]{1,0:T(8,128)(2,1)S(1)}, bf16[384,256]{1,0:T(8,128)(2,1)S(1)}, u32[]{:S(2)}, u32[]{:S(2)}) collective-permute-start(bf16[384,256]{1,0:T(8,128)(2,1)S(1)} %collective-permute-done.7.chunk), channel_id=1, source_target_pairs={{0,2},{1,3},{2,6},{3,7},{6,4},{7,5},{4,0},{5,1},{8,10},{9,11},{10,... | collective-permute-start | bytes 589832 | tf_op jit(solution)/shard_map/near_3/ppermute | solution.py:251
  33.7 7.5 %collective-permute-start.4 = (bf16[384,256]{1,0:T(8,128)(2,1)S(1)}, bf16[384,256]{1,0:T(8,128)(2,1)S(1)}, u32[]{:S(2)}, u32[]{:S(2)}) collective-permute-start(bf16[384,256]{1,0:T(8,128)(2,1)S(1)} %collective-permute-done.3.chunk), channel_id=1, source_target_pairs={{0,2},{1,3},{2,6},{3,7},{6,4},{7,5},{4,0},{5,1},{8,10},{9,11},{10,... | collective-permute-start | bytes 589832 | tf_op jit(solution)/shard_map/far_3/ppermute | solution.py:251
  36.1 5.7 %collective-permute-start.12 = (bf16[1024,256]{1,0:T(8,128)(2,1)S(1)}, bf16[1024,256]{1,0:T(8,128)(2,1)S(1)}, u32[]{:S(2)}, u32[]{:S(2)}) collective-permute-start(bf16[1024,256]{1,0:T(8,128)(2,1)S(1)} %collective-permute-done.10.refs_0_), channel_id=1, source_target_pairs={{0,8},{8,0},{16,24},{24,16},{1,9},{9,1},{17,25},{25,17},{2,10},{10... | collective-permute-start | bytes 1572872 | tf_op jit(solution)/shard_map/share_0/ppermute | solution.py:243
  38.3 3.4 %collective-permute-start.13 = (bf16[1024,256]{1,0:T(8,128)(2,1)S(1)}, bf16[1024,256]{1,0:T(8,128)(2,1)S(1)}, u32[]{:S(2)}, u32[]{:S(2)}) collective-permute-start(bf16[1024,256]{1,0:T(8,128)(2,1)S(1)} %collective-permute-done.11.refs_1_), channel_id=1, source_target_pairs={{0,8},{8,0},{16,24},{24,16},{1,9},{9,1},{17,25},{25,17},{2,10},{10... | collective-permute-start | bytes 1572872 | tf_op jit(solution)/shard_map/share_1/ppermute | solution.py:243
  41.3 15.9 %collective-permute-start.19 = (bf16[384,2048]{1,0:T(8,128)(2,1)S(1)}, bf16[384,2048]{1,0:T(8,128)(2,1)S(1)}, u32[]{:S(2)}, u32[]{:S(2)}) collective-permute-start(bf16[384,2048]{1,0:T(8,128)(2,1)S(1)} %place.15.whole.rest_4_), channel_id=1, source_target_pairs={{0,8},{8,0},{16,24},{24,16},{1,9},{9,1},{17,25},{25,17},{2,10},{10... | collective-permute-start | bytes 4718600 | tf_op jit(solution)/shard_map/scaled_of_sibling/ppermute | solution.py:243
  41.8 0.7 %copy-start.2 = (s32[4]{0:T(128)S(1)}, s32[4]{0:T(128)}, u32[]{:S(2)}) copy-start(s32[4]{0:T(128)} %front_blocks.1) | copy-start | bytes 52
  44.8 0.7 %copy-start.4 = (bf16[384,256]{1,0:T(8,128)(2,1)}, bf16[384,256]{1,0:T(8,128)(2,1)S(1)}, u32[]{:S(2)}) copy-start(bf16[384,256]{1,0:T(8,128)(2,1)S(1)} %get-tuple-element.20) | copy-start | bytes 589828
  45.4 0.7 %copy-start.5 = (bf16[384,256]{1,0:T(8,128)(2,1)}, bf16[384,256]{1,0:T(8,128)(2,1)S(1)}, u32[]{:S(2)}) copy-start(bf16[384,256]{1,0:T(8,128)(2,1)S(1)} %get-tuple-element.19) | copy-start | bytes 589828
  46.1 9.6 %collective-permute-start.16 = (bf16[96,512]{1,0:T(8,128)(2,1)}, bf16[96,512]{1,0:T(8,128)(2,1)S(1)}, u32[]{:S(2)}, u32[]{:S(2)}) collective-permute-start(bf16[96,512]{1,0:T(8,128)(2,1)} %get-tuple-element.23), channel_id=1, source_target_pairs={{0,4},{1,5},{2,6},{3,7},{4,0},{5,1},{6,2},{7,3},{8,12},{9,13},{10,... | collective-permute-start | bytes 294920 | tf_op jit(solution)/shard_map/columns_2/ppermute | solution.py:251
  46.1 11.1 %collective-permute-start.17 = (bf16[96,512]{1,0:T(8,128)(2,1)}, bf16[96,512]{1,0:T(8,128)(2,1)S(1)}, u32[]{:S(2)}, u32[]{:S(2)}) collective-permute-start(bf16[96,512]{1,0:T(8,128)(2,1)} %get-tuple-element.24), channel_id=1, source_target_pairs={{0,6},{1,7},{2,4},{3,5},{4,2},{5,3},{6,0},{7,1},{8,14},{9,15},{10,... | collective-permute-start | bytes 294920 | tf_op jit(solution)/shard_map/columns_3/ppermute | solution.py:251
  49.4 7.8 %collective-permute-start.18 = (bf16[96,512]{1,0:T(8,128)(2,1)}, bf16[96,512]{1,0:T(8,128)(2,1)S(1)}, u32[]{:S(2)}, u32[]{:S(2)}) collective-permute-start(bf16[96,512]{1,0:T(8,128)(2,1)} %get-tuple-element.25), channel_id=1, source_target_pairs={{0,2},{1,3},{2,0},{3,1},{4,6},{5,7},{6,4},{7,5},{8,10},{9,11},{10,... | collective-permute-start | bytes 294920 | tf_op jit(solution)/shard_map/columns_1/ppermute | solution.py:251
  49.4 12.3 %collective-permute-start.14 = (bf16[384,256]{1,0:T(8,128)(2,1)}, bf16[384,256]{1,0:T(8,128)(2,1)S(1)}, u32[]{:S(2)}, u32[]{:S(2)}) collective-permute-start(bf16[384,256]{1,0:T(8,128)(2,1)} %copy-done.5), channel_id=1, source_target_pairs={{0,0},{1,8},{2,2},{3,10},{4,4},{5,12},{6,6},{7,14},{8,1},{9,9},{10... | collective-permute-start | bytes 589832 | tf_op jit(solution)/shard_map/rows_out/ppermute | solution.py:247
  55.7 6.1 %collective-permute-start.15 = (bf16[384,256]{1,0:T(8,128)(2,1)}, bf16[384,256]{1,0:T(8,128)(2,1)S(1)}, u32[]{:S(2)}, u32[]{:S(2)}) collective-permute-start(bf16[384,256]{1,0:T(8,128)(2,1)} %copy-done.4), channel_id=1, source_target_pairs={{0,1},{1,9},{2,3},{3,11},{4,5},{5,13},{6,7},{7,15},{8,0},{9,8},{10... | collective-permute-start | bytes 589832 | tf_op jit(solution)/shard_map/rows_out_other/ppermute | solution.py:247
  57.2 4.1 %copy-start.6 = (bf16[1,768,768]{2,1,0:T(8,128)(2,1)S(1)}, bf16[1,768,768]{2,1,0:T(8,128)(2,1)}, u32[]{:S(2)}) copy-start(bf16[1,768,768]{2,1,0:T(8,128)(2,1)} %param.11) | copy-start | bytes 3538948
  58.5 6.5 %collective-permute-start.20 = (bf16[96,768]{1,0:T(8,128)(2,1)S(1)}, bf16[96,768]{1,0:T(8,128)(2,1)S(1)}, u32[]{:S(2)}, u32[]{:S(2)}) collective-permute-start(bf16[96,768]{1,0:T(8,128)(2,1)S(1)} %pivot.1), channel_id=1, source_target_pairs={{0,0},{1,8},{2,2},{3,10},{4,4},{5,12},{6,6},{7,14},{8,1},{9,9},{10... | collective-permute-start | bytes 442376 | tf_op jit(solution)/shard_map/term_out/ppermute | solution.py:247
